TPU v7x, 128 devices: a whole 4x4x4 slice. The times are simulated.
128 devices in a mesh: dp: 32 (over y, z, core), expert: 4 (over x).
Axes of the slice: x: 4, y: 4, z: 4, core: 2. Of those that a mesh axis runs over, the one named last changes fastest.
Arguments:
- tokens: bfloat16 [16384, 768], P(('dp', 'expert')), may hold values from -6 to 6
- norm_attn: bfloat16 [768], P('dp'), may hold values from 0.5 to 1.5
- w_qkv: bfloat16 [768, 2304], P('dp'), may hold values from -0.09375 to 0.09375
- w_attn_out: bfloat16 [768, 768], P('dp'), may hold values from -1.75 to 1.75
- bias_table: bfloat16 [32, 12], P('dp'), may hold values from -4 to 4
- norm_moe: bfloat16 [768], P('dp'), may hold values from 0.5 to 1.5
- router: bfloat16 [768, 4], P('dp'), may hold values from -0.15625 to 0.15625
- w_in: bfloat16 [768, 4, 3072], P('dp', 'expert'), may hold values from -0.21875 to 0.21875
- w_out: bfloat16 [3072, 4, 768], P('dp', 'expert'), may hold values from -0.4375 to 0.4375
- routes: int32 [16384, 1], P(('dp', 'expert')), may hold values from 0 to 3; in each aligned block of 128 rows (0 to 127, 128 to 255, ...) at most 40 rows name the same one
- buckets: int32 [1023], replicated, may hold values from 0 to 31, as said below
- cotangent: bfloat16 [16384, 768], P(('dp', 'expert')), may hold values from -6 to 6
Outputs:
- mixed: bfloat16 [16384, 768], P(('dp', 'expert'))
- d_tokens: bfloat16 [16384, 768], P(('dp', 'expert'))
- g_norm_attn: float32 [768], P('dp')
- g_w_qkv: float32 [768, 2304], P('dp')
- g_w_attn_out: float32 [768, 768], P('dp')
- g_bias_table: float32 [32, 12], P('dp')
- g_norm_moe: float32 [768], P('dp')
- g_router: float32 [768, 4], P('dp')
- g_w_in: float32 [768, 4, 3072], P('dp', 'expert')
- g_w_out: float32 [3072, 4, 768], P('dp', 'expert')
Inputs may be any that keep to these rules, and one draw needn't show every extreme that they name: `routes`: in each device's rows (aligned blocks of 128 tokens) no expert is named by more than 40 tokens; some expert is named by exactly 40 in some block. Entry r is the bucket of the key-minus-query distance r - 511: 0 at distance 0, buckets below 16 for keys before the query and the others for keys after it, never falling with the distance's size on either side.
All inputs are finite; a program needn't handle non-finite values.
Results may differ from a plain program's by a relative error of at most 0.028.
Values may be sent and summed in bfloat16 or wider, within the bound.
A program may use at most 128 MiB of HBM per device.

v0:
```python
import jax
import jax.numpy as jnp
from jax import lax
from jax.sharding import PartitionSpec as P

epsilon = 1e-06
highest = lax.Precision.HIGHEST


def in_one_piece(arrays, axis, dim, along):
    both = jnp.concatenate(arrays, axis=along)
    result, at, gathered = (lax.all_gather(both, axis, axis=dim, tiled=True), 0, [])
    for a in arrays:
        gathered.append(lax.slice_in_dim(result, at, at + a.shape[along], axis=along))
        at += a.shape[along]
    return tuple(gathered)


def sent_together(arrays, axis, dim, along):
    columns = [a.reshape(*a.shape[:along], -1) for a in arrays]
    both = jnp.concatenate(columns, axis=along)
    result, at, gathered = (lax.all_gather(both, axis, axis=dim, tiled=True), 0, [])
    for a, column in zip(arrays, columns):
        piece = result[..., at : at + column.shape[along]]
        gathered.append(piece.reshape(*piece.shape[:along], *a.shape[along:]))
        at += column.shape[along]
    return tuple(gathered)


def sent_together_2(arrays, axis, dim, along):
    ends, at = ([], 0)
    for a in arrays[:-1]:
        at += a.shape[along]
        ends.append(at)
    both = jnp.concatenate(arrays, axis=along)
    return tuple(
        jnp.split(lax.psum_scatter(both, axis, scatter_dimension=dim, tiled=True), ends, axis=along)
    )


def sent_together_3(arrays, axis, dim, along):
    columns = [a.reshape(*a.shape[:along], -1) for a in arrays]
    both = jnp.concatenate(columns, axis=along)
    result, at, gathered = (lax.psum_scatter(both, axis, scatter_dimension=dim, tiled=True), 0, [])
    for a, column in zip(arrays, columns):
        piece = result[..., at : at + column.shape[along]]
        gathered.append(piece.reshape(*piece.shape[:along], *a.shape[along:]))
        at += column.shape[along]
    return tuple(gathered)


def rms_norm(values, gain_vec):
    return values * lax.rsqrt(jnp.mean(values * values, -1, keepdims=True) + epsilon) * gain_vec


def toeplitz(rel_row, query_rows, key_rows):
    period = query_rows + key_rows - 1
    rolled = jnp.roll(rel_row, -(query_rows - 1))
    tiled = jnp.tile(rolled, query_rows)[: query_rows * (period - 1)]
    return tiled.reshape(query_rows, period - 1)[:, :key_rows]


def relative_bias(table, buckets):
    picks = (buckets[:, None] == jnp.arange(table.shape[0], dtype=jnp.int32)[None, :]).astype(
        jnp.float32
    )
    return (jnp.dot(picks, table.astype(jnp.float32), precision=highest).T, picks)


def split_heads(matrix, head_count):
    return matrix.reshape(matrix.shape[0], head_count, -1).transpose(1, 0, 2)


def join_heads(stack):
    return stack.transpose(1, 0, 2).reshape(stack.shape[1], -1)


def gather_rows(placing, matrix):
    return lax.dot_general(
        placing, matrix, (((0,), (0,)), ((), ())), preferred_element_type=jnp.float32
    )


def per_device(
    tokens,
    norm_attn,
    w_qkv,
    w_attn_out,
    bias_table,
    norm_moe,
    router,
    w_in,
    w_out,
    routes,
    buckets,
    cotangent,
):
    tok_rows, model_width = tokens.shape
    groups = lax.axis_size("expert")
    key_rows = tok_rows * groups
    head_count = bias_table.shape[1]
    experts = router.shape[1]
    local_experts = w_in.shape[1]
    capacity = tok_rows * 5 // (4 * experts)
    slot_count = groups * capacity
    fetched = (
        *in_one_piece((w_qkv, w_attn_out), "dp", 0, 1),
        lax.all_gather(bias_table, "dp", axis=0, tiled=True),
        lax.all_gather(norm_attn, "dp", axis=0, tiled=True),
        *sent_together((norm_moe, router, w_in), "dp", 0, 1),
        lax.all_gather(w_out, "dp", axis=0, tiled=True),
    )
    full_qkv, full_out, full_table, gain_one, gain_two, full_router, full_in, full_outw = fetched
    gain_one = gain_one.astype(jnp.float32)
    gain_two = gain_two.astype(jnp.float32)
    router_full = full_router.astype(jnp.float32)
    resid_in = tokens.astype(jnp.float32)
    normed_low = rms_norm(resid_in, gain_one).astype(jnp.bfloat16)
    projected = jnp.dot(normed_low, full_qkv, preferred_element_type=jnp.float32).astype(
        jnp.bfloat16
    )
    rel_bias, picks = relative_bias(full_table, buckets)
    head_span = head_count // groups
    head_start = lax.axis_index("expert") * head_span
    spread = lax.all_to_all(
        projected.reshape(tok_rows, 3, groups, -1),
        "expert",
        split_axis=2,
        concat_axis=0,
        tiled=True,
    )
    query_heads = split_heads(spread[:, 0, 0], head_span)
    key_heads = split_heads(spread[:, 1, 0], head_span)
    value_heads = split_heads(spread[:, 2, 0], head_span)
    rel_heads = lax.dynamic_slice_in_dim(rel_bias, head_start, head_span, 0)

    def head_forward(inputs):
        query_one, key_one, value_one, rel_one = inputs
        scores = jnp.dot(query_one, key_one.T, preferred_element_type=jnp.float32) + toeplitz(
            rel_one, key_rows, key_rows
        )
        row_max = jnp.max(scores, -1, keepdims=True)
        log_total = row_max + jnp.log(jnp.sum(jnp.exp(scores - row_max), -1, keepdims=True))
        weights = jnp.exp(scores - log_total).astype(jnp.bfloat16)
        return (jnp.dot(weights, value_one, preferred_element_type=jnp.float32), log_total[:, 0])

    head_outs, log_totals = lax.map(head_forward, (query_heads, key_heads, value_heads, rel_heads))
    local_out = join_heads(head_outs).astype(jnp.bfloat16).reshape(key_rows, 1, -1)
    mixed_heads = lax.all_to_all(
        local_out, "expert", split_axis=0, concat_axis=1, tiled=True
    ).reshape(tok_rows, model_width)
    after_attn = resid_in + jnp.dot(mixed_heads, full_out, preferred_element_type=jnp.float32)
    moe_input = rms_norm(after_attn, gain_two).astype(jnp.bfloat16)
    logits = jnp.dot(moe_input.astype(jnp.float32), router_full, precision=highest)
    routed = routes[:, 0]
    chosen_int = (routed[:, None] == jnp.arange(experts, dtype=jnp.int32)[None, :]).astype(
        jnp.int32
    )
    chosen = chosen_int.astype(jnp.float32)

    def gate_of(logit_rows):
        return jnp.sum(jax.nn.softmax(logit_rows, axis=-1) * chosen, -1)

    gate_value, gate_back = jax.vjp(gate_of, logits)
    slot_id = jnp.sum((jnp.cumsum(chosen_int, 0) - 1) * chosen_int, -1)
    column = routed % local_experts * slot_count + routed // local_experts * capacity + slot_id
    placing = (
        column[:, None] == jnp.arange(local_experts * slot_count, dtype=jnp.int32)[None, :]
    ).astype(jnp.bfloat16)
    outgoing = (
        gather_rows(placing, moe_input)
        .astype(jnp.bfloat16)
        .reshape(local_experts, slot_count, model_width)
    )
    incoming = lax.all_to_all(outgoing, "expert", split_axis=1, concat_axis=1, tiled=True)
    hidden = jnp.einsum("ecd,def->ecf", incoming, full_in, preferred_element_type=jnp.float32)
    activated, gelu_back = jax.vjp(jax.nn.gelu, hidden)
    act_low = activated.astype(jnp.bfloat16)
    result = jnp.einsum(
        "ecf,fed->ecd", act_low, full_outw, preferred_element_type=jnp.float32
    ).astype(jnp.bfloat16)
    returned = lax.all_to_all(result, "expert", split_axis=1, concat_axis=1, tiled=True)
    combined = jnp.dot(
        placing, returned.reshape(-1, model_width), preferred_element_type=jnp.float32
    )
    mixed = (after_attn + gate_value[:, None] * combined).astype(jnp.bfloat16)
    upstream = cotangent.astype(jnp.float32)
    d_combined = (gate_value[:, None] * upstream).astype(jnp.bfloat16)
    d_gate = jnp.sum(upstream * combined, -1)
    d_outgoing = (
        gather_rows(placing, d_combined)
        .astype(jnp.bfloat16)
        .reshape(local_experts, slot_count, model_width)
    )
    d_result = lax.all_to_all(d_outgoing, "expert", split_axis=1, concat_axis=1, tiled=True)
    refetched = (
        *in_one_piece((w_qkv, w_attn_out), "dp", 0, 1),
        lax.all_gather(bias_table, "dp", axis=0, tiled=True),
        lax.all_gather(norm_attn, "dp", axis=0, tiled=True),
        *sent_together((norm_moe, router, w_in), "dp", 0, 1),
        lax.all_gather(w_out, "dp", axis=0, tiled=True),
    )
    full_qkv, full_out, full_table, gain_one, gain_two, full_router, full_in, full_outw = refetched
    gain_one = gain_one.astype(jnp.float32)
    gain_two = gain_two.astype(jnp.float32)
    router_full = full_router.astype(jnp.float32)
    rel_bias, picks = relative_bias(full_table, buckets)
    rel_heads = lax.dynamic_slice_in_dim(rel_bias, head_start, head_span, 0)
    d_act = jnp.einsum("ecd,fed->ecf", d_result, full_outw, preferred_element_type=jnp.float32)
    d_hidden = gelu_back(d_act)[0].astype(jnp.bfloat16)
    grad_w_out = jnp.einsum("ecf,ecd->fed", act_low, d_result, preferred_element_type=jnp.float32)
    grad_w_in = jnp.einsum("ecd,ecf->def", incoming, d_hidden, preferred_element_type=jnp.float32)
    d_incoming = jnp.einsum(
        "ecf,def->ecd", d_hidden, full_in, preferred_element_type=jnp.float32
    ).astype(jnp.bfloat16)
    d_returned = lax.all_to_all(d_incoming, "expert", split_axis=1, concat_axis=1, tiled=True)
    d_moe = jnp.dot(
        placing, d_returned.reshape(-1, model_width), preferred_element_type=jnp.float32
    )
    d_logits = gate_back(d_gate)[0]
    grad_router = jnp.dot(moe_input.astype(jnp.float32).T, d_logits, precision=highest)
    d_moe = d_moe + jnp.dot(d_logits, router_full.T, precision=highest)
    _, norm_two_back = jax.vjp(rms_norm, after_attn, gain_two)
    d_after, grad_norm_two = norm_two_back(d_moe)
    d_after = d_after + upstream
    d_attn_low = d_after.astype(jnp.bfloat16)
    grad_attn_out = jnp.dot(mixed_heads.T, d_attn_low, preferred_element_type=jnp.float32)
    d_heads_flat = jnp.dot(d_attn_low, full_out.T, preferred_element_type=jnp.float32).astype(
        jnp.bfloat16
    )
    spread_grads = lax.all_to_all(
        d_heads_flat.reshape(tok_rows, groups, -1),
        "expert",
        split_axis=1,
        concat_axis=0,
        tiled=True,
    )
    d_heads = split_heads(spread_grads[:, 0], head_span)

    def head_backward(inputs):
        query_one, key_one, value_one, rel_one, total_one, d_one = inputs
        bias_block, bias_back = jax.vjp(
            lambda rel_row: toeplitz(rel_row, key_rows, key_rows), rel_one
        )
        scores = jnp.dot(query_one, key_one.T, preferred_element_type=jnp.float32) + bias_block
        weights = jnp.exp(scores - total_one[:, None])
        d_weights = jnp.dot(d_one, value_one.T, preferred_element_type=jnp.float32)
        grad_value = jnp.dot(
            weights.astype(jnp.bfloat16).T, d_one, preferred_element_type=jnp.float32
        )
        d_scores = weights * (d_weights - jnp.sum(weights * d_weights, -1, keepdims=True))
        d_rel = bias_back(d_scores)[0]
        scores_low = d_scores.astype(jnp.bfloat16)
        grad_query = jnp.dot(scores_low, key_one, preferred_element_type=jnp.float32)
        grad_key = jnp.dot(scores_low.T, query_one, preferred_element_type=jnp.float32)
        return (grad_query, grad_key, grad_value, d_rel)

    grad_query, grad_key, grad_value, d_rel = lax.map(
        head_backward, (query_heads, key_heads, value_heads, rel_heads, log_totals, d_heads)
    )
    stacked = jnp.stack(
        [join_heads(grad_query), join_heads(grad_key), join_heads(grad_value)], 1
    ).astype(jnp.bfloat16)[:, :, None, :]
    d_projected = lax.all_to_all(
        stacked, "expert", split_axis=0, concat_axis=2, tiled=True
    ).reshape(tok_rows, 3 * model_width)
    d_rel_full = lax.dynamic_update_slice_in_dim(
        jnp.zeros((head_count, d_rel.shape[1]), jnp.float32), d_rel, head_start, 0
    )
    grad_qkv = jnp.dot(normed_low.T, d_projected, preferred_element_type=jnp.float32)
    d_normed = jnp.dot(d_projected, full_qkv.T, preferred_element_type=jnp.float32)
    _, norm_one_back = jax.vjp(rms_norm, resid_in, gain_one)
    d_resid, grad_norm_one = norm_one_back(d_normed)
    d_tokens = (d_after + d_resid).astype(jnp.bfloat16)
    grad_table = jnp.dot(picks.T, d_rel_full.T, precision=highest)
    split_parts = (
        *tuple(
            (
                part.astype(jnp.float32)
                for part in sent_together_2(
                    (grad_qkv.astype(jnp.bfloat16), grad_attn_out.astype(jnp.bfloat16)), "dp", 0, 1
                )
            )
        ),
        lax.psum_scatter(
            grad_table.astype(jnp.bfloat16), "dp", scatter_dimension=0, tiled=True
        ).astype(jnp.float32),
        lax.psum_scatter(
            grad_norm_one.astype(jnp.bfloat16), "dp", scatter_dimension=0, tiled=True
        ).astype(jnp.float32),
        *tuple(
            (
                part.astype(jnp.float32)
                for part in sent_together_3(
                    (
                        grad_norm_two.astype(jnp.bfloat16),
                        grad_router.astype(jnp.bfloat16),
                        grad_w_in.astype(jnp.bfloat16),
                    ),
                    "dp",
                    0,
                    1,
                )
            )
        ),
        lax.psum_scatter(
            grad_w_out.astype(jnp.bfloat16), "dp", scatter_dimension=0, tiled=True
        ).astype(jnp.float32),
    )
    dense_sums = (
        lax.psum(split_parts[0].astype(jnp.bfloat16), "expert").astype(jnp.float32),
        lax.psum(split_parts[1].astype(jnp.bfloat16), "expert").astype(jnp.float32),
        lax.psum(split_parts[2].astype(jnp.bfloat16), "expert").astype(jnp.float32),
        lax.psum(split_parts[3].astype(jnp.bfloat16), "expert").astype(jnp.float32),
        lax.psum(split_parts[4].astype(jnp.bfloat16), "expert").astype(jnp.float32),
        lax.psum(split_parts[5].astype(jnp.bfloat16), "expert").astype(jnp.float32),
    )
    shares = tuple(dense_sums) + (split_parts[6], split_parts[7])
    return (
        mixed,
        d_tokens,
        shares[3],
        shares[0],
        shares[1],
        shares[2],
        shares[4],
        shares[5],
        shares[6],
        shares[7],
    )


def solution(mesh):
    in_specs = (
        P(("dp", "expert"), None),
        P("dp"),
        P("dp", None),
        P("dp", None),
        P("dp", None),
        P("dp"),
        P("dp", None),
        P("dp", "expert", None),
        P("dp", "expert", None),
        P(("dp", "expert"), None),
        P(),
        P(("dp", "expert"), None),
    )
    out_specs = (
        P(("dp", "expert"), None),
        P(("dp", "expert"), None),
        P("dp"),
        P("dp", None),
        P("dp", None),
        P("dp", None),
        P("dp"),
        P("dp", None),
        P("dp", "expert", None),
        P("dp", "expert", None),
    )
    return jax.shard_map(
        per_device, mesh=mesh, in_specs=in_specs, out_specs=out_specs, check_vma=False
    )
```

profile of v0, /device:TPU:0, one launch (start us, length us, event | category | flops | bytes accessed | tf_op | source)
XLA Modules:
  0.0 611.9 jit_solution(11900003558481887998)
XLA Ops:
  15.8 69.1 %all-reduce.4 = bf16[768]{0:T(1024)(128)(2,1)S(1)} all-reduce(bf16[768]{0:T(1024)(128)(2,1)S(1)} %dynamic-update-slice), channel_id=1, replica_groups=mesh['dp'=32,'expert'=4] {'dp'}, use_global_device_ids=true, to_apply=%add.4 | all-reduce | flops 768 | bytes 3072
  84.9 17.5 %all-gather = bf16[32,1,12]{2,1,0:T(2,128)(2,1)S(1)} all-gather(bf16[1,1,12]{2,1,0:T(2,128)(2,1)} %bitcast.289), channel_id=1, replica_groups=mesh['dp'=32,'expert'=4] {'dp'}, dimensions={0}, use_global_device_ids=true | all-gather | bytes 792 | tf_op jit(solution)/shard_map/all_gather | solution.py:108
  109.3 4.3 all-to-all-start
  114.4 9.6 %all-to-all-done = bf16[128,3,4,192]{0,3,1,2:T(8,128)(2,1)S(1)} async-done(((bf16[128,3,4,192]{0,3,1,2:T(8,128)(2,1)}), bf16[128,3,4,192]{0,3,1,2:T(8,128)(2,1)S(1)}, u32[]{:S(2)}, u32[]{:S(2)}) %all-to-all-start) | async-done | bytes 589856 | tf_op jit(solution)/shard_map/all_to_all | solution.py:125
  124.9 33.5 %while.28 = (s32[]{:T(128)}, bf16[3,512,64]{1,2,0:T(8,128)(2,1)S(1)}, f32[3,512]{1,0:T(4,128)}, bf16[3,512,64]{2,1,0:T(8,128)(2,1)S(1)}, bf16[3,512,64]{2,1,0:T(...) while((s32[]{:T(128)}, ...), condition=%wide.region_4.5_spmd, body=%wide.region_1.4_spmd.sunk | while | flops 68682240 | bytes 26753176 | solution.py:147
  165.3 5.2 all-to-all-done.1
  176.8 3.6 all-to-all-start.2
  181.7 5.3 all-to-all-done.2
  187.2 5.5 fusion.46
  192.7 4.2 fusion.68
  203.6 6.5 %all-to-all-done.3 = bf16[4,2,15360]{2,1,0:T(2,128)(2,1)S(1)} async-done(((bf16[4,2,15360]{2,1,0:T(2,128)(2,1)}), bf16[4,2,15360]{2,1,0:T(2,128)(2,1)S(1)}, u32[]{:S(2)}, u32[]{:S(2)}) %all-to-all-start.3) | async-done | bytes 245792 | tf_op jit(solution)/shard_map/all_to_all | solution.py:182
  215.1 3.8 all-to-all-start.4
  219.1 6.3 %all-to-all-done.4 = bf16[4,2,15360]{2,1,0:T(2,128)(2,1)S(1)} async-done(((bf16[4,2,15360]{2,1,0:T(2,128)(2,1)}), bf16[4,2,15360]{2,1,0:T(2,128)(2,1)S(1)}, u32[]{:S(2)}, u32[]{:S(2)}) %all-to-all-start.4) | async-done | bytes 245792 | tf_op jit(solution)/shard_map/all_to_all | solution.py:195
  225.6 5.3 fusion.57
  230.9 4.4 fusion.71
  242.0 4.7 fusion.42
  250.5 23.3 %concatenate.33 = bf16[768,3077]{0,1:T(8,128)(2,1)} concatenate(bf16[768,1]{0,1:T(2,128)(2,1)S(1)} %convert_element_type.239, bf16[768,4]{0,1:T(4,128)(2,1)S(1)} %convolution_convert_fusion.9, bf16[768,3072]{0,1:T(8,128)(2,1)} %fusion.42), dimensions={1} | concatenate | bytes 9452544 | tf_op jit(solution)/shard_map/concatenate | solution.py:43
  282.7 5.2 fusion.43
  287.9 6.7 %copy.185 = bf16[3072,768]{1,0:T(8,128)(2,1)} copy(bf16[3072,768]{0,1:T(8,128)(2,1)} %fusion.43) | data formatting | bytes 9437184
  296.9 91.0 %while.29 = (s32[]{:T(128)}, bf16[3,512,64]{1,2,0:T(8,128)(2,1)}, bf16[3,512,64]{1,2,0:T(8,128)(2,1)}, bf16[3,512,64]{1,2,0:T(8,128)(2,1)}, f32[3,1023]{1,0:T(4,...) while((s32[]{:T(128)}, bf16[3,512,64]{1,2,0:T(8,128)(2,1)}, ...), condition=%wide.region_17.18_spmd, body=%wide.region_14.17_spmd.sunk | while | flops 170655744 | bytes 58340700 | solution.py:258
  309.7 4.1 reshape.351
  316.8 4.3 reshape.352
  339.9 4.1 reshape.351
  347.1 4.3 reshape.352
  370.3 4.1 reshape.351
  377.5 4.3 reshape.352
  390.5 4.8 all-to-all-start.7
  396.0 10.1 %all-to-all-done.7 = bf16[512,3,1,192]{3,1,2,0:T(4,128)(2,1)S(1)} async-done(((bf16[512,3,1,192]{3,1,2,0:T(4,128)(2,1)}), bf16[512,3,1,192]{3,1,2,0:T(4,128)(2,1)S(1)}, u32[]{:S(2)}, u32[]{:S(2)}) %all-to-all-start.7) | async-done | bytes 589856 | tf_op jit(solution)/shard_map/all_to_all | solution.py:264
  417.0 124.5 %all-reduce.8 = (bf16[768]{0:T(1024)(128)(2,1)S(1)}, bf16[32,12]{1,0:T(8,128)(2,1)S(1)}) all-reduce(bf16[768]{0:T(1024)(128)(2,1)S(1)} %get-tuple-element.266, bf16[32,12]{1,0:T(8,128)(2,1)S(1)} %convolution_convert_fusion.8), channel_id=2, replica_groups=mesh['dp'=32,'expert'=4] {'dp'}, use_global_device_ids=true, to_apply=%region_20.21.clone | all-reduce | flops 1152 | bytes 4608
  548.8 11.9 %reduce-scatter.6.cloned.1.call-done = bf16[24,3072]{1,0:T(8,128)(2,1)} async-done(((bf16[768,3072]{1,0:T(8,128)(2,1)}), bf16[24,3072]{1,0:T(8,128)(2,1)}) %reduce-scatter.6.cloned.1.call-update) | async-done | bytes 147472 | tf_op jit(solution)/shard_map/reduce_scatter | solution.py:37
  564.0 17.3 %all-reduce.9 = (bf16[24]{0:T(256)(128)(2,1)S(1)}, bf16[24,768]{1,0:T(8,128)(2,1)S(1)}, bf16[1,12]{1,0:T(2,128)(2,1)S(1)}, bf16[24]{0:T(256)(128)(2,1)S(1)}, bf16[24,4]{0,1:T(4,128)(2,1)S(1)}) all-reduce(bf16[24]{0:T(256)(128)(2,1)S(1)} %dynamic-slice.6, ...), channel_id=1, replica_groups=mesh['dp'=32,'expert'=4] {'expert'}, use_global_device_ids=true, to_apply=%region_21.22 | all-reduce | flops 18588 | bytes 74352 | tf_op jit(solution)/shard_map/psum | solution.py:314
  584.1 19.1 %all-reduce.13.cloned.1.call-done = bf16[24,2304]{1,0:T(8,128)(2,1)} async-done(((bf16[24,2304]{1,0:T(8,128)(2,1)}), bf16[24,2304]{1,0:T(8,128)(2,1)}) %all-reduce.13.cloned.1.call-update) | async-done | bytes 110608 | tf_op jit(solution)/shard_map/psum | solution.py:311
  (346 shorter events, 191.6 us)
Async XLA Ops:
  7.2 97.4 %all-gather.5.cloned.1.call-start = ((), (), s32[]{:S(2)}) async-start(), calls=%async_computation.10 | async-start | bytes 4866048 | tf_op jit(solution)/shard_map/all_gather | solution.py:12
  8.8 155.4 %all-gather.7.cloned.1.call-start = ((), (), s32[]{:S(2)}) async-start(), calls=%async_computation.11 | async-start | bytes 5068800 | tf_op jit(solution)/shard_map/all_gather | solution.py:22
  12.2 180.6 %all-gather.9.cloned.1.call-start = ((), (), s32[]{:S(2)}) async-start(), calls=%async_computation.12 | async-start | bytes 4866048 | tf_op jit(solution)/shard_map/all_gather | solution.py:111
  84.9 19.8 %copy-start.17 = (f32[768]{0:T(1024)}, f32[768]{0:T(1024)S(1)}, u32[]{:S(2)}) copy-start(f32[768]{0:T(1024)S(1)} %convert_element_type.205) | copy-start | bytes 9220
  109.3 14.8 %all-to-all-start = ((bf16[128,3,4,192]{0,3,1,2:T(8,128)(2,1)}), bf16[128,3,4,192]{0,3,1,2:T(8,128)(2,1)S(1)}, u32[]{:S(2)}, u32[]{:S(2)}) async-start(bf16[128,3,4,192]{0,3,1,2:T(8,128)(2,1)} %copy.150), calls=%async_computation | async-start | bytes 1179648 | tf_op jit(solution)/shard_map/all_to_all | solution.py:125
  124.9 39.3 %copy-start.28 = (s32[128]{0:T(128)S(1)}, s32[128]{0:T(128)}, u32[]{:S(2)}) copy-start(s32[128]{0:T(128)} %select_reduce_fusion) | copy-start | bytes 1540
  159.6 11.6 %copy-start.8 = (bf16[128,768]{1,0:T(8,128)(2,1)S(1)}, bf16[128,768]{1,0:T(8,128)(2,1)}, u32[]{:S(2)}) copy-start(bf16[128,768]{1,0:T(8,128)(2,1)} %param.16) | copy-start | bytes 589828
  160.8 9.7 %all-to-all-start.1 = ((bf16[4,2,12288]{2,1,0:T(2,128)(2,1)}), bf16[4,2,12288]{2,1,0:T(2,128)(2,1)S(1)}, u32[]{:S(2)}, u32[]{:S(2)}) async-start(bf16[4,2,12288]{2,1,0:T(2,128)(2,1)} %reshape.335), calls=%async_computation.1 | async-start | bytes 393216 | tf_op jit(solution)/shard_map/all_to_all | solution.py:149
  173.1 14.1 %copy-start.26 = (f32[128]{0:T(128)}, f32[128]{0:T(128)S(1)}, u32[]{:S(2)}) copy-start(f32[128]{0:T(128)S(1)} %get-tuple-element.324) | copy-start | bytes 1540
  176.8 10.2 %all-to-all-start.2 = ((bf16[4,2,15360]{2,1,0:T(2,128)(2,1)}), bf16[4,2,15360]{2,1,0:T(2,128)(2,1)S(1)}, u32[]{:S(2)}, u32[]{:S(2)}) async-start(bf16[4,2,15360]{2,1,0:T(2,128)(2,1)} %reshape.337), calls=%async_computation.2 | async-start | bytes 491520 | tf_op jit(solution)/shard_map/all_to_all | solution.py:175
  197.0 13.4 %copy-start.12 = (bf16[128,768]{1,0:T(8,128)(2,1)S(1)}, bf16[128,768]{1,0:T(8,128)(2,1)}, u32[]{:S(2)}) copy-start(bf16[128,768]{1,0:T(8,128)(2,1)} %param.27) | copy-start | bytes 589828
  200.2 10.0 %all-to-all-start.3 = ((bf16[4,2,15360]{2,1,0:T(2,128)(2,1)}), bf16[4,2,15360]{2,1,0:T(2,128)(2,1)S(1)}, u32[]{:S(2)}, u32[]{:S(2)}) async-start(bf16[4,2,15360]{2,1,0:T(2,128)(2,1)} %reshape.339), calls=%async_computation.3 | async-start | bytes 491520 | tf_op jit(solution)/shard_map/all_to_all | solution.py:182
  215.1 10.3 %all-to-all-start.4 = ((bf16[4,2,15360]{2,1,0:T(2,128)(2,1)}), bf16[4,2,15360]{2,1,0:T(2,128)(2,1)S(1)}, u32[]{:S(2)}, u32[]{:S(2)}) async-start(bf16[4,2,15360]{2,1,0:T(2,128)(2,1)} %reshape.341), calls=%async_computation.4 | async-start | bytes 491520 | tf_op jit(solution)/shard_map/all_to_all | solution.py:195
  238.5 10.0 %all-to-all-start.5 = ((bf16[4,2,15360]{2,1,0:T(2,128)(2,1)}), bf16[4,2,15360]{2,1,0:T(2,128)(2,1)S(1)}, u32[]{:S(2)}, u32[]{:S(2)}) async-start(bf16[4,2,15360]{2,1,0:T(2,128)(2,1)} %reshape.343), calls=%async_computation.5 | async-start | bytes 491520 | tf_op jit(solution)/shard_map/all_to_all | solution.py:216
  242.0 301.1 %all-reduce.15.cloned.1.call-start = ((), (), s32[]{:S(2)}) async-start(), calls=%async_computation.16 | async-start | bytes 9461760
  279.1 15.5 %all-to-all-start.6 = ((bf16[128,4,192]{0,2,1:T(8,128)(2,1)}), bf16[128,4,192]{0,2,1:T(8,128)(2,1)S(1)}, u32[]{:S(2)}, u32[]{:S(2)}) async-start(bf16[128,4,192]{0,2,1:T(8,128)(2,1)} %bitcast.47), calls=%async_computation.6 | async-start | bytes 393216 | tf_op jit(solution)/shard_map/all_to_all | solution.py:231
  282.4 265.3 %reduce-scatter.8.cloned.1.call-start = ((), (), s32[]{:S(2)}) async-start(), calls=%async_computation.15 | async-start | bytes 4866048
  296.9 9.1 %copy-start.6 = (bf16[3,512,64]{1,2,0:T(8,128)(2,1)}, bf16[3,512,64]{1,2,0:T(8,128)(2,1)S(1)}, u32[]{:S(2)}) copy-start(bf16[3,512,64]{1,2,0:T(8,128)(2,1)S(1)} %get-tuple-element.519) | copy-start | bytes 589828 | tf_op jit(solution)/shard_map/while
  296.9 10.1 %copy-start = (bf16[3,512,64]{2,1,0:T(8,128)(2,1)}, bf16[3,512,64]{2,1,0:T(8,128)(2,1)S(1)}, u32[]{:S(2)}) copy-start(bf16[3,512,64]{2,1,0:T(8,128)(2,1)S(1)} %get-tuple-element.516) | copy-start | bytes 589828 | tf_op jit(solution)/shard_map/while
  327.2 9.1 %copy-start.2 = (bf16[3,512,64]{2,1,0:T(8,128)(2,1)}, bf16[3,512,64]{2,1,0:T(8,128)(2,1)S(1)}, u32[]{:S(2)}) copy-start(bf16[3,512,64]{2,1,0:T(8,128)(2,1)S(1)} %get-tuple-element.520) | copy-start | bytes 589828 | tf_op jit(solution)/shard_map/while
  327.2 9.1 %copy-start.6 = (bf16[3,512,64]{1,2,0:T(8,128)(2,1)}, bf16[3,512,64]{1,2,0:T(8,128)(2,1)S(1)}, u32[]{:S(2)}) copy-start(bf16[3,512,64]{1,2,0:T(8,128)(2,1)S(1)} %get-tuple-element.519) | copy-start | bytes 589828 | tf_op jit(solution)/shard_map/while
  327.2 10.1 %copy-start = (bf16[3,512,64]{2,1,0:T(8,128)(2,1)}, bf16[3,512,64]{2,1,0:T(8,128)(2,1)S(1)}, u32[]{:S(2)}) copy-start(bf16[3,512,64]{2,1,0:T(8,128)(2,1)S(1)} %get-tuple-element.516) | copy-start | bytes 589828 | tf_op jit(solution)/shard_map/while
  357.4 9.3 %copy-start.2 = (bf16[3,512,64]{2,1,0:T(8,128)(2,1)}, bf16[3,512,64]{2,1,0:T(8,128)(2,1)S(1)}, u32[]{:S(2)}) copy-start(bf16[3,512,64]{2,1,0:T(8,128)(2,1)S(1)} %get-tuple-element.520) | copy-start | bytes 589828 | tf_op jit(solution)/shard_map/while
  357.4 9.3 %copy-start.6 = (bf16[3,512,64]{1,2,0:T(8,128)(2,1)}, bf16[3,512,64]{1,2,0:T(8,128)(2,1)S(1)}, u32[]{:S(2)}) copy-start(bf16[3,512,64]{1,2,0:T(8,128)(2,1)S(1)} %get-tuple-element.519) | copy-start | bytes 589828 | tf_op jit(solution)/shard_map/while
  357.4 10.3 %copy-start = (bf16[3,512,64]{2,1,0:T(8,128)(2,1)}, bf16[3,512,64]{2,1,0:T(8,128)(2,1)S(1)}, u32[]{:S(2)}) copy-start(bf16[3,512,64]{2,1,0:T(8,128)(2,1)S(1)} %get-tuple-element.516) | copy-start | bytes 589828 | tf_op jit(solution)/shard_map/while
  390.5 15.7 %all-to-all-start.7 = ((bf16[512,3,1,192]{3,1,2,0:T(4,128)(2,1)}), bf16[512,3,1,192]{3,1,2,0:T(4,128)(2,1)S(1)}, u32[]{:S(2)}, u32[]{:S(2)}) async-start(bf16[512,3,1,192]{3,1,2,0:T(4,128)(2,1)} %copy.173), calls=%async_computation.7 | async-start | bytes 2097152 | tf_op jit(solution)/shard_map/all_to_all | solution.py:264
  395.3 12.4 %copy-start.9 = (bf16[128,768]{1,0:T(8,128)(2,1)S(1)}, bf16[128,768]{1,0:T(8,128)(2,1)}, u32[]{:S(2)}) copy-start(bf16[128,768]{1,0:T(8,128)(2,1)} %param.16) | copy-start | bytes 589828
  395.3 12.4 %copy-start.18 = (f32[768]{0:T(1024)S(1)}, f32[768]{0:T(1024)}, u32[]{:S(2)}) copy-start(f32[768]{0:T(1024)} %copy-done.17) | copy-start | bytes 9220
  395.3 12.4 %copy-start.23 = (f32[128]{0:T(128)S(1)}, f32[128]{0:T(128)}, u32[]{:S(2)}) copy-start(f32[128]{0:T(128)} %copy-done.22) | copy-start | bytes 1540
  395.3 165.4 %reduce-scatter.6.cloned.1.call-start = ((), (), s32[]{:S(2)}) async-start(), calls=%async_computation.13 | async-start | bytes 4866048 | tf_op jit(solution)/shard_map/reduce_scatter | solution.py:37
  411.8 191.4 %all-reduce.13.cloned.1.call-start = ((), (), s32[]{:S(2)}) async-start(), calls=%async_computation.14 | async-start | bytes 221184 | tf_op jit(solution)/shard_map/psum | solution.py:311
  413.4 128.8 %copy-start.25 = (f32[128]{0:T(128)S(1)}, f32[128]{0:T(128)}, u32[]{:S(2)}) copy-start(f32[128]{0:T(128)} %copy-done.24) | copy-start | bytes 1540
  (38 other events, 124.2 us)
Sparse Core Ops, SparseCore 0:
  10.8 49.5 all-gather.4
  63.3 46.4 all-gather.6
  112.0 46.2 all-gather.8
  274.0 112.7 all-reduce.14
  390.4 83.2 reduce-scatter.7
  477.7 82.9 reduce-scatter.5
  563.6 39.5 all-reduce.12
where the time goes:
time: 623 us; the launch traced here: 612 us
  blocking collectives  228 us (37%)
  local copies, waits for them, and re-layouts  167 us (27%)
  waiting for transfers between devices  76.7 us (12%)
  matrix products  58.7 us (9%)
  other arithmetic  33.6 us (5%)
  starting transfers between devices  30.6 us (5%)
  between operations  16.5 us (3%)
    unnamed x2, blocking collectives  194 us
    reshape x9, local copies, waits for them, and re-layouts, toeplitz(): return tiled.reshape(query_rows, period - 1)[:, :key_rows]  29.7 us
    concatenate x1, local copies, waits for them, and re-layouts, sent_together_3(): both = jnp.concatenate(columns, axis=along)  23.3 us
    unnamed x71, local copies, waits for them, and re-layouts  21.3 us
    psum x1, waiting for transfers between devices, per_device(): lax.psum(split_parts[0].astype(jnp.bfloat16), 'expert').astype(jnp.float32)  19.1 us
    all_gather x1, blocking collectives, per_device(): lax.all_gather(bias_table, 'dp', axis=0, tiled=True)  17.5 us
    another operation x12, local copies, waits for them, and re-layouts, toeplitz(): tiled = jnp.tile(rolled, query_rows)[:query_rows * (period - 1)]  17.5 us
    psum x1, blocking collectives, per_device(): lax.psum(split_parts[3].astype(jnp.bfloat16), 'expert').astype(jnp.float32)  17.3 us
  transfers between devices with their start and end apart: 15, of which 9 were waited for; matrix products, arithmetic and copies ran while one was open for 30% of the time, Pallas kernels for 0%

commit v1 on v0

v1 whole, which is shorter than its diff:
```python
import jax
import jax.numpy as jnp
from jax import lax
from jax.experimental import pallas as pl
from jax.experimental.pallas import tpu as pltpu
from jax.sharding import PartitionSpec as P

epsilon = 1e-06
highest = lax.Precision.HIGHEST
bf16 = jnp.bfloat16
f32 = jnp.float32
NT = (((1,), (1,)), ((), ()))
TN = (((0,), (0,)), ((), ()))


def mm(a, b):
    return jnp.dot(a, b, preferred_element_type=f32)


def mm_nt(a, b):
    return lax.dot_general(a, b, NT, preferred_element_type=f32)


def mm_tn(a, b):
    return lax.dot_general(a, b, TN, preferred_element_type=f32)


def stack_heads(pair):
    left = lax.broadcasted_iota(jnp.int32, pair.shape, 1) < 64
    zero = jnp.zeros_like(pair)
    return jnp.concatenate([jnp.where(left, pair, zero), jnp.where(left, zero, pair)], 0)


def join_pair(stacked):
    rows = stacked.shape[0] // 2
    left = lax.broadcasted_iota(jnp.int32, (rows, 128), 1) < 64
    return jnp.where(left, stacked[:rows], stacked[rows:])


def toeplitz(window_row, rows, keys):
    width = window_row.shape[1]
    wide = jnp.broadcast_to(window_row, (rows, width))
    rolled = pltpu.roll(wide, width - (rows - 1), 1, stride=1, stride_axis=0)
    return rolled[:, :keys]


def diagonal_sums(block, width):
    rows, keys = block.shape
    wide = jnp.concatenate([block, jnp.zeros((rows, width - keys), f32)], 1)
    half = rows // 2
    while half >= 8:
        wide = wide[:half] + pltpu.roll(wide[half:], width - half, 1)
        half //= 2
    row = lax.broadcasted_iota(jnp.int32, wide.shape, 0)
    for bit in (1, 2, 4):
        wide = jnp.where((row & bit) != 0, pltpu.roll(wide, width - bit, 1), wide)
    total = jnp.sum(wide, 0, keepdims=True)
    return pltpu.roll(total, rows - 1, 1)


def attention_forward(query, key, value, window, out, weights):
    pair = pl.program_id(0)
    rows = query.shape[0]
    keys = key.shape[0]
    bias = jnp.concatenate(
        [toeplitz(window[pl.ds(2 * pair + j, 1), :], rows, keys) for j in (0, 1)], 0
    )
    scores = mm_nt(stack_heads(query[...]), key[...]) + bias
    top = jnp.max(scores, -1, keepdims=True)
    raised = jnp.exp(scores - top)
    probability = raised / jnp.sum(raised, -1, keepdims=True)
    weights[...] = probability.reshape(2, rows, keys)
    out[...] = join_pair(mm(probability.astype(bf16), value[...])).astype(bf16)


def attention_backward(query, key, value, weights, d_out, d_query, d_key, d_value, d_window):
    rows = query.shape[0]
    keys = key.shape[0]
    probability = weights[...].reshape(2 * rows, keys)
    d_stack = stack_heads(d_out[...])
    d_weights = mm_nt(d_stack, value[...])
    d_value[...] = mm_tn(probability.astype(bf16), d_stack).astype(bf16)
    d_scores = probability * (
        d_weights - jnp.sum(probability * d_weights, -1, keepdims=True)
    )
    for j in (0, 1):
        d_window[0, j : j + 1, :] = diagonal_sums(
            d_scores[j * rows : (j + 1) * rows], d_window.shape[2]
        )
    low = d_scores.astype(bf16)
    d_query[...] = join_pair(mm(low, key[...])).astype(bf16)
    d_key[...] = mm_tn(low, stack_heads(query[...])).astype(bf16)


def rms_forward(values, gain):
    r = lax.rsqrt(jnp.mean(values * values, -1, keepdims=True) + epsilon)
    return r, values * r * gain


def rms_backward(values, r, gain, grad):
    u = grad * gain
    d_values = r * u - values * (r * r * r) * jnp.mean(u * values, -1, keepdims=True)
    return d_values, jnp.sum(grad * values * r, 0)


MESH = pl.DeviceIdType.MESH


class Place:
    def __init__(self):
        d = lax.axis_index("dp")
        self.d = d
        self.x = lax.axis_index("expert")
        self.c = lax.rem(d, 2)
        self.z = lax.rem(lax.div(d, 2), 4)
        self.y = lax.div(d, 8)
        self.p = self.z * (1 - self.c) + self.y * self.c
        self.q = self.y * (1 - self.c) + self.z * self.c

    def at(self, p, q):
        y = q * (1 - self.c) + p * self.c
        z = p * (1 - self.c) + q * self.c
        return ((y * 4 + z) * 2 + self.c, self.x)

    def along_p(self, by):
        return self.at(lax.rem(self.p + by, 4), self.q)

    def along_q(self, by):
        return self.at(self.p, lax.rem(self.q + by, 4))

    def along_x(self, by):
        return (self.d, lax.rem(self.x + by, 4))

    def sibling(self):
        return (self.d + 1 - 2 * self.c, self.x)

    def each_core(self, body):
        pl.when(self.c == 0)(lambda: body(0))
        pl.when(self.c == 1)(lambda: body(1))

    def barrier(self, with_x):
        peers = [self.sibling()] + [self.along_p(i) for i in (1, 2, 3)]
        peers += [self.along_q(i) for i in (1, 2, 3)]
        if with_x:
            peers += [self.along_x(i) for i in (1, 2, 3)]
        sem = pltpu.get_barrier_semaphore()
        for peer in peers:
            pl.semaphore_signal(sem, inc=1, device_id=peer, device_id_type=MESH)
        pl.semaphore_wait(sem, len(peers))


def remote(src, dst, send, recv, to):
    return pltpu.make_async_remote_copy(
        src_ref=src, dst_ref=dst, send_sem=send, recv_sem=recv, device_id=to, device_id_type=MESH
    )


def block_of(ref, tall, k, p, q):
    y, z = (q, p) if k == 0 else (p, q)
    return ref.at[y, z, k] if tall else ref.at[k, y, z]


def slab_of(ref, tall, k, q, low=0, count=4):
    y, z = (q, pl.ds(low, count)) if k == 0 else (pl.ds(low, count), q)
    return ref.at[y, z, k] if tall else ref.at[k, y, z]


class Gather:
    sends = 11
    recvs = 11

    def __init__(self, place, ref, tall, send, recv, number):
        self.o, self.ref, self.tall, self.send, self.recv = place, ref, tall, send, recv
        self.number = number

    def block(self, k, by):
        return block_of(self.ref, self.tall, k, lax.rem(self.o.p + by, 4), self.o.q)

    def slab(self, k, by, low=0, count=4):
        return slab_of(self.ref, self.tall, k, lax.rem(self.o.q + by, 4), low, count)

    def go(self, part, s, r, to):
        def body(k):
            src = part(k)
            remote(src, src, self.send.at[s], self.recv.at[r], to).start()

        self.o.each_core(body)

    def arrived(self, r, count):
        if count == 1:
            view = block_of(self.ref, self.tall, 0, 0, 0)
        else:
            view = slab_of(self.ref, self.tall, 0, 0, 0, count)
        remote(view, view, self.send.at[0], self.recv.at[r], self.o.sibling()).wait_recv()

    def sent(self, s, count):
        if count == 1:
            view = block_of(self.ref, self.tall, 0, 0, 0)
        else:
            view = slab_of(self.ref, self.tall, 0, 0, 0, count)
        remote(view, view, self.send.at[s], self.recv.at[0], self.o.sibling()).wait_send()

    def ring_one(self):
        self.go(lambda k: self.block(k, 0), 0, 0, self.o.along_p(1))
        self.go(lambda k: self.block(k, 0), 1, 1, self.o.along_p(3))

    def ring_one_far(self):
        self.arrived(0, 1)
        self.arrived(1, 1)
        if self.number % 2 == 0:
            self.go(lambda k: self.block(k, 3), 2, 2, self.o.along_p(1))
        else:
            self.go(lambda k: self.block(k, 1), 2, 2, self.o.along_p(3))

    def ring_two(self):
        self.arrived(2, 1)
        self.go(lambda k: self.slab(k, 0), 3, 3, self.o.along_q(1))
        self.go(lambda k: self.slab(k, 0), 4, 4, self.o.along_q(3))
        self.go(lambda k: self.slab(k, 0), 7, 7, self.o.sibling())

    def ring_two_far(self):
        self.arrived(3, 4)
        self.go(lambda k: self.slab(k, 3, 0, 2), 5, 5, self.o.along_q(1))
        self.arrived(4, 4)
        self.go(lambda k: self.slab(k, 1, 2, 2), 6, 6, self.o.along_q(3))
        self.go(lambda k: self.slab(k, 3), 8, 8, self.o.sibling())
        self.go(lambda k: self.slab(k, 1), 9, 9, self.o.sibling())

    def last(self):
        self.arrived(5, 2)
        self.arrived(6, 2)
        self.go(lambda k: self.slab(k, 2), 10, 10, self.o.sibling())

    def finish(self):
        for r in (7, 8, 9, 10):
            self.arrived(r, 4)

    def drain(self):
        for s, count in ((0, 1), (1, 1), (2, 1), (3, 4), (4, 4), (5, 2), (6, 2), (7, 4), (8, 4), (9, 4), (10, 4)):
            self.sent(s, count)


class SmallSum:
    def __init__(self, place, value, arrivals, send, recv, with_x):
        self.o, self.value, self.arrivals, self.send, self.recv = place, value, arrivals, send, recv
        o = place
        self.steps = [[o.sibling()], [o.along_p(i) for i in (1, 2, 3)], [o.along_q(i) for i in (1, 2, 3)]]
        if with_x:
            self.steps.append([o.along_x(i) for i in (1, 2, 3)])
        self.copies = []
        n = 0
        for s, peers in enumerate(self.steps):
            row = []
            for peer in peers:
                row.append(
                    remote(value.at[s], arrivals.at[n], send.at[n], recv.at[n], peer)
                )
                n += 1
            self.copies.append(row)

    def start(self, s):
        for copy in self.copies[s]:
            copy.start()

    def add(self, s):
        first = sum(len(row) for row in self.copies[:s])
        total = self.value[s]
        for i, copy in enumerate(self.copies[s]):
            copy.wait_recv()
            total = total + self.arrivals[first + i]
        self.value[s + 1] = total

    def drain(self):
        for row in self.copies:
            for copy in row:
                copy.wait_send()


def place_small(o, pack):
    row = lax.broadcasted_iota(jnp.int32, (32, 1024), 0)
    lane = lax.broadcasted_iota(jnp.int32, (32, 1024), 1)
    target = jnp.where(row < 24, 24 * o.d + row, jnp.where(row == 24, 768 + o.d, -1))
    hit = jnp.where(lane == target, 1.0, 0.0)
    spread = mm_tn(pack[...].astype(bf16), hit.astype(bf16))
    return jnp.concatenate(
        [spread[0:8, :768], spread[8:16, 768:896], spread[16:24, 768:896]], 1
    )


def meet(o, halves, stage, other, sem):
    at = 0
    for ref in halves:
        n = ref.shape[1] // 2
        own = pl.ds(pl.multiple_of(o.c * n, 128), n)
        theirs = pl.ds(pl.multiple_of((1 - o.c) * n, 128), n)
        stage[pl.ds(pl.multiple_of(24 * o.c, 8), 24), at : at + n] = ref[:, own].astype(f32)
        other[:, at : at + n] = ref[:, theirs].astype(f32)
        at += n
    return remote(
        other, stage.at[pl.ds(pl.multiple_of(24 * o.c, 8), 24)], sem.at[0], sem.at[1], o.sibling()
    )


def gather_kernel(
    w_qkv, w_ao, w_in, w_out, pack, g_qkv, g_ao, g_in, g_out, small,
    stage, other, pair_sem, sends, recvs, arrivals, small_send, small_recv,
):
    o = Place()
    o.barrier(False)
    flows = [
        Gather(o, ref, tall, sends.at[i], recvs.at[i], i)
        for i, (ref, tall) in enumerate(((g_qkv, 0), (g_ao, 0), (g_in, 0), (g_out, 1)))
    ]
    qkv, ao, win, wout = flows
    pair = meet(o, (w_qkv, w_ao, w_in), stage, other, pair_sem)
    pair.start()
    tot = SmallSum(o, small, arrivals, small_send, small_recv, False)
    small[0] = place_small(o, pack)
    tot.start(0)
    g_out[o.y, o.z, o.c] = w_out[...]
    pair.wait_recv()
    at = 0
    for ref in (g_qkv, g_ao, g_in):
        n = ref.shape[-1]
        ref[o.c, o.y, o.z] = stage[:, at : at + n].astype(bf16)
        at += n
    qkv.ring_one()
    tot.add(0)
    tot.start(1)
    qkv.ring_one_far()
    qkv.ring_two()
    for f in (ao, win, wout):
        f.ring_one()
    tot.add(1)
    tot.start(2)
    for f in (ao, win, wout):
        f.ring_one_far()
    qkv.ring_two_far()
    for f in (ao, win, wout):
        f.ring_two()
    tot.add(2)
    qkv.last()
    ao.ring_two_far()
    qkv.finish()
    ao.last()
    win.ring_two_far()
    ao.finish()
    win.last()
    wout.ring_two_far()
    win.finish()
    wout.last()
    wout.finish()
    pair.wait_send()
    tot.drain()
    for f in flows:
        f.drain()


def gather_all(w_qkv, w_ao, w_in, w_out, pack):
    vm = pl.BlockSpec(memory_space=pltpu.VMEM)
    return pl.pallas_call(
        gather_kernel,
        in_specs=[vm] * 5,
        out_specs=[vm] * 5,
        out_shape=[
            jax.ShapeDtypeStruct((2, 4, 4, 48, 1152), bf16),
            jax.ShapeDtypeStruct((2, 4, 4, 48, 384), bf16),
            jax.ShapeDtypeStruct((2, 4, 4, 48, 1536), bf16),
            jax.ShapeDtypeStruct((4, 4, 2, 96, 768), bf16),
            jax.ShapeDtypeStruct((4, 8, 1024), f32),
        ],
        scratch_shapes=[
            pltpu.VMEM((48, 3072), f32),
            pltpu.VMEM((24, 3072), f32),
            pltpu.SemaphoreType.DMA((2,)),
            pltpu.SemaphoreType.DMA((4, 11)),
            pltpu.SemaphoreType.DMA((4, 11)),
            pltpu.VMEM((7, 8, 1024), f32),
            pltpu.SemaphoreType.DMA((7,)),
            pltpu.SemaphoreType.DMA((7,)),
        ],
        compiler_params=pltpu.CompilerParams(
            collective_id=0, has_side_effects=True, vmem_limit_bytes=48 * 2**20
        ),
    )(w_qkv, w_ao, w_in, w_out, pack)


def per_device(
    tokens, norm_attn, w_qkv, w_attn_out, bias_table, norm_moe, router, w_in, w_out, routes, buckets, cotangent
):
    rows, width = tokens.shape
    dp = lax.axis_index("dp")
    ex = lax.axis_index("expert")
    groups = 4
    keys = rows * groups
    heads = 12
    window_width = keys + rows

    own = norm_attn.shape[0]
    pack = jnp.concatenate([norm_attn[:, None], norm_moe[:, None], router, jnp.zeros((own, 122), bf16)], 1)
    last = jnp.concatenate([jnp.zeros((1, 8), bf16), bias_table, jnp.zeros((1, 108), bf16)], 1)
    pack = jnp.concatenate([pack, last, jnp.zeros((7, 128), bf16)], 0).astype(f32)
    g_qkv, g_ao, g_in, g_out, small = gather_all(w_qkv, w_attn_out, w_in[:, 0], w_out[:, 0], pack)
    small = small[3]
    full_qkv = jnp.concatenate([g_qkv[0].reshape(768, -1), g_qkv[1].reshape(768, -1)], 1)
    full_out = jnp.concatenate([g_ao[0].reshape(768, -1), g_ao[1].reshape(768, -1)], 1)
    full_in = jnp.concatenate([g_in[0].reshape(768, -1), g_in[1].reshape(768, -1)], 1)
    full_outw = g_out.reshape(3072, 768)
    gain_one, gain_two, router_t = small[0:1, :768], small[1:2, :768], small[2:6, :768]
    table_full = jnp.concatenate([small[:8, 768:800], small[:4, 896:928]], 0)

    x = tokens.astype(f32)
    r_one, normed = rms_forward(x, gain_one)
    normed = normed.astype(bf16)
    projected = mm(normed, full_qkv).astype(bf16)
    query = projected[:, :768]
    kv = lax.all_gather(projected[:, 768:], "expert", axis=0, tiled=True)
    key, value = kv[:, :768], kv[:, 768:]
    padded = jnp.concatenate([buckets, jnp.zeros((1,), jnp.int32)])
    bucket_window = lax.dynamic_slice_in_dim(padded, (groups - 1 - ex) * rows, window_width, 0)
    picks = (bucket_window[None, :] == jnp.arange(32, dtype=jnp.int32)[:, None]).astype(f32)
    window = jnp.concatenate(
        [jnp.dot(table_full, picks, precision=highest), jnp.zeros((4, window_width), f32)], 0
    )

    pairs = heads // 2
    heads_out, weights = pl.pallas_call(
        attention_forward,
        grid=(pairs,),
        in_specs=[
            pl.BlockSpec((rows, 128), lambda p: (0, p)),
            pl.BlockSpec((keys, 128), lambda p: (0, p)),
            pl.BlockSpec((keys, 128), lambda p: (0, p)),
            pl.BlockSpec((16, window_width), lambda p: (0, 0)),
        ],
        out_specs=[
            pl.BlockSpec((rows, 128), lambda p: (0, p)),
            pl.BlockSpec((2, rows, keys), lambda p: (p, 0, 0)),
        ],
        out_shape=[
            jax.ShapeDtypeStruct((rows, width), bf16),
            jax.ShapeDtypeStruct((heads, rows, keys), f32),
        ],
        compiler_params=pltpu.CompilerParams(vmem_limit_bytes=32 * 2**20),
    )(query, key, value, window)

    after_attn = x + mm(heads_out, full_out)
    r_two, moe_input = rms_forward(after_attn, gain_two)
    moe_input = moe_input.astype(bf16)
    logits = jnp.dot(moe_input.astype(f32), router_t.T, precision=highest)
    probs = jax.nn.softmax(logits, -1)
    chosen_int = (routes == jnp.arange(4, dtype=jnp.int32)[None, :]).astype(jnp.int32)
    chosen = chosen_int.astype(f32)
    gate = jnp.sum(probs * chosen, -1, keepdims=True)
    slots = 48
    slot = jnp.sum((jnp.cumsum(chosen_int, 0) - 1) * chosen_int, -1)
    column = routes[:, 0] * slots + slot
    placing = (column[:, None] == jnp.arange(4 * slots, dtype=jnp.int32)[None, :]).astype(bf16)
    upstream = cotangent.astype(f32)
    d_combined = (gate * upstream).astype(bf16)
    outgoing = mm_tn(placing, jnp.concatenate([moe_input, d_combined], 1)).astype(bf16)
    incoming = lax.all_to_all(outgoing, "expert", split_axis=0, concat_axis=0, tiled=True)
    sent, d_result = incoming[:, :768], incoming[:, 768:]
    hidden = mm(sent, full_in)
    activated, gelu_back = jax.vjp(jax.nn.gelu, hidden)
    act_low = activated.astype(bf16)
    result = mm(act_low, full_outw).astype(bf16)
    d_act = mm_nt(d_result, full_outw)
    d_hidden = gelu_back(d_act)[0].astype(bf16)
    grad_w_out = mm_tn(act_low, d_result).astype(bf16)
    grad_w_in = mm_tn(sent, d_hidden).astype(bf16)
    out_in = lax.psum_scatter(grad_w_in, "dp", scatter_dimension=0, tiled=True)
    out_outw = lax.psum_scatter(grad_w_out, "dp", scatter_dimension=0, tiled=True)
    d_incoming = mm_nt(d_hidden, full_in).astype(bf16)
    back = lax.all_to_all(
        jnp.concatenate([result, d_incoming], 1), "expert", split_axis=0, concat_axis=0, tiled=True
    )
    returned = mm(placing, back)
    combined, d_moe = returned[:, :768], returned[:, 768:]
    mixed = (after_attn + gate * combined).astype(bf16)
    d_gate = jnp.sum(upstream * combined, -1, keepdims=True)
    d_logits = probs * (d_gate * chosen - d_gate * gate)
    grad_router = jnp.dot(d_logits.T, moe_input.astype(f32), precision=highest)
    d_moe = d_moe + jnp.dot(d_logits, router_t, precision=highest)
    d_after, grad_norm_two = rms_backward(after_attn, r_two, gain_two, d_moe)
    d_after = d_after + upstream
    d_attn = d_after.astype(bf16)
    grad_attn_out = mm_tn(heads_out, d_attn).astype(bf16)
    d_heads = mm_nt(d_attn, full_out).astype(bf16)

    d_query, d_key, d_value, d_window = pl.pallas_call(
        attention_backward,
        grid=(pairs,),
        in_specs=[
            pl.BlockSpec((rows, 128), lambda p: (0, p)),
            pl.BlockSpec((keys, 128), lambda p: (0, p)),
            pl.BlockSpec((keys, 128), lambda p: (0, p)),
            pl.BlockSpec((2, rows, keys), lambda p: (p, 0, 0)),
            pl.BlockSpec((rows, 128), lambda p: (0, p)),
        ],
        out_specs=[
            pl.BlockSpec((rows, 128), lambda p: (0, p)),
            pl.BlockSpec((keys, 128), lambda p: (0, p)),
            pl.BlockSpec((keys, 128), lambda p: (0, p)),
            pl.BlockSpec((1, 8, window_width), lambda p: (p, 0, 0)),
        ],
        out_shape=[
            jax.ShapeDtypeStruct((rows, width), bf16),
            jax.ShapeDtypeStruct((keys, width), bf16),
            jax.ShapeDtypeStruct((keys, width), bf16),
            jax.ShapeDtypeStruct((pairs, 8, window_width), f32),
        ],
        compiler_params=pltpu.CompilerParams(vmem_limit_bytes=32 * 2**20),
    )(query, key, value, weights, d_heads)
    d_window = d_window[:, :2].reshape(heads, window_width)
    grad_table_t = lax.dot_general(d_window, picks, NT, precision=highest)
    d_kv = jnp.concatenate([d_key, d_value], 1).reshape(groups, rows, 2 * width)
    d_kv = lax.all_to_all(d_kv, "expert", split_axis=0, concat_axis=0, tiled=True)
    d_kv = jnp.sum(d_kv.astype(f32), 0).astype(bf16)
    d_projected = jnp.concatenate([d_query, d_kv], 1)
    grad_qkv = mm_tn(normed, d_projected).astype(bf16)
    d_normed = mm_nt(d_projected, full_qkv)
    d_resid, grad_norm_one = rms_backward(x, r_one, gain_one, d_normed)
    d_tokens = (d_after + d_resid).astype(bf16)

    dense = lax.psum_scatter(
        jnp.concatenate([grad_qkv, grad_attn_out], 1), "dp", scatter_dimension=0, tiled=True
    )
    dense = lax.psum(dense.astype(bf16), "expert").astype(f32)
    small_grads = jnp.concatenate(
        [
            jnp.concatenate(
                [grad_norm_one[None], grad_norm_two[None], grad_router, jnp.zeros((2, 768), f32)], 0
            ),
            jnp.pad(grad_table_t[:8], ((0, 0), (0, 96))),
            jnp.pad(grad_table_t[8:], ((0, 4), (0, 96))),
        ],
        1,
    )
    small_grads = lax.psum(small_grads, ("dp", "expert"))
    mine = lax.dynamic_slice(small_grads, (0, dp * own), (8, own))
    table_col = jnp.concatenate(
        [
            lax.dynamic_slice(small_grads, (0, 768 + dp), (8, 1)),
            lax.dynamic_slice(small_grads, (0, 896 + dp), (4, 1)),
        ],
        0,
    )
    return (
        mixed,
        d_tokens,
        mine[0],
        dense[:, :2304],
        dense[:, 2304:],
        table_col.T,
        mine[1],
        mine[2:6].T,
        out_in.astype(f32)[:, None],
        out_outw.astype(f32)[:, None],
    )


def solution(mesh):
    both = ("dp", "expert")
    in_specs = (
        P(both, None), P("dp"), P("dp", None), P("dp", None), P("dp", None), P("dp"), P("dp", None),
        P("dp", "expert", None), P("dp", "expert", None), P(both, None), P(), P(both, None),
    )
    out_specs = (
        P(both, None), P(both, None), P("dp"), P("dp", None), P("dp", None), P("dp", None), P("dp"),
        P("dp", None), P("dp", "expert", None), P("dp", "expert", None),
    )
    return jax.shard_map(
        per_device, mesh=mesh, in_specs=in_specs, out_specs=out_specs, check_vma=False
    )
```

time: 623 us -> 454 us (0.73); the launches traced: 612 us -> 453 us
  blocking collectives: 228 us -> 77 us
  local copies, waits for them, and re-layouts: 167 us -> 26 us
  waiting for transfers between devices: 76.7 us -> 202 us
  Pallas kernels: 0 us -> 75.7 us
  starting transfers between devices: 30.6 us -> 7.65 us
  other arithmetic: 33.6 us -> 10.9 us
  matrix products: 58.7 us -> 39 us
    unnamed x2 -> x0, blocking collectives: 194 us -> none
    reduce_scatter x1 -> x3, waiting for transfers between devices: 11.9 us -> 115 us  [the longest x1 86.5 us: per_device(): lax.psum_scatter(grad_w_out, 'dp', scatter_dimension=0, tiled=True)]
    pallas_call x0 -> x3, Pallas kernels: none -> 75.7 us  [the longest x1 64.2 us: gather_all(): pl.pallas_call(gather_kernel, in_specs=[vm] * 5, out_specs=[vm] * 5, out_...]
    psum x1, blocking collectives: 17.3 us -> 65.1 us  [per_device(): small_grads = lax.psum(small_grads, ('dp', 'expert'))]
    reshape x17 -> x1, local copies, waits for them, and re-layouts: 45.7 us -> 0.02 us  [per_device(): d_window = d_window[:, :2].reshape(heads, window_width)]
    concatenate x2, local copies, waits for them, and re-layouts: 25 us -> 0.09 us  [the longest x1 0.08 us: per_device(): jnp.concatenate([pack, last, jnp.zeros((7, 128), bf16)], 0).astype(f32)]
    all_gather x3 -> x1, waiting for transfers between devices: 0.04 us -> 23.8 us  [per_device(): kv = lax.all_gather(projected[:, 768:], 'expert', axis=0, tiled=True)]
    all_to_all x8 -> x2, starting transfers between devices: 30 us -> 7.05 us  [the longest x1 3.57 us: per_device(): lax.all_to_all(d_kv, 'expert', split_axis=0, concat_axis=0, tiled=True)]
  transfers between devices with their start and end apart: 15 -> 7, of which waited for: 9 -> 6; matrix products, arithmetic and copies ran while one was open for 30% -> 9% of each run, Pallas kernels for 0% -> 1%
where the time goes in v1:
time: 454 us; the launch traced here: 453 us
  waiting for transfers between devices  202 us (44%)
  blocking collectives  77 us (17%)
  Pallas kernels  75.7 us (17%)
  matrix products  39 us (9%)
  local copies, waits for them, and re-layouts  26 us (6%)
  between operations  14.4 us (3%)
  other arithmetic  10.9 us (2%)
  starting transfers between devices  7.65 us (2%)
    reduce_scatter x1, waiting for transfers between devices, per_device(): lax.psum_scatter(grad_w_out, 'dp', scatter_dimension=0, tiled=True)  86.5 us
    psum x1, blocking collectives, per_device(): small_grads = lax.psum(small_grads, ('dp', 'expert'))  65.1 us
    pallas_call x1, Pallas kernels, gather_all(): pl.pallas_call(gather_kernel, in_specs=[vm] * 5, out_specs=[vm] * 5, out_...  64.2 us
    psum x1, waiting for transfers between devices, per_device(): dense = lax.psum(dense.astype(bf16), 'expert').astype(f32)  40.8 us
    reduce_scatter x1, waiting for transfers between devices, per_device(): lax.psum_scatter(jnp.concatenate([grad_qkv, grad_attn_out], 1), 'dp', sca...  28.3 us
    all_gather x1, waiting for transfers between devices, per_device(): kv = lax.all_gather(projected[:, 768:], 'expert', axis=0, tiled=True)  23.8 us
    all_to_all x1, waiting for transfers between devices, per_device(): lax.all_to_all(d_kv, 'expert', split_axis=0, concat_axis=0, tiled=True)  17.6 us
    dot_general x5, matrix products, mm_tn(): return lax.dot_general(a, b, TN, preferred_element_type=f32)  14.4 us
  transfers between devices with their start and end apart: 7, of which 6 were waited for; matrix products, arithmetic and copies ran while one was open for 9% of the time, Pallas kernels for 1%

profile of v1, /device:TPU:0, one launch (start us, length us, event | category | flops | bytes accessed | tf_op | source)
XLA Modules:
  0.0 453.2 jit_solution(2361963459273971048)
XLA Ops:
  13.8 64.2 %shard_map.195 = (bf16[2,4,4,48,1152]{4,3,2,1,0:T(8,128)(2,1)S(1)}, bf16[2,4,4,48,384]{4,3,2,1,0:T(8,128)(2,1)S(1)}, bf16[2,4,4,48,1536]{4,3,2,1,0:T(8,128)(2,1)...) custom-call(bf16[24,2304]{1,0:T(8,128)(2,1)S(1)} %copy-done.4, bf16[24,768]{1,0:T(8,128)(2,1)S(1)} %copy-done.5, ...), custom_call_target="tpu_custom_call" | custom-call | tf_op jit(solution)/shard_map/pallas_call | solution.py:361
  82.7 23.8 %all-gather.2.cloned.1.call-done = bf16[512,1536]{1,0:T(8,128)(2,1)} async-done(((bf16[128,1536]{1,0:T(8,128)(2,1)}), bf16[512,1536]{1,0:T(8,128)(2,1)}) %all-gather.2.cloned.1.call-update) | async-done | bytes 1572880 | tf_op jit(solution)/shard_map/all_gather | solution.py:417
  106.6 1.5 fusion.75
  108.1 4.7 %shard_map.196 = (bf16[128,768]{1,0:T(8,128)(2,1)S(1)}, f32[12,128,512]{2,1,0:T(8,128)S(1)}) custom-call(bf16[128,768]{1,0:T(8,128)(2,1)S(1)} %slice.113.query, bf16[512,768]{1,0:T(8,128)(2,1)S(1)} %get-tuple-element.73.key, bf16[512,768]{1,0:T(8,128)(2,1)S(1)} %get-tuple-element.72.value, f32[16,640]{1,0:T(8,128)S(1)} %concatenate.57.window), custom_call_target="tpu_custom_call" | custom-call | tf_op jit(solution)/shard_map/pallas_call | solution.py:427
  114.5 1.3 convolution_convert_fusion.4
  115.8 3.5 all-to-all-start
  119.5 4.9 %fusion.73 = (bf16[1,4,4,48,1536]{4,3,2,1,0:T(8,128)(2,1)}, bf16[1,4,4,48,1536]{4,3,2,1,0:T(8,128)(2,1)}) fusion(bf16[2,4,4,48,1536]{4,3,2,1,0:T(8,128)(2,1)} %get-tuple-element.25), kind=kLoop, calls=%fused_computation.133 | loop fusion | bytes 9437184 | tf_op jit(solution)/shard_map/slice | solution.py:407
  124.4 5.3 %all-to-all-done = bf16[4,48,1536]{2,1,0:T(8,128)(2,1)S(1)} async-done(((bf16[4,48,1536]{2,1,0:T(8,128)(2,1)}), bf16[4,48,1536]{2,1,0:T(8,128)(2,1)S(1)}, u32[]{:S(2)}, u32[]{:S(2)}) %all-to-all-start) | async-done | bytes 589856 | tf_op jit(solution)/shard_map/all_to_all | solution.py:462
  129.7 3.7 fusion.1
  133.4 5.6 %fusion.8 = bf16[192,3072]{1,0:T(8,128)(2,1)S(1)} fusion(f32[192,3072]{1,0:T(8,128)S(1)} %fusion.1, bf16[3072,768]{1,0:T(8,128)(2,1)} %bitcast.77, bf16[192,1536]{1,0:T(8,128)(2,1)S(1)} %bitcast.63), kind=kOutput, calls=%fused_computation.18 | convolution fusion | flops 917766144 | bytes 8552448 | tf_op jit(solution)/shard_map/dot_general | solution.py:21
  139.1 1.1 copy-done.19
  140.2 3.6 convolution_convert_fusion.2
  143.8 4.6 %fusion.10 = bf16[192,768]{1,0:T(8,128)(2,1)S(1)} fusion(bf16[192,3072]{1,0:T(8,128)(2,1)} %copy-done.19, bf16[768,1536]{1,0:T(8,128)(2,1)} %bitcast.57, bf16[768,1536]{1,0:T(8,128)(2,1)} %bitcast.55), kind=kOutput, calls=%fused_computation.23 | convolution fusion | flops 915554304 | bytes 6193152 | tf_op jit(solution)/shard_map/dot_general | solution.py:21
  148.3 3.8 convolution_convert_fusion.6
  152.2 12.0 %all_to_all.29 = bf16[4,48,1536]{2,1,0:T(8,128)(2,1)S(1)} all-to-all(bf16[4,48,1536]{2,1,0:T(8,128)(2,1)S(1)} %bitcast.53), channel_id=1, replica_groups=mesh['dp'=32,'expert'=4] {'expert'}, dimensions={0} | all-to-all | bytes 1179648 | tf_op jit(solution)/shard_map/all_to_all | solution.py:475
  167.5 6.8 %shard_map.197 = (bf16[128,768]{1,0:T(8,128)(2,1)S(1)}, bf16[512,768]{1,0:T(8,128)(2,1)S(1)}, bf16[512,768]{1,0:T(8,128)(2,1)S(1)}, f32[6,8,640]{2,1,0:T(8,128)S(1)}) custom-call(bf16[128,768]{1,0:T(8,128)(2,1)S(1)} %slice.113.query, bf16[512,768]{1,0:T(8,128)(2,1)S(1)} %get-tuple-element.73.key, bf16[512,768]{1,0:T(8,128)(2,1)S(1)} %get-tuple-element.72.value, ...), custom_call_target="tpu_custom_call" | custom-call | tf_op jit(solution)/shard_map/pallas_call | solution.py:491
  174.3 1.3 pad_maximum_fusion.7
  175.5 3.6 all-to-all-start.2
  179.2 1.5 convolution_convert_fusion.5
  180.7 17.6 %all-to-all-done.2 = bf16[4,128,1536]{2,1,0:T(8,128)(2,1)S(1)} async-done(((bf16[4,128,1536]{2,1,0:T(8,128)(2,1)}), bf16[4,128,1536]{2,1,0:T(8,128)(2,1)S(1)}, u32[]{:S(2)}, u32[]{:S(2)}) %all-to-all-start.2) | async-done | bytes 1572896 | tf_op jit(solution)/shard_map/all_to_all | solution.py:518
  198.3 1.1 reduce_sum.112
  199.4 2.2 convolution_convert_fusion
  201.6 2.8 pad_maximum_fusion.1
  205.4 5.9 %convolution_convert_fusion.1 = bf16[3072,768]{1,0:T(8,128)(2,1)} fusion(bf16[192,1536]{1,0:T(8,128)(2,1)S(1)} %bitcast.65, f32[192,3072]{1,0:T(8,128)} %copy-done.26), kind=kOutput, calls=%fused_computation.1 | convolution fusion | flops 913637376 | bytes 7372800 | tf_op jit(solution)/shard_map/dot_general | solution.py:25
  212.5 3.5 fusion.22
  216.1 65.1 %psum.14 = f32[8,1024]{1,0:T(8,128)S(1)} all-reduce(f32[8,1024]{1,0:T(8,128)S(1)} %select_maximum_fusion), channel_id=1, replica_groups=mesh['dp'=32,'expert'=4] {'dp','expert'}, use_global_device_ids=true, to_apply=%region_13.14 | all-reduce | flops 8192 | bytes 65536 | tf_op jit(solution)/shard_map/psum | solution.py:540
  285.0 1.0 copy.46
  286.0 28.3 %reduce-scatter.4.cloned.1.call-done = bf16[24,3072]{1,0:T(8,128)(2,1)} async-done(((bf16[768,3072]{1,0:T(8,128)(2,1)}), bf16[24,3072]{1,0:T(8,128)(2,1)}) %reduce-scatter.4.cloned.1.call-update) | async-done | bytes 147472 | tf_op jit(solution)/shard_map/reduce_scatter | solution.py:526
  314.4 86.5 %reduce-scatter.8.cloned.1.call-done = bf16[96,768]{1,0:T(8,128)(2,1)} async-done(((bf16[3072,768]{1,0:T(8,128)(2,1)}), bf16[96,768]{1,0:T(8,128)(2,1)}) %reduce-scatter.8.cloned.1.call-update) | async-done | bytes 147472 | tf_op jit(solution)/shard_map/reduce_scatter | solution.py:473
  402.9 40.8 %all-reduce.5.cloned.1.call-done = bf16[24,3072]{1,0:T(8,128)(2,1)} async-done(((bf16[24,3072]{1,0:T(8,128)(2,1)}), bf16[24,3072]{1,0:T(8,128)(2,1)}) %all-reduce.5.cloned.1.call-update) | async-done | bytes 147472 | tf_op jit(solution)/shard_map/psum | solution.py:529
  443.7 1.6 slice.127
  445.2 1.4 slice.128
  (134 shorter events, 24.4 us)
Async XLA Ops:
  7.2 99.4 %all-gather.2.cloned.1.call-start = ((), (), s32[]{:S(2)}) async-start(), calls=%async_computation.6 | async-start | bytes 1966080 | tf_op jit(solution)/shard_map/all_gather | solution.py:417
  10.3 0.9 copy-start.2
  11.2 0.9 copy-start.3
  78.1 0.9 copy-start.10
  78.4 1.5 copy-start.13
  78.4 1.8 copy-start.14
  79.1 1.9 copy-start.24
  79.1 2.2 copy-start.25
  82.7 30.1 %copy-start.20 = (bf16[1,4,4,48,384]{4,3,2,1,0:T(8,128)(2,1)}, bf16[1,4,4,48,384]{4,3,2,1,0:T(8,128)(2,1)S(1)}, u32[]{:S(2)}) copy-start(bf16[1,4,4,48,384]{4,3,2,1,0:T(8,128)(2,1)S(1)} %get-tuple-element.74) | copy-start | bytes 1769476
  106.6 6.3 %copy-start.22 = (bf16[1,4,4,48,384]{4,3,2,1,0:T(8,128)(2,1)S(1)}, bf16[1,4,4,48,384]{4,3,2,1,0:T(8,128)(2,1)}, u32[]{:S(2)}) copy-start(bf16[1,4,4,48,384]{4,3,2,1,0:T(8,128)(2,1)} %get-tuple-element.75) | copy-start | bytes 1769476
  108.1 5.7 %copy-start.15 = (bf16[128,768]{1,0:T(8,128)(2,1)S(1)}, bf16[128,768]{1,0:T(8,128)(2,1)}, u32[]{:S(2)}) copy-start(bf16[128,768]{1,0:T(8,128)(2,1)} %param.23) | copy-start | bytes 589828
  112.8 2.9 copy-start
  113.4 1.1 copy-start.8
  115.8 13.9 %all-to-all-start = ((bf16[4,48,1536]{2,1,0:T(8,128)(2,1)}), bf16[4,48,1536]{2,1,0:T(8,128)(2,1)S(1)}, u32[]{:S(2)}, u32[]{:S(2)}) async-start(bf16[4,48,1536]{2,1,0:T(8,128)(2,1)} %bitcast.12), calls=%async_computation | async-start | bytes 1179648 | tf_op jit(solution)/shard_map/all_to_all | solution.py:462
  119.3 164.8 %reduce-scatter.6.cloned.1.call-start = ((), (), s32[]{:S(2)}) async-start(), calls=%async_computation.9 | async-start | bytes 4866048 | tf_op jit(solution)/shard_map/reduce_scatter | solution.py:472
  129.7 9.3 %copy-start.16 = (bf16[4,48,1536]{2,1,0:T(8,128)(2,1)}, bf16[4,48,1536]{2,1,0:T(8,128)(2,1)S(1)}, u32[]{:S(2)}) copy-start(bf16[4,48,1536]{2,1,0:T(8,128)(2,1)S(1)} %all-to-all-done) | copy-start | bytes 1769476
  133.4 5.7 %copy-start.26 = (f32[192,3072]{1,0:T(8,128)}, f32[192,3072]{1,0:T(8,128)S(1)}, u32[]{:S(2)}) copy-start(f32[192,3072]{1,0:T(8,128)S(1)} %fusion.1) | copy-start | bytes 7077892
  139.0 1.1 copy-start.19
  143.8 4.6 %copy-start.27 = (f32[192,3072]{1,0:T(8,128)S(1)}, f32[192,3072]{1,0:T(8,128)}, u32[]{:S(2)}) copy-start(f32[192,3072]{1,0:T(8,128)} %copy-done.26) | copy-start | bytes 7077892
  164.2 2.0 copy-start.21
  164.2 2.0 copy-start.23
  165.3 2.2 copy-start.1
  175.5 22.7 %all-to-all-start.2 = ((bf16[4,128,1536]{2,1,0:T(8,128)(2,1)}), bf16[4,128,1536]{2,1,0:T(8,128)(2,1)S(1)}, u32[]{:S(2)}, u32[]{:S(2)}) async-start(bf16[4,128,1536]{2,1,0:T(8,128)(2,1)} %bitcast.51), calls=%async_computation.2 | async-start | bytes 3145728 | tf_op jit(solution)/shard_map/all_to_all | solution.py:518
  179.1 20.3 %copy-start.11 = (bf16[128,768]{1,0:T(8,128)(2,1)S(1)}, bf16[128,768]{1,0:T(8,128)(2,1)}, u32[]{:S(2)}) copy-start(bf16[128,768]{1,0:T(8,128)(2,1)} %param.12) | copy-start | bytes 589828
  179.1 135.2 %reduce-scatter.4.cloned.1.call-start = ((), (), s32[]{:S(2)}) async-start(), calls=%async_computation.7 | async-start | bytes 4866048 | tf_op jit(solution)/shard_map/reduce_scatter | solution.py:526
  204.3 1.1 copy-start.17
  204.4 196.6 %reduce-scatter.8.cloned.1.call-start = ((), (), s32[]{:S(2)}) async-start(), calls=%async_computation.10 | async-start | bytes 4866048 | tf_op jit(solution)/shard_map/reduce_scatter | solution.py:473
  211.3 0.9 copy-start.9
  211.3 1.1 copy-start.12
  211.3 1.2 copy-start.18
  211.3 232.3 %all-reduce.5.cloned.1.call-start = ((), (), s32[]{:S(2)}) async-start(), calls=%async_computation.8 | async-start | bytes 294912 | tf_op jit(solution)/shard_map/psum | solution.py:529
  212.5 70.8 %copy-start.7 = (f32[128,768]{1,0:T(8,128)S(1)}, f32[128,768]{1,0:T(8,128)}, u32[]{:S(2)}) copy-start(f32[128,768]{1,0:T(8,128)} %copy-done.6) | copy-start | bytes 1179652
  (3 other events, 2.4 us)
Sparse Core Ops, SparseCore 0:
  81.1 25.4 all-gather.1
  143.9 83.2 reduce-scatter.5
  231.4 82.9 reduce-scatter.3
  318.0 82.9 reduce-scatter.7
  403.2 40.3 all-reduce.4

commit v2 on v1

--- a/solution.py
+++ b/solution.py
@@ -385,6 +385,418 @@
     )(w_qkv, w_ao, w_in, w_out, pack)
 
 
+class Scatter:
+    def __init__(self, place, ref, tall, pair, far, near, side, send, recv):
+        self.o, self.ref, self.tall = place, ref, tall
+        self.pair, self.far, self.near, self.side = pair, far, near, side
+        self.send, self.recv = send, recv
+
+    def where(self, p, q):
+        o = self.o
+        return q * (1 - o.c) + p * o.c, p * (1 - o.c) + q * o.c
+
+    def q_at(self, by):
+        return lax.rem(self.o.q + by, 4)
+
+    def own(self, p, q):
+        y, z = self.where(p, q)
+        return (y, z, self.o.c) if self.tall else (self.o.c, y, z)
+
+    def to_pair(self, s, low, count):
+        rows = pl.ds(low, count)
+        theirs = 1 - self.o.c
+        src = self.ref.at[rows, :, theirs] if self.tall else self.ref.at[theirs, rows]
+        remote(src, self.pair.at[rows], self.send.at[s], self.recv.at[s], self.o.sibling()).start()
+
+    def from_pair(self, s, count):
+        view = self.pair.at[pl.ds(0, count)]
+        remote(view, view, self.send.at[s], self.recv.at[s], self.o.sibling()).wait_recv()
+
+    def add_pair(self, by):
+        q = self.q_at(by)
+
+        def body(p, carry):
+            y, z = self.where(p, q)
+            at = self.own(p, q)
+            self.ref[at] = (self.ref[at].astype(f32) + self.pair[y, z].astype(f32)).astype(bf16)
+            return carry
+
+        lax.fori_loop(0, 4, body, 0)
+
+    def go(self, s, by, low, dst, to):
+        def body(k):
+            src = slab_of(self.ref, self.tall, k, self.q_at(by), low, 2)
+            remote(src, dst, self.send.at[s], self.recv.at[s], to).start()
+
+        self.o.each_core(body)
+
+    def ring(self):
+        o = self.o
+        self.add_pair(2)
+        self.go(2, 2, 0, self.far.at[0], o.along_q(1))
+        self.go(3, 2, 2, self.far.at[1], o.along_q(3))
+        self.add_pair(1)
+        self.go(4, 1, 2, self.near.at[0, pl.ds(2, 2)], o.along_q(1))
+        self.add_pair(3)
+        self.go(5, 3, 0, self.near.at[1, pl.ds(0, 2)], o.along_q(3))
+        self.add_pair(0)
+
+    def landed(self, s, view):
+        remote(view, view, self.send.at[s], self.recv.at[s], self.o.sibling()).wait_recv()
+
+    def add_far(self, i, by, low):
+        q = self.q_at(by)
+
+        def body(j, carry):
+            at = self.own(low + j, q)
+            self.ref[at] = (self.ref[at].astype(f32) + self.far[i, j].astype(f32)).astype(bf16)
+            return carry
+
+        lax.fori_loop(0, 2, body, 0)
+
+    def ring_far(self):
+        o = self.o
+        self.landed(2, self.far.at[0])
+        self.add_far(0, 1, 0)
+        self.go(6, 1, 0, self.near.at[0, pl.ds(0, 2)], o.along_q(1))
+        self.landed(3, self.far.at[1])
+        self.add_far(1, 3, 2)
+        self.go(7, 3, 2, self.near.at[1, pl.ds(2, 2)], o.along_q(3))
+
+    def across(self):
+        o = self.o
+        half = self.near.at[0, pl.ds(0, 2)]
+        for s in (4, 5, 6, 7):
+            self.landed(s, half)
+
+        def body(p, carry):
+            at = self.own(p, o.q)
+            total = self.ref[at].astype(f32) + self.near[0, p].astype(f32)
+            self.ref[at] = (total + self.near[1, p].astype(f32)).astype(bf16)
+            return carry
+
+        lax.fori_loop(0, 4, body, 0)
+        for i in (1, 2, 3):
+            src = self.ref.at[self.own(lax.rem(o.p + i, 4), o.q)]
+            remote(
+                src, self.side.at[i - 1], self.send.at[7 + i], self.recv.at[7 + i], o.along_p(i)
+            ).start()
+
+    def total(self):
+        o = self.o
+        for i in (0, 1, 2):
+            self.landed(8 + i, self.side.at[i])
+        total = self.ref[self.own(o.p, o.q)].astype(f32)
+        for i in (0, 1, 2):
+            total = total + self.side[i].astype(f32)
+        return total
+
+    def sent(self, s, view):
+        remote(view, view, self.send.at[s], self.recv.at[s], self.o.sibling()).wait_send()
+
+    def drain(self, pair_parts):
+        for s, count in pair_parts:
+            self.sent(s, self.pair.at[pl.ds(0, count)])
+        for s in range(2, 8):
+            self.sent(s, self.far.at[0])
+        for s in range(8, 11):
+            self.sent(s, self.side.at[0])
+
+
+SQ = 0.7978845608028654
+
+
+def gelu_both(h):
+    t = jnp.tanh(SQ * (h + 0.044715 * (h * h * h)))
+    value = 0.5 * h * (1.0 + t)
+    slope = 0.5 * (1.0 + t) + 0.5 * h * (1.0 - t * t) * (SQ * (1.0 + 3 * 0.044715 * (h * h)))
+    return value, slope
+
+
+def expert_chunk(j, sent, sent_t, d_result, g_in, g_out, h_in, h_out, result, d_incoming):
+    half, at = lax.div(j, 4), pl.ds(pl.multiple_of(lax.rem(j, 4) * 384, 128), 384)
+    y, z = lax.div(j, 2), pl.ds(lax.rem(j, 2) * 2, 2)
+    first = g_in[half, :, :, :, at].reshape(768, 384)
+    second = g_out[y, z].reshape(384, 768)
+    hidden = mm(sent[...], first)
+    value, slope = gelu_both(hidden)
+    act = value.astype(bf16)
+    result[...] += mm(act, second)
+    d_act = mm_nt(d_result[...], second)
+    d_hidden = (d_act * slope).astype(bf16)
+    h_out[y, z] = mm_tn(act, d_result[...]).astype(bf16).reshape(2, 2, 96, 768)
+    h_in[half, :, :, :, at] = mm(sent_t[...], d_hidden).astype(bf16).reshape(4, 4, 48, 384)
+    d_incoming[...] += mm_nt(d_hidden, first)
+
+
+def pair_backward(o, i, query, key, value, weights, d_heads, d_query, d_kv, d_kr, d_window, send, recv):
+    lanes = pl.ds(pl.multiple_of(i * 128, 128), 128)
+    probability = weights[pl.ds(2 * i, 2)].reshape(256, 512)
+    d_stack = stack_heads(d_heads[:, lanes])
+    d_weights = mm_nt(d_stack, value[:, lanes])
+    d_kv[:, 1, :, lanes] = (
+        mm_tn(probability.astype(bf16), d_stack).astype(bf16).reshape(4, 128, 128)
+    )
+    d_scores = probability * (d_weights - jnp.sum(probability * d_weights, -1, keepdims=True))
+    low = d_scores.astype(bf16)
+    d_kv[:, 0, :, lanes] = (
+        mm_tn(low, stack_heads(query[:, lanes])).astype(bf16).reshape(4, 128, 128)
+    )
+    for by in (1, 2, 3):
+        there = lax.rem(o.x + by, 4)
+        remote(
+            d_kv.at[there, :, :, lanes], d_kr.at[by - 1, :, :, lanes],
+            send.at[i, by - 1], recv.at[i, by - 1], o.along_x(by),
+        ).start()
+    d_query[:, lanes] = join_pair(mm(low, key[:, lanes])).astype(bf16)
+    for j in (0, 1):
+        d_window[pl.ds(2 * i + j, 1), :] = diagonal_sums(d_scores[j * 128 : (j + 1) * 128], 640)
+
+
+def back_kernel(
+    g_qkv, g_ao, g_in, g_out, sent, d_result, placing, after_attn, probs, chosen, cotangent,
+    moe_input, heads_out, tokens, query, kv, weights, small_in, buckets,
+    mixed, d_tokens, out_qkv, out_ao, out_in, out_out, small,
+    h_qkv, h_ao, h_in, h_out, sent_t, result, d_incoming, ret, back, d_query, d_kv, d_kr, d_window,
+    d_heads_ref, d_after_ref, total_q, total_a, total_i, xs, xr, xa,
+    pair_q, pair_a, pair_i, pair_o, far_q, far_a, far_i, far_o, near_q, near_a, near_i, near_o,
+    side_q, side_a, side_i, side_o,
+    sends, recvs, ret_send, ret_recv, dk_send, dk_recv, x_send, x_recv, last_send, last_recv,
+    arrivals, small_send, small_recv,
+):
+    o = Place()
+    o.barrier(True)
+    fq = Scatter(o, h_qkv, 0, pair_q, far_q, near_q, side_q, sends.at[0], recvs.at[0])
+    fa = Scatter(o, h_ao, 0, pair_a, far_a, near_a, side_a, sends.at[1], recvs.at[1])
+    fi = Scatter(o, h_in, 0, pair_i, far_i, near_i, side_i, sends.at[2], recvs.at[2])
+    fo = Scatter(o, h_out, 1, pair_o, far_o, near_o, side_o, sends.at[3], recvs.at[3])
+    tot = SmallSum(o, small, arrivals, small_send, small_recv, True)
+
+    sent_t[...] = sent[...].astype(f32).T.astype(bf16)
+    result[...] = jnp.zeros_like(result)
+    d_incoming[...] = jnp.zeros_like(d_incoming)
+
+    def chunk(j, carry):
+        expert_chunk(j, sent, sent_t, d_result, g_in, g_out, h_in, h_out, result, d_incoming)
+        return carry
+
+    start = 4 * (1 - o.c)
+    lax.fori_loop(start, start + 4, chunk, 0)
+    fi.to_pair(0, 0, 4)
+    fo.to_pair(0, 2 * (1 - o.c), 2)
+    lax.fori_loop(4 - start, 8 - start, chunk, 0)
+    fo.to_pair(1, 2 * o.c, 2)
+    ret[:, 0] = result[...].astype(bf16).reshape(4, 48, 768)
+    ret[:, 1] = d_incoming[...].astype(bf16).reshape(4, 48, 768)
+    ret_copies = [
+        remote(
+            ret.at[lax.rem(o.x + by, 4)], back.at[o.x], ret_send.at[by - 1], ret_recv.at[by - 1],
+            o.along_x(by),
+        )
+        for by in (1, 2, 3)
+    ]
+    for copy in ret_copies:
+        copy.start()
+    back[o.x] = ret[o.x]
+    fi.from_pair(0, 4)
+    fi.ring()
+    for copy in ret_copies:
+        copy.wait_recv()
+
+    small8 = small_in[:, :768]
+    gain_one, gain_two = small8[0:1], small8[1:2]
+    returned = mm(placing[...], back[:, 0].reshape(192, 768))
+    d_moe = mm(placing[...], back[:, 1].reshape(192, 768))
+    attn = after_attn[...]
+    upstream = cotangent[...].astype(f32)
+    gate = jnp.sum(probs[...] * chosen[...], -1, keepdims=True)
+    mixed[...] = (attn + gate * returned).astype(bf16)
+    d_gate = jnp.sum(upstream * returned, -1, keepdims=True)
+    d_logits = probs[...] * (d_gate * chosen[...] - d_gate * gate)
+    d_moe = d_moe + jnp.dot(d_logits, small8, precision=highest, preferred_element_type=f32)
+    grad_router = lax.dot_general(
+        d_logits, moe_input[...].astype(f32), TN, precision=highest, preferred_element_type=f32
+    )
+    r_two = lax.rsqrt(jnp.mean(attn * attn, -1, keepdims=True) + epsilon)
+    d_after, grad_norm_two = rms_backward(attn, r_two, gain_two, d_moe)
+    d_after = d_after + upstream
+    d_after_ref[...] = d_after
+    d_attn = d_after.astype(bf16)
+    d_heads = jnp.zeros((128, 768), f32)
+    for h in (0, 1):
+        part = d_attn[:, h * 384 : (h + 1) * 384]
+        h_ao[h] = mm_tn(heads_out[...], part).astype(bf16).reshape(4, 4, 48, 384)
+        d_heads = d_heads + mm_nt(part, g_ao[h].reshape(768, 384))
+    fa.to_pair(0, 0, 4)
+    d_heads_ref[...] = d_heads.astype(bf16)
+    fo.from_pair(0, 2)
+    fo.from_pair(1, 2)
+    fo.ring()
+
+    d_window[...] = jnp.zeros_like(d_window)
+    key, value = kv.at[:, pl.ds(0, 768)], kv.at[:, pl.ds(768, 768)]
+
+    def pair(i, carry):
+        pair_backward(
+            o, i, query, key, value, weights, d_heads_ref, d_query, d_kv, d_kr, d_window, dk_send, dk_recv
+        )
+        return carry
+
+    lax.fori_loop(0, 2, pair, 0)
+    fi.ring_far()
+    fa.from_pair(0, 4)
+    fa.ring()
+    lax.fori_loop(2, 4, pair, 0)
+    fo.ring_far()
+    fi.across()
+    lax.fori_loop(4, 6, pair, 0)
+    fa.ring_far()
+
+    x = tokens[...].astype(f32)
+    r_one, normed = rms_forward(x, gain_one)
+    normed_t = normed.T.astype(bf16)
+
+    def project(h, d_part):
+        h_qkv[h] = mm(normed_t, d_part).astype(bf16).reshape(4, 4, 48, 1152)
+        return mm_nt(d_part, g_qkv[h].reshape(768, 1152))
+
+    bucket_row = buckets[:, pl.ds(pl.multiple_of((3 - o.x) * 128, 128), 640)]
+    picks = jnp.where(
+        jnp.broadcast_to(bucket_row, (128, 640)) == lax.broadcasted_iota(jnp.int32, (128, 640), 0), 1.0, 0.0
+    )
+    grad_table = lax.dot_general(
+        d_window[...], picks, NT, precision=highest, preferred_element_type=f32
+    )
+    fo.across()
+    for i in range(6):
+        for by in (1, 2, 3):
+            view = d_kr.at[by - 1, :, :, pl.ds(0, 128)]
+            remote(view, view, dk_send.at[i, by - 1], dk_recv.at[i, by - 1], o.sibling()).wait_recv()
+    d_own = d_kv[o.x].astype(f32)
+    for by in (0, 1, 2):
+        d_own = d_own + d_kr[by].astype(f32)
+    d_own = d_own.astype(bf16)
+    d_key, d_value = d_own[0], d_own[1]
+    d_normed = project(0, jnp.concatenate([d_query[...], d_key[:, :384]], 1))
+    d_normed = d_normed + project(1, jnp.concatenate([d_key[:, 384:], d_value], 1))
+    fq.to_pair(0, 0, 4)
+    d_resid, grad_norm_one = rms_backward(x, r_one, gain_one, d_normed)
+    d_tokens[...] = (d_after_ref[...] + d_resid).astype(bf16)
+    row = lax.broadcasted_iota(jnp.int32, (8, 768), 0)
+    top = jnp.where(row == 0, grad_norm_one[None, :], jnp.where(row == 1, grad_norm_two[None, :], grad_router))
+    small[0] = jnp.concatenate([top, grad_table[0:8], grad_table[8:16]], 1)
+    tot.start(0)
+    fa.across()
+    fq.from_pair(0, 4)
+    fq.ring()
+    tot.add(0)
+    tot.start(1)
+    out_out[...] = fo.total()
+
+    def hand(k, total, out, value):
+        n = value.shape[1]
+        total[...] = value
+        mine = pl.ds(pl.multiple_of(o.c * n, 128), n)
+        out[:, mine] = total[pl.ds(pl.multiple_of(24 * o.c, 8), 24), :]
+        copy = remote(
+            total.at[pl.ds(pl.multiple_of(24 * (1 - o.c), 8), 24)], out.at[:, mine],
+            last_send.at[k], last_recv.at[k], o.sibling(),
+        )
+        copy.start()
+        return copy
+
+    last = [hand(0, total_i, out_in, fi.total())]
+    total_a[...] = fa.total()
+    tot.add(1)
+    tot.start(2)
+    fq.ring_far()
+    fq.across()
+    tot.add(2)
+    tot.start(3)
+    dense = jnp.concatenate([fq.total(), total_a[...]], 1).astype(bf16)
+    for j in range(4):
+        xs[j] = dense[:, j * 384 : (j + 1) * 384]
+    first = [
+        remote(xs.at[lax.rem(o.x + by, 4)], xr.at[by - 1], x_send.at[by - 1], x_recv.at[by - 1], o.along_x(by))
+        for by in (1, 2, 3)
+    ]
+    for copy in first:
+        copy.start()
+    for copy in first:
+        copy.wait_recv()
+    own = xs[o.x].astype(f32)
+    for j in range(3):
+        own = own + xr[j].astype(f32)
+    xa[o.x] = own.astype(bf16)
+    second = [
+        remote(xa.at[o.x], xa.at[o.x], x_send.at[by + 2], x_recv.at[by + 2], o.along_x(by)) for by in (1, 2, 3)
+    ]
+    for copy in second:
+        copy.start()
+    for copy in second:
+        copy.wait_recv()
+    whole = jnp.concatenate([xa[0], xa[1], xa[2], xa[3]], 1).astype(f32)
+    last.append(hand(1, total_q, out_qkv, whole[:, :1152]))
+    last.append(hand(2, total_a, out_ao, whole[:, 1152:]))
+    tot.add(3)
+    for copy in last:
+        copy.wait_recv()
+    for copy in ret_copies + first + second + last:
+        copy.wait_send()
+    for i in range(6):
+        for by in (1, 2, 3):
+            view = d_kr.at[by - 1, :, :, pl.ds(0, 128)]
+            remote(view, view, dk_send.at[i, by - 1], dk_recv.at[i, by - 1], o.sibling()).wait_send()
+    tot.drain()
+    for f in (fq, fa, fi):
+        f.drain([(0, 4)])
+    fo.drain([(0, 2), (1, 2)])
+
+
+def backward_all(*operands):
+    vm = pl.BlockSpec(memory_space=pltpu.VMEM)
+    dma = pltpu.SemaphoreType.DMA
+
+    def low(*shape):
+        return pltpu.VMEM(shape, bf16)
+
+    def full(*shape):
+        return pltpu.VMEM(shape, f32)
+
+    sizes = ((48, 1152), (48, 384), (48, 1536), (96, 768))
+    return pl.pallas_call(
+        back_kernel,
+        in_specs=[vm] * len(operands),
+        out_specs=[vm] * 7,
+        out_shape=[
+            jax.ShapeDtypeStruct((128, 768), bf16),
+            jax.ShapeDtypeStruct((128, 768), bf16),
+            jax.ShapeDtypeStruct((24, 2304), f32),
+            jax.ShapeDtypeStruct((24, 768), f32),
+            jax.ShapeDtypeStruct((24, 3072), f32),
+            jax.ShapeDtypeStruct((96, 768), f32),
+            jax.ShapeDtypeStruct((5, 8, 1024), f32),
+        ],
+        scratch_shapes=[
+            low(2, 4, 4, 48, 1152), low(2, 4, 4, 48, 384), low(2, 4, 4, 48, 1536), low(4, 4, 2, 96, 768),
+            low(768, 192), full(192, 768), full(192, 768), low(4, 2, 48, 768), low(4, 2, 48, 768),
+            low(128, 768), low(4, 2, 128, 768), low(3, 2, 128, 768), full(16, 640),
+            low(128, 768), full(128, 768), full(48, 1152), full(48, 384), full(48, 1536),
+            low(4, 48, 384), low(3, 48, 384), low(4, 48, 384),
+            *[low(4, 4, *s) for s in sizes],
+            *[low(2, 2, *s) for s in sizes],
+            *[low(2, 4, *s) for s in sizes],
+            *[low(3, *s) for s in sizes],
+            dma((4, 11)), dma((4, 11)), dma((3,)), dma((3,)), dma((6, 3)), dma((6, 3)),
+            dma((6,)), dma((6,)), dma((3,)), dma((3,)),
+            full(10, 8, 1024), dma((10,)), dma((10,)),
+        ],
+        compiler_params=pltpu.CompilerParams(
+            collective_id=1, has_side_effects=True, vmem_limit_bytes=60 * 2**20
+        ),
+    )(*operands)
+
+
 def per_device(
     tokens, norm_attn, w_qkv, w_attn_out, bias_table, norm_moe, router, w_in, w_out, routes, buckets, cotangent
 ):
@@ -404,8 +816,6 @@
     small = small[3]
     full_qkv = jnp.concatenate([g_qkv[0].reshape(768, -1), g_qkv[1].reshape(768, -1)], 1)
     full_out = jnp.concatenate([g_ao[0].reshape(768, -1), g_ao[1].reshape(768, -1)], 1)
-    full_in = jnp.concatenate([g_in[0].reshape(768, -1), g_in[1].reshape(768, -1)], 1)
-    full_outw = g_out.reshape(3072, 768)
     gain_one, gain_two, router_t = small[0:1, :768], small[1:2, :768], small[2:6, :768]
     table_full = jnp.concatenate([small[:8, 768:800], small[:4, 896:928]], 0)
 
@@ -460,84 +870,13 @@
     d_combined = (gate * upstream).astype(bf16)
     outgoing = mm_tn(placing, jnp.concatenate([moe_input, d_combined], 1)).astype(bf16)
     incoming = lax.all_to_all(outgoing, "expert", split_axis=0, concat_axis=0, tiled=True)
-    sent, d_result = incoming[:, :768], incoming[:, 768:]
-    hidden = mm(sent, full_in)
-    activated, gelu_back = jax.vjp(jax.nn.gelu, hidden)
-    act_low = activated.astype(bf16)
-    result = mm(act_low, full_outw).astype(bf16)
-    d_act = mm_nt(d_result, full_outw)
-    d_hidden = gelu_back(d_act)[0].astype(bf16)
-    grad_w_out = mm_tn(act_low, d_result).astype(bf16)
-    grad_w_in = mm_tn(sent, d_hidden).astype(bf16)
-    out_in = lax.psum_scatter(grad_w_in, "dp", scatter_dimension=0, tiled=True)
-    out_outw = lax.psum_scatter(grad_w_out, "dp", scatter_dimension=0, tiled=True)
-    d_incoming = mm_nt(d_hidden, full_in).astype(bf16)
-    back = lax.all_to_all(
-        jnp.concatenate([result, d_incoming], 1), "expert", split_axis=0, concat_axis=0, tiled=True
-    )
-    returned = mm(placing, back)
-    combined, d_moe = returned[:, :768], returned[:, 768:]
-    mixed = (after_attn + gate * combined).astype(bf16)
-    d_gate = jnp.sum(upstream * combined, -1, keepdims=True)
-    d_logits = probs * (d_gate * chosen - d_gate * gate)
-    grad_router = jnp.dot(d_logits.T, moe_input.astype(f32), precision=highest)
-    d_moe = d_moe + jnp.dot(d_logits, router_t, precision=highest)
-    d_after, grad_norm_two = rms_backward(after_attn, r_two, gain_two, d_moe)
-    d_after = d_after + upstream
-    d_attn = d_after.astype(bf16)
-    grad_attn_out = mm_tn(heads_out, d_attn).astype(bf16)
-    d_heads = mm_nt(d_attn, full_out).astype(bf16)
-
-    d_query, d_key, d_value, d_window = pl.pallas_call(
-        attention_backward,
-        grid=(pairs,),
-        in_specs=[
-            pl.BlockSpec((rows, 128), lambda p: (0, p)),
-            pl.BlockSpec((keys, 128), lambda p: (0, p)),
-            pl.BlockSpec((keys, 128), lambda p: (0, p)),
-            pl.BlockSpec((2, rows, keys), lambda p: (p, 0, 0)),
-            pl.BlockSpec((rows, 128), lambda p: (0, p)),
-        ],
-        out_specs=[
-            pl.BlockSpec((rows, 128), lambda p: (0, p)),
-            pl.BlockSpec((keys, 128), lambda p: (0, p)),
-            pl.BlockSpec((keys, 128), lambda p: (0, p)),
-            pl.BlockSpec((1, 8, window_width), lambda p: (p, 0, 0)),
-        ],
-        out_shape=[
-            jax.ShapeDtypeStruct((rows, width), bf16),
-            jax.ShapeDtypeStruct((keys, width), bf16),
-            jax.ShapeDtypeStruct((keys, width), bf16),
-            jax.ShapeDtypeStruct((pairs, 8, window_width), f32),
-        ],
-        compiler_params=pltpu.CompilerParams(vmem_limit_bytes=32 * 2**20),
-    )(query, key, value, weights, d_heads)
-    d_window = d_window[:, :2].reshape(heads, window_width)
-    grad_table_t = lax.dot_general(d_window, picks, NT, precision=highest)
-    d_kv = jnp.concatenate([d_key, d_value], 1).reshape(groups, rows, 2 * width)
-    d_kv = lax.all_to_all(d_kv, "expert", split_axis=0, concat_axis=0, tiled=True)
-    d_kv = jnp.sum(d_kv.astype(f32), 0).astype(bf16)
-    d_projected = jnp.concatenate([d_query, d_kv], 1)
-    grad_qkv = mm_tn(normed, d_projected).astype(bf16)
-    d_normed = mm_nt(d_projected, full_qkv)
-    d_resid, grad_norm_one = rms_backward(x, r_one, gain_one, d_normed)
-    d_tokens = (d_after + d_resid).astype(bf16)
-
-    dense = lax.psum_scatter(
-        jnp.concatenate([grad_qkv, grad_attn_out], 1), "dp", scatter_dimension=0, tiled=True
-    )
-    dense = lax.psum(dense.astype(bf16), "expert").astype(f32)
-    small_grads = jnp.concatenate(
-        [
-            jnp.concatenate(
-                [grad_norm_one[None], grad_norm_two[None], grad_router, jnp.zeros((2, 768), f32)], 0
-            ),
-            jnp.pad(grad_table_t[:8], ((0, 0), (0, 96))),
-            jnp.pad(grad_table_t[8:], ((0, 4), (0, 96))),
-        ],
-        1,
-    )
-    small_grads = lax.psum(small_grads, ("dp", "expert"))
+    probs8 = jnp.concatenate([jnp.zeros((rows, 2), f32), probs, jnp.zeros((rows, 2), f32)], 1)
+    chosen8 = jnp.concatenate([jnp.zeros((rows, 2), f32), chosen, jnp.zeros((rows, 2), f32)], 1)
+    mixed, d_tokens, out_qkv, out_ao, out_in, out_outw, small_grads = backward_all(
+        g_qkv, g_ao, g_in, g_out, incoming[:, :768], incoming[:, 768:], placing, after_attn, probs8, chosen8,
+        cotangent, moe_input, heads_out, tokens, query, kv, weights, small, padded[None, :],
+    )
+    small_grads = small_grads[4]
     mine = lax.dynamic_slice(small_grads, (0, dp * own), (8, own))
     table_col = jnp.concatenate(
         [
@@ -550,13 +889,13 @@
         mixed,
         d_tokens,
         mine[0],
-        dense[:, :2304],
-        dense[:, 2304:],
+        out_qkv,
+        out_ao,
         table_col.T,
         mine[1],
         mine[2:6].T,
-        out_in.astype(f32)[:, None],
-        out_outw.astype(f32)[:, None],
+        out_in[:, None],
+        out_outw[:, None],
     )
 
 

time: 454 us -> 239 us (0.53)
  waiting for transfers between devices: 202 us -> 32.9 us
  Pallas kernels: 75.7 us -> 158 us
  blocking collectives: 77 us -> 0 us
  matrix products: 39 us -> 2.76 us
  other arithmetic: 10.9 us -> 2.77 us
    reduce_scatter x3 -> x0, waiting for transfers between devices: 115 us -> none  [the longest x1 86.5 us: per_device(): lax.psum_scatter(grad_w_out, 'dp', scatter_dimension=0, tiled=True)]
    pallas_call x1, Pallas kernels: 6.79 us -> 88.7 us  [backward_all(): pl.pallas_call(back_kernel, in_specs=[vm] * len(operands), out_specs=[vm]...]
    psum x1 -> x0, blocking collectives: 65.1 us -> none  [per_device(): small_grads = lax.psum(small_grads, ('dp', 'expert'))]
    psum x1 -> x0, waiting for transfers between devices: 40.8 us -> none  [per_device(): dense = lax.psum(dense.astype(bf16), 'expert').astype(f32)]
    all_to_all x1 -> x0, waiting for transfers between devices: 17.6 us -> none  [per_device(): lax.all_to_all(d_kv, 'expert', split_axis=0, concat_axis=0, tiled=True)]
    dot_general x7 -> x0, matrix products: 15.3 us -> none  [the longest x4 14.3 us: mm_nt(): return lax.dot_general(a, b, NT, preferred_element_type=f32)]
    dot_general x5 -> x1, matrix products: 14.4 us -> 1.24 us  [mm_tn(): return lax.dot_general(a, b, TN, preferred_element_type=f32)]
    all_to_all x1 -> x0, blocking collectives: 12 us -> none  [per_device(): lax.all_to_all(jnp.concatenate([result, d_incoming], 1), 'expert', split_...]
  transfers between devices with their start and end apart: 7 -> 2, of which waited for: 6 -> 2; matrix products, arithmetic and copies ran while one was open for 9% -> 1% of each run, Pallas kernels for 1% -> 0%
where the time goes in v2:
time: 239 us; the launch traced here: 238 us
  Pallas kernels  158 us (66%)
  waiting for transfers between devices  32.9 us (14%)
  local copies, waits for them, and re-layouts  23.6 us (10%)
  between operations  14.4 us (6%)
  starting transfers between devices  3.51 us (1%)
  other arithmetic  2.77 us (1%)
  matrix products  2.76 us (1%)
    pallas_call x1, Pallas kernels, backward_all(): pl.pallas_call(back_kernel, in_specs=[vm] * len(operands), out_specs=[vm]...  88.7 us
    pallas_call x1, Pallas kernels, gather_all(): pl.pallas_call(gather_kernel, in_specs=[vm] * 5, out_specs=[vm] * 5, out_...  64.3 us
    all_gather x1, waiting for transfers between devices, per_device(): kv = lax.all_gather(projected[:, 768:], 'expert', axis=0, tiled=True)  24.7 us
    unnamed x49, local copies, waits for them, and re-layouts  14.3 us
    all_to_all x1, waiting for transfers between devices, per_device(): lax.all_to_all(outgoing, 'expert', split_axis=0, concat_axis=0, tiled=True)  8.23 us
  transfers between devices with their start and end apart: 2, of which 2 were waited for; matrix products, arithmetic and copies ran while one was open for 1% of the time, Pallas kernels for 0%

profile of v2, /device:TPU:0, one launch (start us, length us, event | category | flops | bytes accessed | tf_op | source)
XLA Modules:
  0.0 237.6 jit_solution(12556124044809047639)
XLA Ops:
  7.2 0.7 copy.34
  8.0 0.7 copy.35
  8.7 0.8 copy.36
  9.6 0.7 maximum_convert_fusion.pack
  10.3 0.9 copy-done.6
  11.2 0.9 copy-done.7
  12.2 0.9 copy-done.8
  13.1 0.8 copy-done.9
  13.8 64.3 %shard_map.195 = (bf16[2,4,4,48,1152]{4,3,2,1,0:T(8,128)(2,1)S(1)}, bf16[2,4,4,48,384]{4,3,2,1,0:T(8,128)(2,1)S(1)}, bf16[2,4,4,48,1536]{4,3,2,1,0:T(8,128)(2,1)...) custom-call(bf16[24,2304]{1,0:T(8,128)(2,1)S(1)} %copy-done.8, bf16[24,768]{1,0:T(8,128)(2,1)S(1)} %copy-done.9, ...), custom_call_target="tpu_custom_call" | custom-call | tf_op jit(solution)/shard_map/pallas_call | solution.py:361
  78.5 1.4 copy-done
  80.5 0.7 convolution_convert_fusion
  81.2 0.8 slice.88
  83.0 24.7 %all-gather.2.cloned.1.call-done.kv = bf16[512,1536]{1,0:T(8,128)(2,1)} async-done(((bf16[128,1536]{1,0:T(8,128)(2,1)}), bf16[512,1536]{1,0:T(8,128)(2,1)}) %all-gather.2.cloned.1.call-update) | async-done | bytes 1572880 | tf_op jit(solution)/shard_map/all_gather | solution.py:827
  107.6 1.5 fusion.35
  109.1 4.7 %shard_map.196 = (bf16[128,768]{1,0:T(8,128)(2,1)S(1)}, f32[12,128,512]{2,1,0:T(8,128)S(1)}) custom-call(bf16[128,768]{1,0:T(8,128)(2,1)S(1)} %slice.87.query, bf16[512,768]{1,0:T(8,128)(2,1)S(1)} %get-tuple-element.75.key, bf16[512,768]{1,0:T(8,128)(2,1)S(1)} %get-tuple-element.74.value, f32[16,640]{1,0:T(8,128)S(1)} %concatenate.42.window), custom_call_target="tpu_custom_call" | custom-call | tf_op jit(solution)/shard_map/pallas_call | solution.py:837
  115.6 1.2 convolution_convert_fusion.1
  116.8 3.5 %all-to-all-start = ((bf16[4,48,1536]{2,1,0:T(8,128)(2,1)}), bf16[4,48,1536]{2,1,0:T(8,128)(2,1)S(1)}, u32[]{:S(2)}, u32[]{:S(2)}) async-start(bf16[4,48,1536]{2,1,0:T(8,128)(2,1)} %bitcast.12), calls=%async_computation | async-start | bytes 1179648 | tf_op jit(solution)/shard_map/all_to_all | solution.py:872
  120.3 0.7 fusion.15.placing
  121.0 0.7 copy.39.probs
  121.8 0.7 copy.40.chosen
  122.5 8.2 %all-to-all-done = bf16[4,48,1536]{2,1,0:T(8,128)(2,1)S(1)} async-done(((bf16[4,48,1536]{2,1,0:T(8,128)(2,1)}), bf16[4,48,1536]{2,1,0:T(8,128)(2,1)S(1)}, u32[]{:S(2)}, u32[]{:S(2)}) %all-to-all-start) | async-done | bytes 589856 | tf_op jit(solution)/shard_map/all_to_all | solution.py:872
  130.7 0.8 fusion.37
  131.6 88.7 %shard_map.197 = (bf16[128,768]{1,0:T(8,128)(2,1)}, bf16[128,768]{1,0:T(8,128)(2,1)}, f32[24,2304]{1,0:T(8,128)}, f32[24,768]{1,0:T(8,128)}, f32[24,3072]{1,0:T(...) custom-call(bf16[2,4,4,48,1152]{4,3,2,1,0:T(8,128)(2,1)} %copy-done, bf16[2,4,4,48,384]{4,3,2,1,0:T(8,128)(2,1)} %copy-done.1, ...), custom_call_target="tpu_custom_call" | custom-call | tf_op jit(solution)/shard_map/pallas_call | solution.py:767
  220.3 0.8 slice.81
  221.1 0.6 slice_bitcast_fusion.1
  222.6 2.0 copy.41
  224.6 2.0 copy.42
  226.6 0.6 maximum_bitcast_fusion
  227.2 1.6 copy.47
  228.8 0.7 copy.48
  229.5 0.7 copy.49
  230.1 0.6 copy.50
  (76 shorter events, 4.5 us)
Async XLA Ops:
  7.2 100.5 %all-gather.2.cloned.1.call-start = ((), (), s32[]{:S(2)}) async-start(), calls=%async_computation.1 | async-start | bytes 1966080 | tf_op jit(solution)/shard_map/all_gather | solution.py:827
  10.3 0.9 copy-start.6
  11.2 0.9 copy-start.7
  12.2 0.9 copy-start.8
  13.1 0.8 copy-start.9
  78.1 1.8 copy-start
  78.2 2.2 copy-start.1
  78.2 36.3 %copy-start.14 = (f32[8,1024]{1,0:T(8,128)}, f32[8,1024]{1,0:T(8,128)S(1)}, u32[]{:S(2)}) copy-start(f32[8,1024]{1,0:T(8,128)S(1)} %slice_bitcast_fusion.small_in) | copy-start | bytes 98308
  78.2 2.1 copy-start.13
  80.5 1.6 copy-start.19
  81.2 1.3 copy-start.20
  81.2 1.7 copy-start.2
  82.1 27.1 %copy-start.4 = (bf16[128,768]{1,0:T(8,128)(2,1)}, bf16[128,768]{1,0:T(8,128)(2,1)S(1)}, u32[]{:S(2)}) copy-start(bf16[128,768]{1,0:T(8,128)(2,1)S(1)} %slice.87.query) | copy-start | bytes 589828
  82.6 26.6 %copy-start.18 = (s32[1024]{0:T(1024)}, s32[1024]{0:T(1024)S(1)}, u32[]{:S(2)}) copy-start(s32[1024]{0:T(1024)S(1)} %pad_add_fusion) | copy-start | bytes 12292
  113.8 1.6 copy-start.3
  113.9 1.7 copy-start.5
  113.9 1.2 copy-start.12
  114.3 7.4 %copy-start.11 = (f32[128,768]{1,0:T(8,128)}, f32[128,768]{1,0:T(8,128)S(1)}, u32[]{:S(2)}) copy-start(f32[128,768]{1,0:T(8,128)S(1)} %get-tuple-element.87.after_attn) | copy-start | bytes 1179652
  114.5 17.1 %copy-start.10 = (bf16[128,768]{1,0:T(8,128)(2,1)}, bf16[128,768]{1,0:T(8,128)(2,1)S(1)}, u32[]{:S(2)}) copy-start(bf16[128,768]{1,0:T(8,128)(2,1)S(1)} %multiply_convert_fusion.1.moe_input) | copy-start | bytes 589828
  116.8 13.9 %all-to-all-start = ((bf16[4,48,1536]{2,1,0:T(8,128)(2,1)}), bf16[4,48,1536]{2,1,0:T(8,128)(2,1)S(1)}, u32[]{:S(2)}, u32[]{:S(2)}) async-start(bf16[4,48,1536]{2,1,0:T(8,128)(2,1)} %bitcast.12), calls=%async_computation | async-start | bytes 1179648 | tf_op jit(solution)/shard_map/all_to_all | solution.py:872
  220.2 8.6 %copy-start.16 = (bf16[128,768]{1,0:T(8,128)(2,1)S(1)}, bf16[128,768]{1,0:T(8,128)(2,1)}, u32[]{:S(2)}) copy-start(bf16[128,768]{1,0:T(8,128)(2,1)} %get-tuple-element.101) | copy-start | bytes 589828
  220.2 9.2 %copy-start.15 = (f32[24,2304]{1,0:T(8,128)S(1)}, f32[24,2304]{1,0:T(8,128)}, u32[]{:S(2)}) copy-start(f32[24,2304]{1,0:T(8,128)} %get-tuple-element.103) | copy-start | bytes 663556
  220.2 9.9 %copy-start.17 = (f32[24,768]{1,0:T(8,128)S(1)}, f32[24,768]{1,0:T(8,128)}, u32[]{:S(2)}) copy-start(f32[24,768]{1,0:T(8,128)} %get-tuple-element.104) | copy-start | bytes 221188
Sparse Core Ops, SparseCore 0:
  82.1 25.4 all-gather.1

commit v3 on v2

--- a/solution.py
+++ b/solution.py
@@ -56,45 +56,6 @@
         wide = jnp.where((row & bit) != 0, pltpu.roll(wide, width - bit, 1), wide)
     total = jnp.sum(wide, 0, keepdims=True)
     return pltpu.roll(total, rows - 1, 1)
-
-
-def attention_forward(query, key, value, window, out, weights):
-    pair = pl.program_id(0)
-    rows = query.shape[0]
-    keys = key.shape[0]
-    bias = jnp.concatenate(
-        [toeplitz(window[pl.ds(2 * pair + j, 1), :], rows, keys) for j in (0, 1)], 0
-    )
-    scores = mm_nt(stack_heads(query[...]), key[...]) + bias
-    top = jnp.max(scores, -1, keepdims=True)
-    raised = jnp.exp(scores - top)
-    probability = raised / jnp.sum(raised, -1, keepdims=True)
-    weights[...] = probability.reshape(2, rows, keys)
-    out[...] = join_pair(mm(probability.astype(bf16), value[...])).astype(bf16)
-
-
-def attention_backward(query, key, value, weights, d_out, d_query, d_key, d_value, d_window):
-    rows = query.shape[0]
-    keys = key.shape[0]
-    probability = weights[...].reshape(2 * rows, keys)
-    d_stack = stack_heads(d_out[...])
-    d_weights = mm_nt(d_stack, value[...])
-    d_value[...] = mm_tn(probability.astype(bf16), d_stack).astype(bf16)
-    d_scores = probability * (
-        d_weights - jnp.sum(probability * d_weights, -1, keepdims=True)
-    )
-    for j in (0, 1):
-        d_window[0, j : j + 1, :] = diagonal_sums(
-            d_scores[j * rows : (j + 1) * rows], d_window.shape[2]
-        )
-    low = d_scores.astype(bf16)
-    d_query[...] = join_pair(mm(low, key[...])).astype(bf16)
-    d_key[...] = mm_tn(low, stack_heads(query[...])).astype(bf16)
-
-
-def rms_forward(values, gain):
-    r = lax.rsqrt(jnp.mean(values * values, -1, keepdims=True) + epsilon)
-    return r, values * r * gain
 
 
 def rms_backward(values, r, gain, grad):
@@ -301,90 +262,6 @@
     )
 
 
-def gather_kernel(
-    w_qkv, w_ao, w_in, w_out, pack, g_qkv, g_ao, g_in, g_out, small,
-    stage, other, pair_sem, sends, recvs, arrivals, small_send, small_recv,
-):
-    o = Place()
-    o.barrier(False)
-    flows = [
-        Gather(o, ref, tall, sends.at[i], recvs.at[i], i)
-        for i, (ref, tall) in enumerate(((g_qkv, 0), (g_ao, 0), (g_in, 0), (g_out, 1)))
-    ]
-    qkv, ao, win, wout = flows
-    pair = meet(o, (w_qkv, w_ao, w_in), stage, other, pair_sem)
-    pair.start()
-    tot = SmallSum(o, small, arrivals, small_send, small_recv, False)
-    small[0] = place_small(o, pack)
-    tot.start(0)
-    g_out[o.y, o.z, o.c] = w_out[...]
-    pair.wait_recv()
-    at = 0
-    for ref in (g_qkv, g_ao, g_in):
-        n = ref.shape[-1]
-        ref[o.c, o.y, o.z] = stage[:, at : at + n].astype(bf16)
-        at += n
-    qkv.ring_one()
-    tot.add(0)
-    tot.start(1)
-    qkv.ring_one_far()
-    qkv.ring_two()
-    for f in (ao, win, wout):
-        f.ring_one()
-    tot.add(1)
-    tot.start(2)
-    for f in (ao, win, wout):
-        f.ring_one_far()
-    qkv.ring_two_far()
-    for f in (ao, win, wout):
-        f.ring_two()
-    tot.add(2)
-    qkv.last()
-    ao.ring_two_far()
-    qkv.finish()
-    ao.last()
-    win.ring_two_far()
-    ao.finish()
-    win.last()
-    wout.ring_two_far()
-    win.finish()
-    wout.last()
-    wout.finish()
-    pair.wait_send()
-    tot.drain()
-    for f in flows:
-        f.drain()
-
-
-def gather_all(w_qkv, w_ao, w_in, w_out, pack):
-    vm = pl.BlockSpec(memory_space=pltpu.VMEM)
-    return pl.pallas_call(
-        gather_kernel,
-        in_specs=[vm] * 5,
-        out_specs=[vm] * 5,
-        out_shape=[
-            jax.ShapeDtypeStruct((2, 4, 4, 48, 1152), bf16),
-            jax.ShapeDtypeStruct((2, 4, 4, 48, 384), bf16),
-            jax.ShapeDtypeStruct((2, 4, 4, 48, 1536), bf16),
-            jax.ShapeDtypeStruct((4, 4, 2, 96, 768), bf16),
-            jax.ShapeDtypeStruct((4, 8, 1024), f32),
-        ],
-        scratch_shapes=[
-            pltpu.VMEM((48, 3072), f32),
-            pltpu.VMEM((24, 3072), f32),
-            pltpu.SemaphoreType.DMA((2,)),
-            pltpu.SemaphoreType.DMA((4, 11)),
-            pltpu.SemaphoreType.DMA((4, 11)),
-            pltpu.VMEM((7, 8, 1024), f32),
-            pltpu.SemaphoreType.DMA((7,)),
-            pltpu.SemaphoreType.DMA((7,)),
-        ],
-        compiler_params=pltpu.CompilerParams(
-            collective_id=0, has_side_effects=True, vmem_limit_bytes=48 * 2**20
-        ),
-    )(w_qkv, w_ao, w_in, w_out, pack)
-
-
 class Scatter:
     def __init__(self, place, ref, tall, pair, far, near, side, send, recv):
         self.o, self.ref, self.tall = place, ref, tall
@@ -553,10 +430,55 @@
         d_window[pl.ds(2 * i + j, 1), :] = diagonal_sums(d_scores[j * 128 : (j + 1) * 128], 640)
 
 
-def back_kernel(
-    g_qkv, g_ao, g_in, g_out, sent, d_result, placing, after_attn, probs, chosen, cotangent,
-    moe_input, heads_out, tokens, query, kv, weights, small_in, buckets,
+class Spread:
+    def __init__(self, place, ref, send, recv):
+        self.o, self.ref, self.send, self.recv = place, ref, send, recv
+
+    def view(self, by, low, count):
+        row = pl.multiple_of(lax.rem(self.o.x + by, 4) * 128, 128)
+        return self.ref.at[pl.ds(row, 128), pl.ds(low, count)]
+
+    def copy(self, n, by, low, count, to):
+        view = self.view(by, low, count)
+        return remote(view, view, self.send.at[n], self.recv.at[n], self.o.along_x(to))
+
+    def start(self, part):
+        self.copy(2 * part, 0, part * 768, 768, 1).start()
+        self.copy(2 * part + 1, 0, part * 768, 768, 3).start()
+
+    def forward(self):
+        self.copy(0, 3, 0, 768, 1).wait_recv()
+        self.copy(4, 3, 0, 768, 1).start()
+        self.copy(3, 1, 768, 768, 3).wait_recv()
+        self.copy(5, 1, 768, 768, 3).start()
+
+    def finish(self):
+        for n in (1, 2, 4, 5):
+            self.copy(n, 0, 0, 768, 1).wait_recv()
+
+    def drain(self):
+        for n in range(6):
+            self.copy(n, 0, 0, 768, 1).wait_send()
+
+
+def pair_forward(i, query, kv, window, heads_out, weights):
+    lanes = pl.ds(pl.multiple_of(i * 128, 128), 128)
+    value_lanes = pl.ds(pl.multiple_of(i * 128 + 768, 128), 128)
+    bias = jnp.concatenate([toeplitz(window[pl.ds(2 * i + j, 1), :], 128, 512) for j in (0, 1)], 0)
+    scores = mm_nt(stack_heads(query[:, lanes]), kv[:, lanes]) + bias
+    top = jnp.max(scores, -1, keepdims=True)
+    raised = jnp.exp(scores - top)
+    probability = raised / jnp.sum(raised, -1, keepdims=True)
+    weights[pl.ds(2 * i, 2)] = probability.reshape(2, 128, 512)
+    heads_out[:, lanes] = join_pair(mm(probability.astype(bf16), kv[:, value_lanes])).astype(bf16)
+
+
+def layer_kernel(
+    w_qkv, w_ao, w_in, w_out, pack, tokens, routes, buckets, cotangent,
     mixed, d_tokens, out_qkv, out_ao, out_in, out_out, small,
+    stage, other, pair_sem, g_sends, g_recvs, side_in, side_arrivals, side_send, side_recv,
+    g_qkv, g_ao, g_in, g_out, normed_ref, query, kv, kv_send, kv_recv, window, weights, heads_out,
+    after_attn, moe_input, placing, probs, chosen, disp, inc, disp_send, disp_recv, sent, d_result,
     h_qkv, h_ao, h_in, h_out, sent_t, result, d_incoming, ret, back, d_query, d_kv, d_kr, d_window,
     d_heads_ref, d_after_ref, total_q, total_a, total_i, xs, xr, xa,
     pair_q, pair_a, pair_i, pair_o, far_q, far_a, far_i, far_o, near_q, near_a, near_i, near_o,
@@ -566,6 +488,121 @@
 ):
     o = Place()
     o.barrier(True)
+    flows = [
+        Gather(o, ref, tall, g_sends.at[i], g_recvs.at[i], i)
+        for i, (ref, tall) in enumerate(((g_qkv, 0), (g_ao, 0), (g_in, 0), (g_out, 1)))
+    ]
+    qkv, ao, win, wout = flows
+    pair_copy = meet(o, (w_qkv, w_ao, w_in), stage, other, pair_sem)
+    pair_copy.start()
+    side = SmallSum(o, side_in, side_arrivals, side_send, side_recv, False)
+    side_in[0] = place_small(o, pack)
+    side.start(0)
+    g_out[o.y, o.z, o.c] = w_out[...]
+    pair_copy.wait_recv()
+    at = 0
+    for ref in (g_qkv, g_ao, g_in):
+        n = ref.shape[-1]
+        ref[o.c, o.y, o.z] = stage[:, at : at + n].astype(bf16)
+        at += n
+    qkv.ring_one()
+    side.add(0)
+    side.start(1)
+    qkv.ring_one_far()
+    qkv.ring_two()
+    for f in (ao, win, wout):
+        f.ring_one()
+    side.add(1)
+    side.start(2)
+    x = tokens[...].astype(f32)
+    r_one = lax.rsqrt(jnp.mean(x * x, -1, keepdims=True) + epsilon)
+    bucket_row = buckets[:, pl.ds(pl.multiple_of((3 - o.x) * 128, 128), 640)]
+    picks = jnp.where(
+        jnp.broadcast_to(bucket_row, (128, 640)) == lax.broadcasted_iota(jnp.int32, (128, 640), 0), 1.0, 0.0
+    )
+    for f in (ao, win, wout):
+        f.ring_one_far()
+    qkv.ring_two_far()
+    for f in (ao, win, wout):
+        f.ring_two()
+    side.add(2)
+    small_in = side_in.at[3]
+    normed_ref[...] = (x * r_one * small_in[0:1, :768]).astype(bf16)
+    table_t = jnp.concatenate([small_in[:, 768:896], small_in[:, 896:1024]], 0)
+    window[...] = mm(table_t.astype(bf16), picks.astype(bf16))
+    qkv.last()
+    ao.ring_two_far()
+    qkv.finish()
+
+    own_rows = pl.ds(pl.multiple_of(o.x * 128, 128), 128)
+    spread = Spread(o, kv, kv_send, kv_recv)
+    high = mm(normed_ref[...], g_qkv[1].reshape(768, 1152)).astype(bf16)
+    kv[own_rows, 384:1536] = high
+    spread.start(1)
+    low = mm(normed_ref[...], g_qkv[0].reshape(768, 1152)).astype(bf16)
+    kv[own_rows, 0:384] = low[:, 768:]
+    spread.start(0)
+    query[...] = low[:, :768]
+    ao.last()
+    win.ring_two_far()
+    spread.forward()
+    ao.finish()
+    spread.finish()
+
+    def ahead(i, carry):
+        pair_forward(i, query, kv, window, heads_out, weights)
+        return carry
+
+    lax.fori_loop(0, 3, ahead, 0)
+    win.last()
+    lax.fori_loop(3, 6, ahead, 0)
+    wout.ring_two_far()
+    mixed_heads = heads_out[...]
+    attn = x + jnp.concatenate([mm(mixed_heads, g_ao[h].reshape(768, 384)) for h in (0, 1)], 1)
+    after_attn[...] = attn
+    small8 = small_in[:, :768]
+    r_two = lax.rsqrt(jnp.mean(attn * attn, -1, keepdims=True) + epsilon)
+    moe_low = (attn * r_two * small8[1:2]).astype(bf16)
+    moe_input[...] = moe_low
+    logits = mm_nt(moe_low, small8.astype(bf16))
+    lane = lax.broadcasted_iota(jnp.int32, (128, 8), 1)
+    logits = jnp.where((lane >= 2) & (lane < 6), logits, -1e30)
+    raised = jnp.exp(logits - jnp.max(logits, -1, keepdims=True))
+    probability = raised / jnp.sum(raised, -1, keepdims=True)
+    probs[...] = probability
+    picked = jnp.where(lane == routes[...] + 2, 1.0, 0.0)
+    chosen[...] = picked
+    gate = jnp.sum(probability * picked, -1, keepdims=True)
+    before = jnp.where(
+        lax.broadcasted_iota(jnp.int32, (128, 128), 1) < lax.broadcasted_iota(jnp.int32, (128, 128), 0), 1.0, 0.0
+    )
+    slot = jnp.sum(mm(before.astype(bf16), picked.astype(bf16)) * picked, -1, keepdims=True)
+    column = routes[...].astype(f32) * 48.0 + slot
+    place = jnp.where(
+        lax.broadcasted_iota(jnp.int32, (128, 192), 1).astype(f32) == column, 1.0, 0.0
+    ).astype(bf16)
+    placing[...] = place
+    disp[:, 0] = mm_tn(place, moe_low).astype(bf16).reshape(4, 48, 768)
+    d_combined = (gate * cotangent[...].astype(f32)).astype(bf16)
+    disp[:, 1] = mm_tn(place, d_combined).astype(bf16).reshape(4, 48, 768)
+    disp_copies = [
+        remote(
+            disp.at[lax.rem(o.x + by, 4)], inc.at[o.x], disp_send.at[by - 1], disp_recv.at[by - 1],
+            o.along_x(by),
+        )
+        for by in (1, 2, 3)
+    ]
+    for copy in disp_copies:
+        copy.start()
+    inc[o.x] = disp[o.x]
+    win.finish()
+    wout.last()
+    for copy in disp_copies:
+        copy.wait_recv()
+    sent[...] = inc[:, 0].reshape(192, 768)
+    d_result[...] = inc[:, 1].reshape(192, 768)
+    wout.finish()
+
     fq = Scatter(o, h_qkv, 0, pair_q, far_q, near_q, side_q, sends.at[0], recvs.at[0])
     fa = Scatter(o, h_ao, 0, pair_a, far_a, near_a, side_a, sends.at[1], recvs.at[1])
     fi = Scatter(o, h_in, 0, pair_i, far_i, near_i, side_i, sends.at[2], recvs.at[2])
@@ -603,11 +640,11 @@
     for copy in ret_copies:
         copy.wait_recv()
 
-    small8 = small_in[:, :768]
     gain_one, gain_two = small8[0:1], small8[1:2]
     returned = mm(placing[...], back[:, 0].reshape(192, 768))
     d_moe = mm(placing[...], back[:, 1].reshape(192, 768))
     attn = after_attn[...]
+    r_two = lax.rsqrt(jnp.mean(attn * attn, -1, keepdims=True) + epsilon)
     upstream = cotangent[...].astype(f32)
     gate = jnp.sum(probs[...] * chosen[...], -1, keepdims=True)
     mixed[...] = (attn + gate * returned).astype(bf16)
@@ -617,7 +654,6 @@
     grad_router = lax.dot_general(
         d_logits, moe_input[...].astype(f32), TN, precision=highest, preferred_element_type=f32
     )
-    r_two = lax.rsqrt(jnp.mean(attn * attn, -1, keepdims=True) + epsilon)
     d_after, grad_norm_two = rms_backward(attn, r_two, gain_two, d_moe)
     d_after = d_after + upstream
     d_after_ref[...] = d_after
@@ -653,17 +689,12 @@
     fa.ring_far()
 
     x = tokens[...].astype(f32)
-    r_one, normed = rms_forward(x, gain_one)
-    normed_t = normed.T.astype(bf16)
+    normed_t = normed_ref[...].astype(f32).T.astype(bf16)
 
     def project(h, d_part):
         h_qkv[h] = mm(normed_t, d_part).astype(bf16).reshape(4, 4, 48, 1152)
         return mm_nt(d_part, g_qkv[h].reshape(768, 1152))
 
-    bucket_row = buckets[:, pl.ds(pl.multiple_of((3 - o.x) * 128, 128), 640)]
-    picks = jnp.where(
-        jnp.broadcast_to(bucket_row, (128, 640)) == lax.broadcasted_iota(jnp.int32, (128, 640), 0), 1.0, 0.0
-    )
     grad_table = lax.dot_general(
         d_window[...], picks, NT, precision=highest, preferred_element_type=f32
     )
@@ -677,6 +708,7 @@
         d_own = d_own + d_kr[by].astype(f32)
     d_own = d_own.astype(bf16)
     d_key, d_value = d_own[0], d_own[1]
+    r_one = lax.rsqrt(jnp.mean(x * x, -1, keepdims=True) + epsilon)
     d_normed = project(0, jnp.concatenate([d_query[...], d_key[:, :384]], 1))
     d_normed = d_normed + project(1, jnp.concatenate([d_key[:, 384:], d_value], 1))
     fq.to_pair(0, 0, 4)
@@ -751,9 +783,16 @@
     for f in (fq, fa, fi):
         f.drain([(0, 4)])
     fo.drain([(0, 2), (1, 2)])
-
-
-def backward_all(*operands):
+    pair_copy.wait_send()
+    side.drain()
+    spread.drain()
+    for copy in disp_copies:
+        copy.wait_send()
+    for f in flows:
+        f.drain()
+
+
+def layer(*operands):
     vm = pl.BlockSpec(memory_space=pltpu.VMEM)
     dma = pltpu.SemaphoreType.DMA
 
@@ -764,8 +803,9 @@
         return pltpu.VMEM(shape, f32)
 
     sizes = ((48, 1152), (48, 384), (48, 1536), (96, 768))
+    weights = (low(2, 4, 4, 48, 1152), low(2, 4, 4, 48, 384), low(2, 4, 4, 48, 1536), low(4, 4, 2, 96, 768))
     return pl.pallas_call(
-        back_kernel,
+        layer_kernel,
         in_specs=[vm] * len(operands),
         out_specs=[vm] * 7,
         out_shape=[
@@ -778,7 +818,13 @@
             jax.ShapeDtypeStruct((5, 8, 1024), f32),
         ],
         scratch_shapes=[
-            low(2, 4, 4, 48, 1152), low(2, 4, 4, 48, 384), low(2, 4, 4, 48, 1536), low(4, 4, 2, 96, 768),
+            full(48, 3072), full(24, 3072), dma((2,)), dma((4, 11)), dma((4, 11)),
+            full(4, 8, 1024), full(7, 8, 1024), dma((7,)), dma((7,)),
+            *weights, low(128, 768), low(128, 768), low(512, 1536), dma((6,)), dma((6,)), full(16, 640),
+            full(12, 128, 512), low(128, 768), full(128, 768), low(128, 768), low(128, 192),
+            full(128, 8), full(128, 8), low(4, 2, 48, 768), low(4, 2, 48, 768), dma((3,)), dma((3,)),
+            low(192, 768), low(192, 768),
+            *weights,
             low(768, 192), full(192, 768), full(192, 768), low(4, 2, 48, 768), low(4, 2, 48, 768),
             low(128, 768), low(4, 2, 128, 768), low(3, 2, 128, 768), full(16, 640),
             low(128, 768), full(128, 768), full(48, 1152), full(48, 384), full(48, 1536),
@@ -792,7 +838,7 @@
             full(10, 8, 1024), dma((10,)), dma((10,)),
         ],
         compiler_params=pltpu.CompilerParams(
-            collective_id=1, has_side_effects=True, vmem_limit_bytes=60 * 2**20
+            collective_id=0, has_side_effects=True, vmem_limit_bytes=62 * 2**20
         ),
     )(*operands)
 
@@ -800,102 +846,27 @@
 def per_device(
     tokens, norm_attn, w_qkv, w_attn_out, bias_table, norm_moe, router, w_in, w_out, routes, buckets, cotangent
 ):
-    rows, width = tokens.shape
     dp = lax.axis_index("dp")
-    ex = lax.axis_index("expert")
-    groups = 4
-    keys = rows * groups
-    heads = 12
-    window_width = keys + rows
-
     own = norm_attn.shape[0]
     pack = jnp.concatenate([norm_attn[:, None], norm_moe[:, None], router, jnp.zeros((own, 122), bf16)], 1)
     last = jnp.concatenate([jnp.zeros((1, 8), bf16), bias_table, jnp.zeros((1, 108), bf16)], 1)
-    pack = jnp.concatenate([pack, last, jnp.zeros((7, 128), bf16)], 0).astype(f32)
-    g_qkv, g_ao, g_in, g_out, small = gather_all(w_qkv, w_attn_out, w_in[:, 0], w_out[:, 0], pack)
-    small = small[3]
-    full_qkv = jnp.concatenate([g_qkv[0].reshape(768, -1), g_qkv[1].reshape(768, -1)], 1)
-    full_out = jnp.concatenate([g_ao[0].reshape(768, -1), g_ao[1].reshape(768, -1)], 1)
-    gain_one, gain_two, router_t = small[0:1, :768], small[1:2, :768], small[2:6, :768]
-    table_full = jnp.concatenate([small[:8, 768:800], small[:4, 896:928]], 0)
-
-    x = tokens.astype(f32)
-    r_one, normed = rms_forward(x, gain_one)
-    normed = normed.astype(bf16)
-    projected = mm(normed, full_qkv).astype(bf16)
-    query = projected[:, :768]
-    kv = lax.all_gather(projected[:, 768:], "expert", axis=0, tiled=True)
-    key, value = kv[:, :768], kv[:, 768:]
-    padded = jnp.concatenate([buckets, jnp.zeros((1,), jnp.int32)])
-    bucket_window = lax.dynamic_slice_in_dim(padded, (groups - 1 - ex) * rows, window_width, 0)
-    picks = (bucket_window[None, :] == jnp.arange(32, dtype=jnp.int32)[:, None]).astype(f32)
-    window = jnp.concatenate(
-        [jnp.dot(table_full, picks, precision=highest), jnp.zeros((4, window_width), f32)], 0
-    )
-
-    pairs = heads // 2
-    heads_out, weights = pl.pallas_call(
-        attention_forward,
-        grid=(pairs,),
-        in_specs=[
-            pl.BlockSpec((rows, 128), lambda p: (0, p)),
-            pl.BlockSpec((keys, 128), lambda p: (0, p)),
-            pl.BlockSpec((keys, 128), lambda p: (0, p)),
-            pl.BlockSpec((16, window_width), lambda p: (0, 0)),
-        ],
-        out_specs=[
-            pl.BlockSpec((rows, 128), lambda p: (0, p)),
-            pl.BlockSpec((2, rows, keys), lambda p: (p, 0, 0)),
-        ],
-        out_shape=[
-            jax.ShapeDtypeStruct((rows, width), bf16),
-            jax.ShapeDtypeStruct((heads, rows, keys), f32),
-        ],
-        compiler_params=pltpu.CompilerParams(vmem_limit_bytes=32 * 2**20),
-    )(query, key, value, window)
-
-    after_attn = x + mm(heads_out, full_out)
-    r_two, moe_input = rms_forward(after_attn, gain_two)
-    moe_input = moe_input.astype(bf16)
-    logits = jnp.dot(moe_input.astype(f32), router_t.T, precision=highest)
-    probs = jax.nn.softmax(logits, -1)
-    chosen_int = (routes == jnp.arange(4, dtype=jnp.int32)[None, :]).astype(jnp.int32)
-    chosen = chosen_int.astype(f32)
-    gate = jnp.sum(probs * chosen, -1, keepdims=True)
-    slots = 48
-    slot = jnp.sum((jnp.cumsum(chosen_int, 0) - 1) * chosen_int, -1)
-    column = routes[:, 0] * slots + slot
-    placing = (column[:, None] == jnp.arange(4 * slots, dtype=jnp.int32)[None, :]).astype(bf16)
-    upstream = cotangent.astype(f32)
-    d_combined = (gate * upstream).astype(bf16)
-    outgoing = mm_tn(placing, jnp.concatenate([moe_input, d_combined], 1)).astype(bf16)
-    incoming = lax.all_to_all(outgoing, "expert", split_axis=0, concat_axis=0, tiled=True)
-    probs8 = jnp.concatenate([jnp.zeros((rows, 2), f32), probs, jnp.zeros((rows, 2), f32)], 1)
-    chosen8 = jnp.concatenate([jnp.zeros((rows, 2), f32), chosen, jnp.zeros((rows, 2), f32)], 1)
-    mixed, d_tokens, out_qkv, out_ao, out_in, out_outw, small_grads = backward_all(
-        g_qkv, g_ao, g_in, g_out, incoming[:, :768], incoming[:, 768:], placing, after_attn, probs8, chosen8,
-        cotangent, moe_input, heads_out, tokens, query, kv, weights, small, padded[None, :],
-    )
-    small_grads = small_grads[4]
-    mine = lax.dynamic_slice(small_grads, (0, dp * own), (8, own))
+    pack = jnp.concatenate([pack, last, jnp.zeros((7, 128), bf16)], 0)
+    padded = jnp.concatenate([buckets, jnp.zeros((1,), jnp.int32)])[None, :]
+    mixed, d_tokens, out_qkv, out_ao, out_in, out_out, small = layer(
+        w_qkv, w_attn_out, w_in[:, 0], w_out[:, 0], pack, tokens, routes, padded, cotangent
+    )
+    small = small[4]
+    mine = lax.dynamic_slice(small, (0, dp * own), (8, own))
     table_col = jnp.concatenate(
         [
-            lax.dynamic_slice(small_grads, (0, 768 + dp), (8, 1)),
-            lax.dynamic_slice(small_grads, (0, 896 + dp), (4, 1)),
+            lax.dynamic_slice(small, (0, 768 + dp), (8, 1)),
+            lax.dynamic_slice(small, (0, 896 + dp), (4, 1)),
         ],
         0,
     )
     return (
-        mixed,
-        d_tokens,
-        mine[0],
-        out_qkv,
-        out_ao,
-        table_col.T,
-        mine[1],
-        mine[2:6].T,
-        out_in[:, None],
-        out_outw[:, None],
+        mixed, d_tokens, mine[0], out_qkv, out_ao, table_col.T, mine[1], mine[2:6].T,
+        out_in[:, None], out_out[:, None],
     )
 
 

time: 239 us -> 168 us (0.70)
  waiting for transfers between devices: 32.9 us -> 0 us
  between operations: 14.4 us -> 0.7 us
  local copies, waits for them, and re-layouts: 23.6 us -> 13.2 us
  Pallas kernels: 158 us -> 150 us
  starting transfers between devices: 3.51 us -> 0 us
  matrix products: 2.76 us -> 0 us
    all_gather x1 -> x0, waiting for transfers between devices: 24.7 us -> none  [per_device(): kv = lax.all_gather(projected[:, 768:], 'expert', axis=0, tiled=True)]
    all_to_all x1 -> x0, waiting for transfers between devices: 8.23 us -> none  [per_device(): lax.all_to_all(outgoing, 'expert', split_axis=0, concat_axis=0, tiled=True)]
    pallas_call x3 -> x1, Pallas kernels: 158 us -> 150 us  [layer(): pl.pallas_call(layer_kernel, in_specs=[vm] * len(operands), out_specs=[vm...]
    unnamed x49 -> x30, local copies, waits for them, and re-layouts: 14.3 us -> 10.6 us
    slice x10 -> x1, local copies, waits for them, and re-layouts: 4.4 us -> 0.76 us  [per_device(): small = small[4]]
    all_to_all x1 -> x0, starting transfers between devices: 3.48 us -> none  [per_device(): lax.all_to_all(outgoing, 'expert', split_axis=0, concat_axis=0, tiled=True)]
    dot_general x5 -> x0, matrix products: 2.76 us -> none  [the longest x1 1.24 us: mm_tn(): return lax.dot_general(a, b, TN, preferred_element_type=f32)]
  transfers between devices with their start and end apart: 2 -> 0, of which waited for: 2 -> 0; matrix products, arithmetic and copies ran while one was open for 1% -> 0% of each run, Pallas kernels for 0% -> 0%
where the time goes in v3:
time: 168 us; the launch traced here: 166 us
  Pallas kernels  150 us (89%)
  local copies, waits for them, and re-layouts  13.2 us (8%)
  other arithmetic  1.94 us (1%)
    pallas_call x1, Pallas kernels, layer(): pl.pallas_call(layer_kernel, in_specs=[vm] * len(operands), out_specs=[vm...  150 us
    unnamed x30, local copies, waits for them, and re-layouts  10.6 us

profile of v3, /device:TPU:0, one launch (start us, length us, event | category | flops | bytes accessed | tf_op | source)
XLA Modules:
  0.0 166.1 jit_solution(4124304672459241642)
XLA Ops:
  0.6 0.0 copy-start.7
  0.7 0.6 copy-done.7
  1.3 0.7 copy.31.routes
  2.0 0.7 copy-done.9
  2.7 0.1 copy.28
  2.8 0.7 copy-done.10
  3.5 0.1 copy.29
  3.6 0.6 copy-done.6
  4.1 0.1 copy.30
  4.2 0.1 pad.11.clone
  4.3 0.6 copy-done.8
  5.0 0.7 maximum_maximum_fusion.pack
  5.7 0.0 copy-done.5
  5.7 0.7 pad_add_fusion
  6.3 150.2 %shard_map.195 = (bf16[128,768]{1,0:T(8,128)(2,1)}, bf16[128,768]{1,0:T(8,128)(2,1)}, f32[24,2304]{1,0:T(8,128)}, f32[24,768]{1,0:T(8,128)}, f32[24,3072]{1,0:T(...) custom-call(bf16[24,2304]{1,0:T(8,128)(2,1)} %w_qkv.1, bf16[24,768]{1,0:T(8,128)(2,1)} %w_ao.1, ...), custom_call_target="tpu_custom_call" | custom-call | tf_op jit(solution)/shard_map/pallas_call | solution.py:807
  156.6 0.8 slice.17
  157.3 0.2 dynamic-slice_reduce_fusion
  157.5 0.2 dynamic-slice_reduce_fusion.1
  157.7 0.6 maximum_bitcast_fusion
  158.3 0.1 constant_dynamic-slice_fusion
  158.4 0.5 slice_bitcast_fusion.1
  158.9 0.6 slice_bitcast_fusion
  159.5 2.0 %copy.32 = f32[24,1,3072]{2,1,0:T(1,128)} copy(f32[24,1,3072]{2,0,1:T(8,128)} %bitcast.20) | data formatting | bytes 589824
  161.5 0.0 copy-done
  161.5 1.0 copy.33
  162.5 0.7 copy.38
  163.2 0.3 copy-done.2
  163.5 0.7 copy.39
  164.2 0.3 copy-done.1
  164.5 0.7 copy.40
  165.2 0.2 copy-done.4
  165.5 0.6 copy.41
  (15 shorter events, 0.0 us)
Async XLA Ops:
  0.6 0.7 copy-start.7
  2.0 0.7 copy-start.9
  2.8 0.7 copy-start.10
  3.5 0.7 copy-start.6
  4.3 0.7 copy-start.8
  5.0 0.7 copy-start.5
  159.5 2.0 %copy-start = (f32[96,768]{1,0:T(8,128)S(1)}, f32[96,768]{1,0:T(8,128)}, u32[]{:S(2)}) copy-start(f32[96,768]{1,0:T(8,128)} %get-tuple-element.23) | copy-start | bytes 884740
  161.5 1.0 copy-start.3
  162.5 1.0 copy-start.2
  163.5 1.0 copy-start.1
  164.5 0.9 copy-start.4

commit v4 on v3

--- a/solution.py
+++ b/solution.py
@@ -58,6 +58,11 @@
     return pltpu.roll(total, rows - 1, 1)
 
 
+def rms_forward(values, gain):
+    r = lax.rsqrt(jnp.mean(values * values, -1, keepdims=True) + epsilon)
+    return r, values * r * gain
+
+
 def rms_backward(values, r, gain, grad):
     u = grad * gain
     d_values = r * u - values * (r * r * r) * jnp.mean(u * values, -1, keepdims=True)
@@ -107,7 +112,7 @@
         sem = pltpu.get_barrier_semaphore()
         for peer in peers:
             pl.semaphore_signal(sem, inc=1, device_id=peer, device_id_type=MESH)
-        pl.semaphore_wait(sem, len(peers))
+        return lambda: pl.semaphore_wait(sem, len(peers))
 
 
 def remote(src, dst, send, recv, to):
@@ -164,10 +169,14 @@
     def ring_one(self):
         self.go(lambda k: self.block(k, 0), 0, 0, self.o.along_p(1))
         self.go(lambda k: self.block(k, 0), 1, 1, self.o.along_p(3))
+        if self.number == 0:
+            self.go(lambda k: self.block(k, 0), 2, 2, self.o.along_p(2))
 
     def ring_one_far(self):
         self.arrived(0, 1)
         self.arrived(1, 1)
+        if self.number == 0:
+            return
         if self.number % 2 == 0:
             self.go(lambda k: self.block(k, 3), 2, 2, self.o.along_p(1))
         else:
@@ -237,15 +246,21 @@
                 copy.wait_send()
 
 
-def place_small(o, pack):
-    row = lax.broadcasted_iota(jnp.int32, (32, 1024), 0)
-    lane = lax.broadcasted_iota(jnp.int32, (32, 1024), 1)
-    target = jnp.where(row < 24, 24 * o.d + row, jnp.where(row == 24, 768 + o.d, -1))
-    hit = jnp.where(lane == target, 1.0, 0.0)
-    spread = mm_tn(pack[...].astype(bf16), hit.astype(bf16))
-    return jnp.concatenate(
-        [spread[0:8, :768], spread[8:16, 768:896], spread[16:24, 768:896]], 1
-    )
+def place_small(o, out, na, nm, router_t, table):
+    row = lax.broadcasted_iota(jnp.int32, (24, 768), 0)
+    lane = lax.broadcasted_iota(jnp.int32, (24, 768), 1)
+    hit = jnp.where(lane == 24 * o.d + row, 1.0, 0.0)
+    out[...] = jnp.zeros((8, 1024), f32)
+    out[0:1, 0:768] = mm(na[...].astype(f32), hit)
+    out[1:2, 0:768] = mm(nm[...].astype(f32), hit)
+    out[2:6, 0:768] = mm(router_t[...].astype(f32), hit)
+    head = lax.broadcasted_iota(jnp.int32, (16, 12), 0) == lax.broadcasted_iota(jnp.int32, (16, 12), 1)
+    wide = jnp.broadcast_to(table[...].astype(f32), (16, 12))
+    column = jnp.sum(jnp.where(head, wide, 0.0), -1, keepdims=True)
+    own = lax.broadcasted_iota(jnp.int32, (16, 128), 1) == o.d
+    placed = jnp.where(own, jnp.broadcast_to(column, (16, 128)), 0.0)
+    out[:, 768:896] = placed[0:8]
+    out[:, 896:1024] = placed[8:16]
 
 
 def meet(o, halves, stage, other, sem):
@@ -390,75 +405,51 @@
     return value, slope
 
 
-def expert_chunk(j, sent, sent_t, d_result, g_in, g_out, h_in, h_out, result, d_incoming):
-    half, at = lax.div(j, 4), pl.ds(pl.multiple_of(lax.rem(j, 4) * 384, 128), 384)
-    y, z = lax.div(j, 2), pl.ds(lax.rem(j, 2) * 2, 2)
-    first = g_in[half, :, :, :, at].reshape(768, 384)
-    second = g_out[y, z].reshape(384, 768)
-    hidden = mm(sent[...], first)
-    value, slope = gelu_both(hidden)
-    act = value.astype(bf16)
-    result[...] += mm(act, second)
-    d_act = mm_nt(d_result[...], second)
-    d_hidden = (d_act * slope).astype(bf16)
-    h_out[y, z] = mm_tn(act, d_result[...]).astype(bf16).reshape(2, 2, 96, 768)
-    h_in[half, :, :, :, at] = mm(sent_t[...], d_hidden).astype(bf16).reshape(4, 4, 48, 384)
-    d_incoming[...] += mm_nt(d_hidden, first)
-
-
-def pair_backward(o, i, query, key, value, weights, d_heads, d_query, d_kv, d_kr, d_window, send, recv):
+def hidden_lanes(j):
+    return lax.div(j, 2), pl.ds(pl.multiple_of(lax.rem(j, 2) * 768, 128), 768)
+
+
+def expert_hidden(j, sent, g_in, acts, slopes):
+    half, at = hidden_lanes(j)
+    value, slope = gelu_both(mm(sent[...], g_in[half, :, :, :, at].reshape(768, 768)))
+    acts[j] = value.astype(bf16)
+    slopes[j] = slope.astype(bf16)
+
+
+def expert_second_grad(j, d_result, acts, h_out):
+    for r in (0, 1):
+        part = acts[j, :, r * 384 : (r + 1) * 384]
+        h_out[j, pl.ds(2 * r, 2)] = mm_tn(part, d_result[...]).astype(bf16).reshape(2, 2, 96, 768)
+
+
+def expert_result(j, acts, g_out, result):
+    result[...] += mm(acts[j], g_out[j].reshape(768, 768))
+
+
+def expert_back(j, sent_t, d_result, slopes, g_in, g_out, h_in, d_incoming):
+    half, at = hidden_lanes(j)
+    d_act = mm_nt(d_result[...], g_out[j].reshape(768, 768))
+    d_hidden = (d_act * slopes[j].astype(f32)).astype(bf16)
+    for r in (0, 1):
+        part = sent_t[r * 384 : (r + 1) * 384]
+        h_in[half, pl.ds(2 * r, 2), :, :, at] = mm(part, d_hidden).astype(bf16).reshape(2, 4, 48, 768)
+    d_incoming[...] += mm_nt(d_hidden, g_in[half, :, :, :, at].reshape(768, 768))
+
+
+def pair_backward(i, query, kv, weights, d_heads, d_query, d_kv, d_window):
     lanes = pl.ds(pl.multiple_of(i * 128, 128), 128)
-    probability = weights[pl.ds(2 * i, 2)].reshape(256, 512)
+    value_lanes = pl.ds(pl.multiple_of(i * 128 + 768, 128), 128)
+    kept = weights[pl.ds(2 * i, 2)].reshape(256, 512)
+    probability = kept.astype(f32)
     d_stack = stack_heads(d_heads[:, lanes])
-    d_weights = mm_nt(d_stack, value[:, lanes])
-    d_kv[:, 1, :, lanes] = (
-        mm_tn(probability.astype(bf16), d_stack).astype(bf16).reshape(4, 128, 128)
-    )
+    d_weights = mm_nt(d_stack, kv[:, value_lanes])
+    d_kv[:, value_lanes] = mm_tn(kept, d_stack).astype(bf16)
     d_scores = probability * (d_weights - jnp.sum(probability * d_weights, -1, keepdims=True))
     low = d_scores.astype(bf16)
-    d_kv[:, 0, :, lanes] = (
-        mm_tn(low, stack_heads(query[:, lanes])).astype(bf16).reshape(4, 128, 128)
-    )
-    for by in (1, 2, 3):
-        there = lax.rem(o.x + by, 4)
-        remote(
-            d_kv.at[there, :, :, lanes], d_kr.at[by - 1, :, :, lanes],
-            send.at[i, by - 1], recv.at[i, by - 1], o.along_x(by),
-        ).start()
-    d_query[:, lanes] = join_pair(mm(low, key[:, lanes])).astype(bf16)
+    d_kv[:, lanes] = mm_tn(low, stack_heads(query[:, lanes])).astype(bf16)
+    d_query[:, lanes] = join_pair(mm(low, kv[:, lanes])).astype(bf16)
     for j in (0, 1):
         d_window[pl.ds(2 * i + j, 1), :] = diagonal_sums(d_scores[j * 128 : (j + 1) * 128], 640)
-
-
-class Spread:
-    def __init__(self, place, ref, send, recv):
-        self.o, self.ref, self.send, self.recv = place, ref, send, recv
-
-    def view(self, by, low, count):
-        row = pl.multiple_of(lax.rem(self.o.x + by, 4) * 128, 128)
-        return self.ref.at[pl.ds(row, 128), pl.ds(low, count)]
-
-    def copy(self, n, by, low, count, to):
-        view = self.view(by, low, count)
-        return remote(view, view, self.send.at[n], self.recv.at[n], self.o.along_x(to))
-
-    def start(self, part):
-        self.copy(2 * part, 0, part * 768, 768, 1).start()
-        self.copy(2 * part + 1, 0, part * 768, 768, 3).start()
-
-    def forward(self):
-        self.copy(0, 3, 0, 768, 1).wait_recv()
-        self.copy(4, 3, 0, 768, 1).start()
-        self.copy(3, 1, 768, 768, 3).wait_recv()
-        self.copy(5, 1, 768, 768, 3).start()
-
-    def finish(self):
-        for n in (1, 2, 4, 5):
-            self.copy(n, 0, 0, 768, 1).wait_recv()
-
-    def drain(self):
-        for n in range(6):
-            self.copy(n, 0, 0, 768, 1).wait_send()
 
 
 def pair_forward(i, query, kv, window, heads_out, weights):
@@ -469,36 +460,44 @@
     top = jnp.max(scores, -1, keepdims=True)
     raised = jnp.exp(scores - top)
     probability = raised / jnp.sum(raised, -1, keepdims=True)
-    weights[pl.ds(2 * i, 2)] = probability.reshape(2, 128, 512)
-    heads_out[:, lanes] = join_pair(mm(probability.astype(bf16), kv[:, value_lanes])).astype(bf16)
+    low = probability.astype(bf16)
+    weights[pl.ds(2 * i, 2)] = low.reshape(2, 128, 512)
+    heads_out[:, lanes] = join_pair(mm(low, kv[:, value_lanes])).astype(bf16)
 
 
 def layer_kernel(
-    w_qkv, w_ao, w_in, w_out, pack, tokens, routes, buckets, cotangent,
-    mixed, d_tokens, out_qkv, out_ao, out_in, out_out, small,
-    stage, other, pair_sem, g_sends, g_recvs, side_in, side_arrivals, side_send, side_recv,
-    g_qkv, g_ao, g_in, g_out, normed_ref, query, kv, kv_send, kv_recv, window, weights, heads_out,
-    after_attn, moe_input, placing, probs, chosen, disp, inc, disp_send, disp_recv, sent, d_result,
-    h_qkv, h_ao, h_in, h_out, sent_t, result, d_incoming, ret, back, d_query, d_kv, d_kr, d_window,
-    d_heads_ref, d_after_ref, total_q, total_a, total_i, xs, xr, xa,
-    pair_q, pair_a, pair_i, pair_o, far_q, far_a, far_i, far_o, near_q, near_a, near_i, near_o,
+    w_qkv, w_ao, w_in, w_out, na, nm, router_t, table, tokens, routes, bucket_list, cotangent,
+    mixed, d_tokens, out_qkv, out_ao, out_in, out_out, own_small,
+    small, buckets, stage, other, pair_sem, g_sends, g_recvs, side_in, side_arrivals, side_send, side_recv,
+    g_qkv, g_ao, g_in, g_out, whole_tokens, tok_send, tok_recv, normed_ref, normed_t, query, kv, window, weights, heads_out,
+    after_attn, moe_input, placing, probs, chosen, disp, inc, disp_send, disp_recv, sent, d_result, acts, slopes,
+    h_qkv, h_ao, h_in, h_out, sent_t, result, back, d_kv, dn_in, d_window,
+    xs, xr, xa,
+    pair_a, pair_i, pair_o, far_q, far_a, far_i, far_o, near_q, near_a, near_i, near_o,
     side_q, side_a, side_i, side_o,
-    sends, recvs, ret_send, ret_recv, dk_send, dk_recv, x_send, x_recv, last_send, last_recv,
+    sends, recvs, ret_send, ret_recv, dn_send, dn_recv, x_send, x_recv, last_send, last_recv,
     arrivals, small_send, small_recv,
 ):
+    d_heads_ref, d_after_ref, d_query = heads_out, after_attn, query
     o = Place()
-    o.barrier(True)
+    entered = o.barrier(True)
     flows = [
         Gather(o, ref, tall, g_sends.at[i], g_recvs.at[i], i)
         for i, (ref, tall) in enumerate(((g_qkv, 0), (g_ao, 0), (g_in, 0), (g_out, 1)))
     ]
     qkv, ao, win, wout = flows
     pair_copy = meet(o, (w_qkv, w_ao, w_in), stage, other, pair_sem)
+    side = SmallSum(o, side_in, side_arrivals, side_send, side_recv, False)
+    place_small(o, side_in.at[0], na, nm, router_t, table)
+    buckets[...] = jnp.zeros_like(buckets)
+    buckets[:, 0:1023] = bucket_list[...]
+    g_out[o.y, o.z, o.c] = w_out[...]
+    own_rows = pl.ds(pl.multiple_of(o.x * 128, 128), 128)
+    whole_tokens[own_rows] = tokens[...]
+    entered()
     pair_copy.start()
-    side = SmallSum(o, side_in, side_arrivals, side_send, side_recv, False)
-    side_in[0] = place_small(o, pack)
     side.start(0)
-    g_out[o.y, o.z, o.c] = w_out[...]
+    wout.ring_one()
     pair_copy.wait_recv()
     at = 0
     for ref in (g_qkv, g_ao, g_in):
@@ -508,55 +507,72 @@
     qkv.ring_one()
     side.add(0)
     side.start(1)
+    ao.ring_one()
+    win.ring_one()
+    tok_copies = [
+        remote(
+            whole_tokens.at[own_rows], whole_tokens.at[own_rows], tok_send.at[by - 1], tok_recv.at[by - 1],
+            o.along_x(by),
+        )
+        for by in (1, 2, 3)
+    ]
+    for copy in tok_copies:
+        copy.start()
     qkv.ring_one_far()
     qkv.ring_two()
-    for f in (ao, win, wout):
-        f.ring_one()
+    for f in (wout, ao, win):
+        f.ring_one_far()
     side.add(1)
     side.start(2)
     x = tokens[...].astype(f32)
-    r_one = lax.rsqrt(jnp.mean(x * x, -1, keepdims=True) + epsilon)
     bucket_row = buckets[:, pl.ds(pl.multiple_of((3 - o.x) * 128, 128), 640)]
     picks = jnp.where(
         jnp.broadcast_to(bucket_row, (128, 640)) == lax.broadcasted_iota(jnp.int32, (128, 640), 0), 1.0, 0.0
     )
-    for f in (ao, win, wout):
-        f.ring_one_far()
     qkv.ring_two_far()
     for f in (ao, win, wout):
         f.ring_two()
+    for copy in tok_copies:
+        copy.wait_recv()
     side.add(2)
     small_in = side_in.at[3]
-    normed_ref[...] = (x * r_one * small_in[0:1, :768]).astype(bf16)
+    gain_row = small_in[0:1, :768]
+
+    def norm_rows(n, carry):
+        rows = pl.ds(n * 128, 128)
+        _, normed = rms_forward(whole_tokens[rows].astype(f32), gain_row)
+        normed_ref[rows] = normed.astype(bf16)
+        normed_t[:, rows] = normed.T.astype(bf16)
+        return carry
+
+    for n in range(4):
+        norm_rows(n, 0)
     table_t = jnp.concatenate([small_in[:, 768:896], small_in[:, 896:1024]], 0)
     window[...] = mm(table_t.astype(bf16), picks.astype(bf16))
     qkv.last()
     ao.ring_two_far()
     qkv.finish()
 
-    own_rows = pl.ds(pl.multiple_of(o.x * 128, 128), 128)
-    spread = Spread(o, kv, kv_send, kv_recv)
-    high = mm(normed_ref[...], g_qkv[1].reshape(768, 1152)).astype(bf16)
-    kv[own_rows, 384:1536] = high
-    spread.start(1)
-    low = mm(normed_ref[...], g_qkv[0].reshape(768, 1152)).astype(bf16)
-    kv[own_rows, 0:384] = low[:, 768:]
-    spread.start(0)
-    query[...] = low[:, :768]
+    query[...] = mm(normed_ref[own_rows], g_qkv[0, :, :, :, 0:768].reshape(768, 768)).astype(bf16)
+
+    def project_rows(n, carry):
+        rows = pl.ds(pl.multiple_of(n * 128, 128), 128)
+        block = normed_ref[rows]
+        kv[rows, 0:384] = mm(block, g_qkv[0, :, :, :, 768:1152].reshape(768, 384)).astype(bf16)
+        kv[rows, 384:1536] = mm(block, g_qkv[1].reshape(768, 1152)).astype(bf16)
+        return carry
+
+    lax.fori_loop(0, 4, project_rows, 0)
     ao.last()
-    win.ring_two_far()
-    spread.forward()
-    ao.finish()
-    spread.finish()
 
     def ahead(i, carry):
         pair_forward(i, query, kv, window, heads_out, weights)
         return carry
 
     lax.fori_loop(0, 3, ahead, 0)
-    win.last()
+    win.ring_two_far()
     lax.fori_loop(3, 6, ahead, 0)
-    wout.ring_two_far()
+    ao.finish()
     mixed_heads = heads_out[...]
     attn = x + jnp.concatenate([mm(mixed_heads, g_ao[h].reshape(768, 384)) for h in (0, 1)], 1)
     after_attn[...] = attn
@@ -570,79 +586,106 @@
     raised = jnp.exp(logits - jnp.max(logits, -1, keepdims=True))
     probability = raised / jnp.sum(raised, -1, keepdims=True)
     probs[...] = probability
-    picked = jnp.where(lane == routes[...] + 2, 1.0, 0.0)
+    named = jnp.broadcast_to(routes[...], (8, 128)) + 2
+    picked = jnp.where(lax.broadcasted_iota(jnp.int32, (8, 128), 0) == named, 1.0, 0.0).T
     chosen[...] = picked
     gate = jnp.sum(probability * picked, -1, keepdims=True)
     before = jnp.where(
         lax.broadcasted_iota(jnp.int32, (128, 128), 1) < lax.broadcasted_iota(jnp.int32, (128, 128), 0), 1.0, 0.0
     )
     slot = jnp.sum(mm(before.astype(bf16), picked.astype(bf16)) * picked, -1, keepdims=True)
-    column = routes[...].astype(f32) * 48.0 + slot
+    column = jnp.sum(picked * ((lane - 2) * 48).astype(f32), -1, keepdims=True) + slot
     place = jnp.where(
         lax.broadcasted_iota(jnp.int32, (128, 192), 1).astype(f32) == column, 1.0, 0.0
     ).astype(bf16)
     placing[...] = place
-    disp[:, 0] = mm_tn(place, moe_low).astype(bf16).reshape(4, 48, 768)
-    d_combined = (gate * cotangent[...].astype(f32)).astype(bf16)
-    disp[:, 1] = mm_tn(place, d_combined).astype(bf16).reshape(4, 48, 768)
-    disp_copies = [
-        remote(
-            disp.at[lax.rem(o.x + by, 4)], inc.at[o.x], disp_send.at[by - 1], disp_recv.at[by - 1],
-            o.along_x(by),
-        )
-        for by in (1, 2, 3)
-    ]
-    for copy in disp_copies:
-        copy.start()
-    inc[o.x] = disp[o.x]
+    def dispatch(part, value):
+        disp[part] = mm_tn(place, value).astype(bf16).reshape(4, 48, 768)
+        copies = [
+            remote(
+                disp.at[part, lax.rem(o.x + by, 4)], inc.at[part, o.x],
+                disp_send.at[part, by - 1], disp_recv.at[part, by - 1], o.along_x(by),
+            )
+            for by in (1, 2, 3)
+        ]
+        for copy in copies:
+            copy.start()
+        inc[part, o.x] = disp[part, o.x]
+        return copies
+
+    tokens_out = dispatch(0, moe_low)
+    grads_out = dispatch(1, (gate * cotangent[...].astype(f32)).astype(bf16))
+    win.last()
+    wout.ring_two_far()
+    for copy in tokens_out:
+        copy.wait_recv()
+    sent[...] = inc[0].reshape(192, 768)
+    sent_t[...] = sent[...].astype(f32).T.astype(bf16)
     win.finish()
-    wout.last()
-    for copy in disp_copies:
-        copy.wait_recv()
-    sent[...] = inc[:, 0].reshape(192, 768)
-    d_result[...] = inc[:, 1].reshape(192, 768)
-    wout.finish()
-
+    pair_q = pair_i.at[:, :, :, pl.ds(0, 1152)]
     fq = Scatter(o, h_qkv, 0, pair_q, far_q, near_q, side_q, sends.at[0], recvs.at[0])
     fa = Scatter(o, h_ao, 0, pair_a, far_a, near_a, side_a, sends.at[1], recvs.at[1])
     fi = Scatter(o, h_in, 0, pair_i, far_i, near_i, side_i, sends.at[2], recvs.at[2])
     fo = Scatter(o, h_out, 1, pair_o, far_o, near_o, side_o, sends.at[3], recvs.at[3])
     tot = SmallSum(o, small, arrivals, small_send, small_recv, True)
 
-    sent_t[...] = sent[...].astype(f32).T.astype(bf16)
+    def times(low, high, body):
+        def step(j, carry):
+            body(j)
+            return carry
+
+        lax.fori_loop(low, high, step, 0)
+
+    times(0, 4, lambda j: expert_hidden(j, sent, g_in, acts, slopes))
+    wout.last()
+    for copy in grads_out:
+        copy.wait_recv()
+    d_result[...] = inc[1].reshape(192, 768)
+    times(0, 4, lambda j: expert_second_grad(j, d_result, acts, h_out))
+    fo.to_pair(0, 0, 4)
+    wout.finish()
     result[...] = jnp.zeros_like(result)
+    times(0, 4, lambda j: expert_result(j, acts, g_out, result))
+
+    def send_back(part, value):
+        for copy in (tokens_out, grads_out)[part]:
+            copy.wait_send()
+        ret = disp
+        ret[part] = value.astype(bf16).reshape(4, 48, 768)
+        copies = [
+            remote(
+                ret.at[part, lax.rem(o.x + by, 4)], back.at[part, o.x],
+                ret_send.at[part, by - 1], ret_recv.at[part, by - 1], o.along_x(by),
+            )
+            for by in (1, 2, 3)
+        ]
+        for copy in copies:
+            copy.start()
+        back[part, o.x] = ret[part, o.x]
+        return copies
+
+    results_back = send_back(0, result[...])
+    fo.from_pair(0, 4)
+    fo.ring()
+    d_incoming = result
     d_incoming[...] = jnp.zeros_like(d_incoming)
-
-    def chunk(j, carry):
-        expert_chunk(j, sent, sent_t, d_result, g_in, g_out, h_in, h_out, result, d_incoming)
-        return carry
-
-    start = 4 * (1 - o.c)
-    lax.fori_loop(start, start + 4, chunk, 0)
+    start = 2 * (1 - o.c)
+
+    def back_chunk(j):
+        expert_back(j, sent_t, d_result, slopes, g_in, g_out, h_in, d_incoming)
+
+    times(start, start + 2, back_chunk)
     fi.to_pair(0, 0, 4)
-    fo.to_pair(0, 2 * (1 - o.c), 2)
-    lax.fori_loop(4 - start, 8 - start, chunk, 0)
-    fo.to_pair(1, 2 * o.c, 2)
-    ret[:, 0] = result[...].astype(bf16).reshape(4, 48, 768)
-    ret[:, 1] = d_incoming[...].astype(bf16).reshape(4, 48, 768)
-    ret_copies = [
-        remote(
-            ret.at[lax.rem(o.x + by, 4)], back.at[o.x], ret_send.at[by - 1], ret_recv.at[by - 1],
-            o.along_x(by),
-        )
-        for by in (1, 2, 3)
-    ]
-    for copy in ret_copies:
-        copy.start()
-    back[o.x] = ret[o.x]
+    times(2 - start, 4 - start, back_chunk)
+    grads_back = send_back(1, d_incoming[...])
     fi.from_pair(0, 4)
     fi.ring()
-    for copy in ret_copies:
+    for copy in results_back + grads_back:
         copy.wait_recv()
 
     gain_one, gain_two = small8[0:1], small8[1:2]
-    returned = mm(placing[...], back[:, 0].reshape(192, 768))
-    d_moe = mm(placing[...], back[:, 1].reshape(192, 768))
+    returned = mm(placing[...], back[0].reshape(192, 768))
+    d_moe = mm(placing[...], back[1].reshape(192, 768))
     attn = after_attn[...]
     r_two = lax.rsqrt(jnp.mean(attn * attn, -1, keepdims=True) + epsilon)
     upstream = cotangent[...].astype(f32)
@@ -665,64 +708,83 @@
         d_heads = d_heads + mm_nt(part, g_ao[h].reshape(768, 384))
     fa.to_pair(0, 0, 4)
     d_heads_ref[...] = d_heads.astype(bf16)
-    fo.from_pair(0, 2)
-    fo.from_pair(1, 2)
-    fo.ring()
+    fo.ring_far()
 
     d_window[...] = jnp.zeros_like(d_window)
-    key, value = kv.at[:, pl.ds(0, 768)], kv.at[:, pl.ds(768, 768)]
-
-    def pair(i, carry):
-        pair_backward(
-            o, i, query, key, value, weights, d_heads_ref, d_query, d_kv, d_kr, d_window, dk_send, dk_recv
-        )
-        return carry
-
-    lax.fori_loop(0, 2, pair, 0)
-    fi.ring_far()
+
+    def pair(i):
+        pair_backward(i, query, kv, weights, d_heads_ref, d_query, d_kv, d_window)
+
+    times(0, 2, pair)
     fa.from_pair(0, 4)
     fa.ring()
-    lax.fori_loop(2, 4, pair, 0)
-    fo.ring_far()
-    fi.across()
-    lax.fori_loop(4, 6, pair, 0)
+    times(2, 4, pair)
+    fi.ring_far()
+    fo.across()
+    times(4, 6, pair)
     fa.ring_far()
-
-    x = tokens[...].astype(f32)
-    normed_t = normed_ref[...].astype(f32).T.astype(bf16)
-
-    def project(h, d_part):
-        h_qkv[h] = mm(normed_t, d_part).astype(bf16).reshape(4, 4, 48, 1152)
-        return mm_nt(d_part, g_qkv[h].reshape(768, 1152))
-
+    def lanes_of(n):
+        return pl.ds(pl.multiple_of(n * 384, 128), 384)
+
+    def query_grad(n):
+        h_qkv[0, :, :, :, lanes_of(n)] = (
+            mm(normed_t[:, own_rows], d_query[:, lanes_of(n)]).astype(bf16).reshape(4, 4, 48, 384)
+        )
+
+    def key_value_grad(n):
+        h_qkv[1, :, :, :, lanes_of(n)] = (
+            mm(normed_t[...], d_kv[:, lanes_of(n + 1)]).astype(bf16).reshape(4, 4, 48, 384)
+        )
+
+    times(0, 2, query_grad)
+    h_qkv[0, :, :, :, 768:1152] = mm(normed_t[...], d_kv[:, 0:384]).astype(bf16).reshape(4, 4, 48, 384)
+    times(0, 3, key_value_grad)
+    fq.to_pair(0, 0, 4)
     grad_table = lax.dot_general(
         d_window[...], picks, NT, precision=highest, preferred_element_type=f32
     )
-    fo.across()
-    for i in range(6):
-        for by in (1, 2, 3):
-            view = d_kr.at[by - 1, :, :, pl.ds(0, 128)]
-            remote(view, view, dk_send.at[i, by - 1], dk_recv.at[i, by - 1], o.sibling()).wait_recv()
-    d_own = d_kv[o.x].astype(f32)
-    for by in (0, 1, 2):
-        d_own = d_own + d_kr[by].astype(f32)
-    d_own = d_own.astype(bf16)
-    d_key, d_value = d_own[0], d_own[1]
+    dn = acts.at[:, pl.ds(0, 128), :]
+
+    result[0:8] = jnp.zeros((8, 768), f32)
+
+    def back_rows(n):
+        rows = pl.ds(n * 128, 128)
+        part = mm_nt(d_kv[rows, 0:384], g_qkv[0, :, :, :, 768:1152].reshape(768, 384))
+        part = part + mm_nt(d_kv[rows, 384:1536], g_qkv[1].reshape(768, 1152))
+        dn[n] = part.astype(bf16)
+        block = whole_tokens[rows].astype(f32)
+        r = lax.rsqrt(jnp.mean(block * block, -1, keepdims=True) + epsilon)
+        result[0:1] += jnp.sum(part * block * r, 0, keepdims=True)
+
+    for n in range(4):
+        back_rows(n)
+    dn_copies = [
+        remote(dn.at[lax.rem(o.x + by, 4)], dn_in.at[by - 1], dn_send.at[by - 1], dn_recv.at[by - 1], o.along_x(by))
+        for by in (1, 2, 3)
+    ]
+    for copy in dn_copies:
+        copy.start()
+    d_own = mm_nt(d_query[...], g_qkv[0, :, :, :, 0:768].reshape(768, 768))
     r_one = lax.rsqrt(jnp.mean(x * x, -1, keepdims=True) + epsilon)
-    d_normed = project(0, jnp.concatenate([d_query[...], d_key[:, :384]], 1))
-    d_normed = d_normed + project(1, jnp.concatenate([d_key[:, 384:], d_value], 1))
-    fq.to_pair(0, 0, 4)
-    d_resid, grad_norm_one = rms_backward(x, r_one, gain_one, d_normed)
-    d_tokens[...] = (d_after_ref[...] + d_resid).astype(bf16)
+    grad_norm_one = result[0:1] + jnp.sum(d_own * x * r_one, 0, keepdims=True)
+    fi.across()
+    fa.across()
     row = lax.broadcasted_iota(jnp.int32, (8, 768), 0)
-    top = jnp.where(row == 0, grad_norm_one[None, :], jnp.where(row == 1, grad_norm_two[None, :], grad_router))
+    top = jnp.where(row == 0, grad_norm_one, jnp.where(row == 1, grad_norm_two[None, :], grad_router))
     small[0] = jnp.concatenate([top, grad_table[0:8], grad_table[8:16]], 1)
     tot.start(0)
-    fa.across()
     fq.from_pair(0, 4)
     fq.ring()
     tot.add(0)
     tot.start(1)
+    for copy in dn_copies:
+        copy.wait_recv()
+    d_normed = d_own + dn[o.x].astype(f32)
+    for by in (0, 1, 2):
+        d_normed = d_normed + dn_in[by].astype(f32)
+    d_resid, _ = rms_backward(x, r_one, gain_one, d_normed)
+    d_tokens[...] = (d_after_ref[...] + d_resid).astype(bf16)
+    total_q, total_a, total_i = (stage.at[:, pl.ds(a, n)] for a, n in ((0, 1152), (1152, 384), (1536, 1536)))
     out_out[...] = fo.total()
 
     def hand(k, total, out, value):
@@ -771,23 +833,24 @@
     last.append(hand(1, total_q, out_qkv, whole[:, :1152]))
     last.append(hand(2, total_a, out_ao, whole[:, 1152:]))
     tot.add(3)
+    take = lax.broadcasted_iota(jnp.int32, (768, 128), 0) == lax.broadcasted_iota(jnp.int32, (768, 128), 1) + 24 * o.d
+    own_small[:, 0:128] = jnp.dot(
+        small[4, :, 0:768], jnp.where(take, 1.0, 0.0), precision=highest, preferred_element_type=f32
+    )
+    heads_of = jnp.concatenate([small[4, :, 768:896], small[4, :, 896:1024]], 0)
+    mine = jnp.where(lax.broadcasted_iota(jnp.int32, (16, 128), 1) == o.d, heads_of, 0.0)
+    column = jnp.broadcast_to(jnp.sum(mine, -1, keepdims=True), (16, 128))
+    same = lax.broadcasted_iota(jnp.int32, (16, 128), 0) == lax.broadcasted_iota(jnp.int32, (16, 128), 1)
+    own_small[0:1, 128:256] = jnp.sum(jnp.where(same, column, 0.0), 0, keepdims=True)
     for copy in last:
         copy.wait_recv()
-    for copy in ret_copies + first + second + last:
+    for copy in results_back + grads_back + dn_copies + tok_copies + first + second + last:
         copy.wait_send()
-    for i in range(6):
-        for by in (1, 2, 3):
-            view = d_kr.at[by - 1, :, :, pl.ds(0, 128)]
-            remote(view, view, dk_send.at[i, by - 1], dk_recv.at[i, by - 1], o.sibling()).wait_send()
     tot.drain()
-    for f in (fq, fa, fi):
+    for f in (fq, fa, fi, fo):
         f.drain([(0, 4)])
-    fo.drain([(0, 2), (1, 2)])
     pair_copy.wait_send()
     side.drain()
-    spread.drain()
-    for copy in disp_copies:
-        copy.wait_send()
     for f in flows:
         f.drain()
 
@@ -815,59 +878,72 @@
             jax.ShapeDtypeStruct((24, 768), f32),
             jax.ShapeDtypeStruct((24, 3072), f32),
             jax.ShapeDtypeStruct((96, 768), f32),
-            jax.ShapeDtypeStruct((5, 8, 1024), f32),
+            jax.ShapeDtypeStruct((8, 256), f32),
         ],
         scratch_shapes=[
-            full(48, 3072), full(24, 3072), dma((2,)), dma((4, 11)), dma((4, 11)),
+            full(5, 8, 1024), pltpu.VMEM((1, 1024), jnp.int32), full(48, 3072), full(24, 3072), dma((2,)), dma((4, 11)), dma((4, 11)),
             full(4, 8, 1024), full(7, 8, 1024), dma((7,)), dma((7,)),
-            *weights, low(128, 768), low(128, 768), low(512, 1536), dma((6,)), dma((6,)), full(16, 640),
-            full(12, 128, 512), low(128, 768), full(128, 768), low(128, 768), low(128, 192),
-            full(128, 8), full(128, 8), low(4, 2, 48, 768), low(4, 2, 48, 768), dma((3,)), dma((3,)),
-            low(192, 768), low(192, 768),
+            *weights, low(512, 768), dma((3,)), dma((3,)), low(512, 768), low(768, 512), low(128, 768), low(512, 1536), full(16, 640),
+            low(12, 128, 512), low(128, 768), full(128, 768), low(128, 768), low(128, 192),
+            full(128, 8), full(128, 8), low(2, 4, 48, 768), low(2, 4, 48, 768), dma((2, 3)), dma((2, 3)),
+            low(192, 768), low(192, 768), low(4, 192, 768), low(4, 192, 768),
             *weights,
-            low(768, 192), full(192, 768), full(192, 768), low(4, 2, 48, 768), low(4, 2, 48, 768),
-            low(128, 768), low(4, 2, 128, 768), low(3, 2, 128, 768), full(16, 640),
-            low(128, 768), full(128, 768), full(48, 1152), full(48, 384), full(48, 1536),
+            low(768, 192), full(192, 768), low(2, 4, 48, 768),
+            low(512, 1536), low(3, 128, 768), full(16, 640),
             low(4, 48, 384), low(3, 48, 384), low(4, 48, 384),
-            *[low(4, 4, *s) for s in sizes],
+            *[low(4, 4, *s) for s in sizes[1:]],
             *[low(2, 2, *s) for s in sizes],
             *[low(2, 4, *s) for s in sizes],
             *[low(3, *s) for s in sizes],
-            dma((4, 11)), dma((4, 11)), dma((3,)), dma((3,)), dma((6, 3)), dma((6, 3)),
+            dma((4, 11)), dma((4, 11)), dma((2, 3)), dma((2, 3)), dma((3,)), dma((3,)),
             dma((6,)), dma((6,)), dma((3,)), dma((3,)),
             full(10, 8, 1024), dma((10,)), dma((10,)),
         ],
         compiler_params=pltpu.CompilerParams(
-            collective_id=0, has_side_effects=True, vmem_limit_bytes=62 * 2**20
+            collective_id=0, has_side_effects=True, vmem_limit_bytes=63 * 2**20
         ),
     )(*operands)
+
+
+def emit_kernel(
+    mixed, d_tokens, qkv, ao, first, second, own,
+    o_mixed, o_tokens, o_na, o_qkv, o_ao, o_table, o_nm, o_router, o_first, o_second,
+):
+    o_mixed[...] = mixed[...]
+    o_tokens[...] = d_tokens[...]
+    o_qkv[...] = qkv[...]
+    o_ao[...] = ao[...]
+    o_first[:, 0, :] = first[...]
+    o_second[:, 0, :] = second[...]
+    o_na[...] = own[0:1, 0:24]
+    o_nm[...] = own[1:2, 0:24]
+    o_router[...] = own[2:6, 0:24]
+    o_table[...] = own[0:1, 128:140]
+
+
+def emit(*results):
+    vm = pl.BlockSpec(memory_space=pltpu.VMEM)
+    kinds = (
+        ((128, 768), bf16), ((128, 768), bf16), ((1, 24), f32), ((24, 2304), f32), ((24, 768), f32),
+        ((1, 12), f32), ((1, 24), f32), ((4, 24), f32), ((24, 1, 3072), f32), ((96, 1, 768), f32),
+    )
+    return pl.pallas_call(
+        emit_kernel,
+        in_specs=[vm] * 7,
+        out_specs=[vm] * 10,
+        out_shape=[jax.ShapeDtypeStruct(shape, kind) for shape, kind in kinds],
+    )(*results)
 
 
 def per_device(
     tokens, norm_attn, w_qkv, w_attn_out, bias_table, norm_moe, router, w_in, w_out, routes, buckets, cotangent
 ):
-    dp = lax.axis_index("dp")
-    own = norm_attn.shape[0]
-    pack = jnp.concatenate([norm_attn[:, None], norm_moe[:, None], router, jnp.zeros((own, 122), bf16)], 1)
-    last = jnp.concatenate([jnp.zeros((1, 8), bf16), bias_table, jnp.zeros((1, 108), bf16)], 1)
-    pack = jnp.concatenate([pack, last, jnp.zeros((7, 128), bf16)], 0)
-    padded = jnp.concatenate([buckets, jnp.zeros((1,), jnp.int32)])[None, :]
-    mixed, d_tokens, out_qkv, out_ao, out_in, out_out, small = layer(
-        w_qkv, w_attn_out, w_in[:, 0], w_out[:, 0], pack, tokens, routes, padded, cotangent
-    )
-    small = small[4]
-    mine = lax.dynamic_slice(small, (0, dp * own), (8, own))
-    table_col = jnp.concatenate(
-        [
-            lax.dynamic_slice(small, (0, 768 + dp), (8, 1)),
-            lax.dynamic_slice(small, (0, 896 + dp), (4, 1)),
-        ],
-        0,
-    )
-    return (
-        mixed, d_tokens, mine[0], out_qkv, out_ao, table_col.T, mine[1], mine[2:6].T,
-        out_in[:, None], out_out[:, None],
-    )
+    results = layer(
+        w_qkv, w_attn_out, w_in[:, 0], w_out[:, 0], norm_attn[None, :], norm_moe[None, :], router.T, bias_table,
+        tokens, routes.T, buckets[None, :], cotangent,
+    )
+    mixed, d_tokens, g_na, g_qkv, g_ao, g_table, g_nm, g_router, g_in, g_out = emit(*results)
+    return mixed, d_tokens, g_na[0], g_qkv, g_ao, g_table, g_nm[0], g_router.T, g_in, g_out
 
 
 def solution(mesh):

time: 168 us -> 139 us (0.83)
  Pallas kernels: 150 us -> 136 us
  local copies, waits for them, and re-layouts: 13.2 us -> 0 us
  other arithmetic: 1.94 us -> 0 us
    pallas_call x1, Pallas kernels: 150 us -> 134 us  [layer(): pl.pallas_call(layer_kernel, in_specs=[vm] * len(operands), out_specs=[vm...]
    unnamed x30 -> x0, local copies, waits for them, and re-layouts: 10.6 us -> none
    pallas_call x0 -> x1, Pallas kernels: none -> 2.4 us  [emit(): pl.pallas_call(emit_kernel, in_specs=[vm] * 7, out_specs=[vm] * 10, out_s...]
where the time goes in v4:
time: 139 us; the launch traced here: 137 us
  Pallas kernels  136 us (98%)
    pallas_call x1, Pallas kernels, layer(): pl.pallas_call(layer_kernel, in_specs=[vm] * len(operands), out_specs=[vm...  134 us

profile of v4, /device:TPU:0, one launch (start us, length us, event | category | flops | bytes accessed | tf_op | source)
XLA Modules:
  0.0 137.2 jit_solution(13992754254783589091)
XLA Ops:
  0.6 134.1 %shard_map.195 = (bf16[128,768]{1,0:T(8,128)(2,1)}, bf16[128,768]{1,0:T(8,128)(2,1)}, f32[24,2304]{1,0:T(8,128)}, f32[24,768]{1,0:T(8,128)}, f32[24,3072]{1,0:T(...) custom-call(bf16[24,2304]{1,0:T(8,128)(2,1)} %w_qkv.1, bf16[24,768]{1,0:T(8,128)(2,1)} %w_ao.1, bf16[24,3072]{1,0:T(8,128)(2,1)} %bitcast.10, ...), custom_call_target="tpu_custom_call" | custom-call | tf_op jit(solution)/shard_map/pallas_call | solution.py:870
  134.8 2.4 %shard_map.196 = (bf16[128,768]{1,0:T(8,128)(2,1)}, bf16[128,768]{1,0:T(8,128)(2,1)}, f32[1,24]{1,0:T(1,128)}, f32[24,2304]{1,0:T(8,128)}, f32[24,768]{1,0:T(8,1...) custom-call(bf16[128,768]{1,0:T(8,128)(2,1)} %get-tuple-element.27.m, ...), custom_call_target="tpu_custom_call" | custom-call | tf_op jit(solution)/shard_map/pallas_call | solution.py:930

commit v5 on v4

--- a/solution.py
+++ b/solution.py
@@ -182,10 +182,15 @@
         else:
             self.go(lambda k: self.block(k, 1), 2, 2, self.o.along_p(3))
 
+    def ring_two_block(self, by):
+        n = 3 if by == 0 else 9 + 2 * by
+        self.go(lambda k: self.block(k, by), n, 3, self.o.along_q(1))
+        self.go(lambda k: self.block(k, by), 4 if by == 0 else n + 1, 4, self.o.along_q(3))
+
     def ring_two(self):
         self.arrived(2, 1)
-        self.go(lambda k: self.slab(k, 0), 3, 3, self.o.along_q(1))
-        self.go(lambda k: self.slab(k, 0), 4, 4, self.o.along_q(3))
+        for by in (1, 2, 3):
+            self.ring_two_block(by)
         self.go(lambda k: self.slab(k, 0), 7, 7, self.o.sibling())
 
     def ring_two_far(self):
@@ -206,7 +211,8 @@
             self.arrived(r, 4)
 
     def drain(self):
-        for s, count in ((0, 1), (1, 1), (2, 1), (3, 4), (4, 4), (5, 2), (6, 2), (7, 4), (8, 4), (9, 4), (10, 4)):
+        for s, count in ((0, 1), (1, 1), (2, 1), (3, 1), (4, 1), (5, 2), (6, 2), (7, 4), (8, 4), (9, 4), (10, 4),
+                         *((n, 1) for n in range(11, 17))):
             self.sent(s, count)
 
 
@@ -265,13 +271,14 @@
 
 def meet(o, halves, stage, other, sem):
     at = 0
-    for ref in halves:
-        n = ref.shape[1] // 2
-        own = pl.ds(pl.multiple_of(o.c * n, 128), n)
-        theirs = pl.ds(pl.multiple_of((1 - o.c) * n, 128), n)
-        stage[pl.ds(pl.multiple_of(24 * o.c, 8), 24), at : at + n] = ref[:, own].astype(f32)
-        other[:, at : at + n] = ref[:, theirs].astype(f32)
-        at += n
+    for ref, blocks in halves:
+        n = ref.shape[1] // (2 * blocks)
+        for t in range(blocks):
+            own = pl.ds(pl.multiple_of(o.c * n + 2 * t * n, 128), n)
+            theirs = pl.ds(pl.multiple_of((1 - o.c) * n + 2 * t * n, 128), n)
+            stage[pl.ds(pl.multiple_of(24 * o.c, 8), 24), at : at + n] = ref[:, own].astype(f32)
+            other[:, at : at + n] = ref[:, theirs].astype(f32)
+            at += n
     return remote(
         other, stage.at[pl.ds(pl.multiple_of(24 * o.c, 8), 24)], sem.at[0], sem.at[1], o.sibling()
     )
@@ -486,7 +493,7 @@
         for i, (ref, tall) in enumerate(((g_qkv, 0), (g_ao, 0), (g_in, 0), (g_out, 1)))
     ]
     qkv, ao, win, wout = flows
-    pair_copy = meet(o, (w_qkv, w_ao, w_in), stage, other, pair_sem)
+    pair_copy = meet(o, ((w_qkv, 3), (w_ao, 1), (w_in, 1)), stage, other, pair_sem)
     side = SmallSum(o, side_in, side_arrivals, side_send, side_recv, False)
     place_small(o, side_in.at[0], na, nm, router_t, table)
     buckets[...] = jnp.zeros_like(buckets)
@@ -498,6 +505,7 @@
     pair_copy.start()
     side.start(0)
     wout.ring_one()
+    wout.ring_two_block(0)
     pair_copy.wait_recv()
     at = 0
     for ref in (g_qkv, g_ao, g_in):
@@ -505,10 +513,9 @@
         ref[o.c, o.y, o.z] = stage[:, at : at + n].astype(bf16)
         at += n
     qkv.ring_one()
+    qkv.ring_two_block(0)
     side.add(0)
     side.start(1)
-    ao.ring_one()
-    win.ring_one()
     tok_copies = [
         remote(
             whole_tokens.at[own_rows], whole_tokens.at[own_rows], tok_send.at[by - 1], tok_recv.at[by - 1],
@@ -518,10 +525,12 @@
     ]
     for copy in tok_copies:
         copy.start()
+    win.ring_one()
+    ao.ring_one()
+    ao.ring_two_block(0)
+    win.ring_two_block(0)
     qkv.ring_one_far()
     qkv.ring_two()
-    for f in (wout, ao, win):
-        f.ring_one_far()
     side.add(1)
     side.start(2)
     x = tokens[...].astype(f32)
@@ -529,9 +538,12 @@
     picks = jnp.where(
         jnp.broadcast_to(bucket_row, (128, 640)) == lax.broadcasted_iota(jnp.int32, (128, 640), 0), 1.0, 0.0
     )
+    for f in (wout, win, ao):
+        f.ring_one_far()
+    ao.ring_two()
+    win.ring_two()
     qkv.ring_two_far()
-    for f in (ao, win, wout):
-        f.ring_two()
+    wout.ring_two()
     for copy in tok_copies:
         copy.wait_recv()
     side.add(2)
@@ -553,13 +565,17 @@
     ao.ring_two_far()
     qkv.finish()
 
-    query[...] = mm(normed_ref[own_rows], g_qkv[0, :, :, :, 0:768].reshape(768, 768)).astype(bf16)
+    for h in (0, 1):
+        query[:, 384 * h : 384 * h + 384] = mm(
+            normed_ref[own_rows], g_qkv[h, :, :, :, 0:384].reshape(768, 384)
+        ).astype(bf16)
 
     def project_rows(n, carry):
         rows = pl.ds(pl.multiple_of(n * 128, 128), 128)
-        block = normed_ref[rows]
-        kv[rows, 0:384] = mm(block, g_qkv[0, :, :, :, 768:1152].reshape(768, 384)).astype(bf16)
-        kv[rows, 384:1536] = mm(block, g_qkv[1].reshape(768, 1152)).astype(bf16)
+        for h in (0, 1):
+            both = mm(normed_ref[rows], g_qkv[h, :, :, :, 384:1152].reshape(768, 768)).astype(bf16)
+            kv[rows, 384 * h : 384 * h + 384] = both[:, :384]
+            kv[rows, 768 + 384 * h : 1152 + 384 * h] = both[:, 384:]
         return carry
 
     lax.fori_loop(0, 4, project_rows, 0)
@@ -644,6 +660,8 @@
     times(0, 4, lambda j: expert_second_grad(j, d_result, acts, h_out))
     fo.to_pair(0, 0, 4)
     wout.finish()
+    fo.from_pair(0, 4)
+    fo.ring()
     result[...] = jnp.zeros_like(result)
     times(0, 4, lambda j: expert_result(j, acts, g_out, result))
 
@@ -665,8 +683,6 @@
         return copies
 
     results_back = send_back(0, result[...])
-    fo.from_pair(0, 4)
-    fo.ring()
     d_incoming = result
     d_incoming[...] = jnp.zeros_like(d_incoming)
     start = 2 * (1 - o.c)
@@ -715,68 +731,99 @@
     def pair(i):
         pair_backward(i, query, kv, weights, d_heads_ref, d_query, d_kv, d_window)
 
-    times(0, 2, pair)
+    def lanes_of(h, base):
+        return pl.ds(pl.multiple_of(h * 384 + base, 128), 384)
+
+    def dense_grad(h):
+        for t, part in enumerate(
+            (
+                mm(normed_t[:, own_rows], d_query[:, lanes_of(h, 0)]),
+                mm(normed_t[...], d_kv[:, lanes_of(h, 0)]),
+                mm(normed_t[...], d_kv[:, lanes_of(h, 768)]),
+            )
+        ):
+            h_qkv[h, :, :, :, t * 384 : t * 384 + 384] = part.astype(bf16).reshape(4, 4, 48, 384)
+
+    theirs = 1 - o.c
+    times(3 * theirs, 3 * theirs + 3, pair)
+    dense_grad(theirs)
     fa.from_pair(0, 4)
+    fq.to_pair(0, 0, 4)
     fa.ring()
-    times(2, 4, pair)
     fi.ring_far()
+    times(3 * o.c, 3 * o.c + 3, pair)
+    dense_grad(o.c)
     fo.across()
-    times(4, 6, pair)
     fa.ring_far()
-    def lanes_of(n):
-        return pl.ds(pl.multiple_of(n * 384, 128), 384)
-
-    def query_grad(n):
-        h_qkv[0, :, :, :, lanes_of(n)] = (
-            mm(normed_t[:, own_rows], d_query[:, lanes_of(n)]).astype(bf16).reshape(4, 4, 48, 384)
-        )
-
-    def key_value_grad(n):
-        h_qkv[1, :, :, :, lanes_of(n)] = (
-            mm(normed_t[...], d_kv[:, lanes_of(n + 1)]).astype(bf16).reshape(4, 4, 48, 384)
-        )
-
-    times(0, 2, query_grad)
-    h_qkv[0, :, :, :, 768:1152] = mm(normed_t[...], d_kv[:, 0:384]).astype(bf16).reshape(4, 4, 48, 384)
-    times(0, 3, key_value_grad)
-    fq.to_pair(0, 0, 4)
+    fq.from_pair(0, 4)
+    fq.ring()
+    fi.across()
+    fa.across()
     grad_table = lax.dot_general(
         d_window[...], picks, NT, precision=highest, preferred_element_type=f32
     )
+    result[0:8] = jnp.zeros((8, 768), f32)
     dn = acts.at[:, pl.ds(0, 128), :]
 
-    result[0:8] = jnp.zeros((8, 768), f32)
-
-    def back_rows(n):
+    for n in range(4):
         rows = pl.ds(n * 128, 128)
-        part = mm_nt(d_kv[rows, 0:384], g_qkv[0, :, :, :, 768:1152].reshape(768, 384))
-        part = part + mm_nt(d_kv[rows, 384:1536], g_qkv[1].reshape(768, 1152))
+        part = jnp.zeros((128, 768), f32)
+        for h in (0, 1):
+            part = part + mm_nt(
+                d_kv[rows, 384 * h : 384 * h + 384], g_qkv[h, :, :, :, 384:768].reshape(768, 384)
+            )
+            part = part + mm_nt(
+                d_kv[rows, 768 + 384 * h : 1152 + 384 * h], g_qkv[h, :, :, :, 768:1152].reshape(768, 384)
+            )
         dn[n] = part.astype(bf16)
         block = whole_tokens[rows].astype(f32)
         r = lax.rsqrt(jnp.mean(block * block, -1, keepdims=True) + epsilon)
         result[0:1] += jnp.sum(part * block * r, 0, keepdims=True)
 
-    for n in range(4):
-        back_rows(n)
     dn_copies = [
         remote(dn.at[lax.rem(o.x + by, 4)], dn_in.at[by - 1], dn_send.at[by - 1], dn_recv.at[by - 1], o.along_x(by))
         for by in (1, 2, 3)
     ]
     for copy in dn_copies:
         copy.start()
-    d_own = mm_nt(d_query[...], g_qkv[0, :, :, :, 0:768].reshape(768, 768))
+    d_own = jnp.zeros((128, 768), f32)
+    for h in (0, 1):
+        d_own = d_own + mm_nt(
+            d_query[:, 384 * h : 384 * h + 384], g_qkv[h, :, :, :, 0:384].reshape(768, 384)
+        )
     r_one = lax.rsqrt(jnp.mean(x * x, -1, keepdims=True) + epsilon)
     grad_norm_one = result[0:1] + jnp.sum(d_own * x * r_one, 0, keepdims=True)
-    fi.across()
-    fa.across()
     row = lax.broadcasted_iota(jnp.int32, (8, 768), 0)
     top = jnp.where(row == 0, grad_norm_one, jnp.where(row == 1, grad_norm_two[None, :], grad_router))
     small[0] = jnp.concatenate([top, grad_table[0:8], grad_table[8:16]], 1)
     tot.start(0)
-    fq.from_pair(0, 4)
-    fq.ring()
+    fq.ring_far()
     tot.add(0)
     tot.start(1)
+    total_q, total_a, total_i = (stage.at[:, pl.ds(a, n)] for a, n in ((0, 1152), (1152, 384), (1536, 1536)))
+    out_out[...] = fo.total()
+
+    def hand(k, total, out, value, blocks):
+        total[...] = value
+        n = value.shape[1] // blocks
+        copies = []
+        for t in range(blocks):
+            mine = pl.ds(pl.multiple_of(o.c * n + 2 * t * n, 128), n)
+            out[:, mine] = total[pl.ds(pl.multiple_of(24 * o.c, 8), 24), t * n : t * n + n]
+            copies.append(
+                remote(
+                    total.at[pl.ds(pl.multiple_of(24 * (1 - o.c), 8), 24), pl.ds(t * n, n)], out.at[:, mine],
+                    last_send.at[k + t], last_recv.at[k + t], o.sibling(),
+                )
+            )
+            copies[-1].start()
+        return copies
+
+    last = hand(0, total_i, out_in, fi.total(), 1)
+    total_a[...] = fa.total()
+    tot.add(1)
+    tot.start(2)
+    fq.across()
     for copy in dn_copies:
         copy.wait_recv()
     d_normed = d_own + dn[o.x].astype(f32)
@@ -784,27 +831,6 @@
         d_normed = d_normed + dn_in[by].astype(f32)
     d_resid, _ = rms_backward(x, r_one, gain_one, d_normed)
     d_tokens[...] = (d_after_ref[...] + d_resid).astype(bf16)
-    total_q, total_a, total_i = (stage.at[:, pl.ds(a, n)] for a, n in ((0, 1152), (1152, 384), (1536, 1536)))
-    out_out[...] = fo.total()
-
-    def hand(k, total, out, value):
-        n = value.shape[1]
-        total[...] = value
-        mine = pl.ds(pl.multiple_of(o.c * n, 128), n)
-        out[:, mine] = total[pl.ds(pl.multiple_of(24 * o.c, 8), 24), :]
-        copy = remote(
-            total.at[pl.ds(pl.multiple_of(24 * (1 - o.c), 8), 24)], out.at[:, mine],
-            last_send.at[k], last_recv.at[k], o.sibling(),
-        )
-        copy.start()
-        return copy
-
-    last = [hand(0, total_i, out_in, fi.total())]
-    total_a[...] = fa.total()
-    tot.add(1)
-    tot.start(2)
-    fq.ring_far()
-    fq.across()
     tot.add(2)
     tot.start(3)
     dense = jnp.concatenate([fq.total(), total_a[...]], 1).astype(bf16)
@@ -830,8 +856,8 @@
     for copy in second:
         copy.wait_recv()
     whole = jnp.concatenate([xa[0], xa[1], xa[2], xa[3]], 1).astype(f32)
-    last.append(hand(1, total_q, out_qkv, whole[:, :1152]))
-    last.append(hand(2, total_a, out_ao, whole[:, 1152:]))
+    last += hand(1, total_q, out_qkv, whole[:, :1152], 3)
+    last += hand(4, total_a, out_ao, whole[:, 1152:], 1)
     tot.add(3)
     take = lax.broadcasted_iota(jnp.int32, (768, 128), 0) == lax.broadcasted_iota(jnp.int32, (768, 128), 1) + 24 * o.d
     own_small[:, 0:128] = jnp.dot(
@@ -881,7 +907,7 @@
             jax.ShapeDtypeStruct((8, 256), f32),
         ],
         scratch_shapes=[
-            full(5, 8, 1024), pltpu.VMEM((1, 1024), jnp.int32), full(48, 3072), full(24, 3072), dma((2,)), dma((4, 11)), dma((4, 11)),
+            full(5, 8, 1024), pltpu.VMEM((1, 1024), jnp.int32), full(48, 3072), full(24, 3072), dma((2,)), dma((4, 17)), dma((4, 11)),
             full(4, 8, 1024), full(7, 8, 1024), dma((7,)), dma((7,)),
             *weights, low(512, 768), dma((3,)), dma((3,)), low(512, 768), low(768, 512), low(128, 768), low(512, 1536), full(16, 640),
             low(12, 128, 512), low(128, 768), full(128, 768), low(128, 768), low(128, 192),
@@ -896,7 +922,7 @@
             *[low(2, 4, *s) for s in sizes],
             *[low(3, *s) for s in sizes],
             dma((4, 11)), dma((4, 11)), dma((2, 3)), dma((2, 3)), dma((3,)), dma((3,)),
-            dma((6,)), dma((6,)), dma((3,)), dma((3,)),
+            dma((6,)), dma((6,)), dma((5,)), dma((5,)),
             full(10, 8, 1024), dma((10,)), dma((10,)),
         ],
         compiler_params=pltpu.CompilerParams(

time: 139 us -> 132 us (0.950)
  Pallas kernels: 136 us -> 130 us
    pallas_call x1, Pallas kernels: 134 us -> 127 us  [layer(): pl.pallas_call(layer_kernel, in_specs=[vm] * len(operands), out_specs=[vm...]
where the time goes in v5:
time: 132 us; the launch traced here: 130 us
  Pallas kernels  130 us (98%)
    pallas_call x1, Pallas kernels, layer(): pl.pallas_call(layer_kernel, in_specs=[vm] * len(operands), out_specs=[vm...  127 us

profile of v5, /device:TPU:0, one launch (start us, length us, event | category | flops | bytes accessed | tf_op | source)
XLA Modules:
  0.0 130.4 jit_solution(4077266907293700642)
XLA Ops:
  0.6 127.4 %shard_map.195 = (bf16[128,768]{1,0:T(8,128)(2,1)}, bf16[128,768]{1,0:T(8,128)(2,1)}, f32[24,2304]{1,0:T(8,128)}, f32[24,768]{1,0:T(8,128)}, f32[24,3072]{1,0:T(...) custom-call(bf16[24,2304]{1,0:T(8,128)(2,1)} %w_qkv.1, bf16[24,768]{1,0:T(8,128)(2,1)} %w_ao.1, bf16[24,3072]{1,0:T(8,128)(2,1)} %bitcast.10, ...), custom_call_target="tpu_custom_call" | custom-call | tf_op jit(solution)/shard_map/pallas_call | solution.py:896
  128.0 2.4 %shard_map.196 = (bf16[128,768]{1,0:T(8,128)(2,1)}, bf16[128,768]{1,0:T(8,128)(2,1)}, f32[1,24]{1,0:T(1,128)}, f32[24,2304]{1,0:T(8,128)}, f32[24,768]{1,0:T(8,1...) custom-call(bf16[128,768]{1,0:T(8,128)(2,1)} %get-tuple-element.27.m, ...), custom_call_target="tpu_custom_call" | custom-call | tf_op jit(solution)/shard_map/pallas_call | solution.py:956

commit v6 on v5

--- a/solution.py
+++ b/solution.py
@@ -660,8 +660,6 @@
     times(0, 4, lambda j: expert_second_grad(j, d_result, acts, h_out))
     fo.to_pair(0, 0, 4)
     wout.finish()
-    fo.from_pair(0, 4)
-    fo.ring()
     result[...] = jnp.zeros_like(result)
     times(0, 4, lambda j: expert_result(j, acts, g_out, result))
 
@@ -692,10 +690,13 @@
 
     times(start, start + 2, back_chunk)
     fi.to_pair(0, 0, 4)
+    fo.from_pair(0, 4)
+    fo.ring()
     times(2 - start, 4 - start, back_chunk)
     grads_back = send_back(1, d_incoming[...])
     fi.from_pair(0, 4)
     fi.ring()
+    fo.ring_far()
     for copy in results_back + grads_back:
         copy.wait_recv()
 
@@ -724,7 +725,6 @@
         d_heads = d_heads + mm_nt(part, g_ao[h].reshape(768, 384))
     fa.to_pair(0, 0, 4)
     d_heads_ref[...] = d_heads.astype(bf16)
-    fo.ring_far()
 
     d_window[...] = jnp.zeros_like(d_window)
 

time: 132 us -> 130 us (0.985)
  Pallas kernels: 130 us -> 128 us
    pallas_call x1, Pallas kernels: 127 us -> 125 us  [layer(): pl.pallas_call(layer_kernel, in_specs=[vm] * len(operands), out_specs=[vm...]
where the time goes in v6:
time: 130 us; the launch traced here: 128 us
  Pallas kernels  128 us (98%)
    pallas_call x1, Pallas kernels, layer(): pl.pallas_call(layer_kernel, in_specs=[vm] * len(operands), out_specs=[vm...  125 us

profile of v6, /device:TPU:0, one launch (start us, length us, event | category | flops | bytes accessed | tf_op | source)
XLA Modules:
  0.0 128.3 jit_solution(5296613992801583878)
XLA Ops:
  0.6 125.3 %shard_map.195 = (bf16[128,768]{1,0:T(8,128)(2,1)}, bf16[128,768]{1,0:T(8,128)(2,1)}, f32[24,2304]{1,0:T(8,128)}, f32[24,768]{1,0:T(8,128)}, f32[24,3072]{1,0:T(...) custom-call(bf16[24,2304]{1,0:T(8,128)(2,1)} %w_qkv.1, bf16[24,768]{1,0:T(8,128)(2,1)} %w_ao.1, bf16[24,3072]{1,0:T(8,128)(2,1)} %bitcast.10, ...), custom_call_target="tpu_custom_call" | custom-call | tf_op jit(solution)/shard_map/pallas_call | solution.py:896
  125.9 2.4 %shard_map.196 = (bf16[128,768]{1,0:T(8,128)(2,1)}, bf16[128,768]{1,0:T(8,128)(2,1)}, f32[1,24]{1,0:T(1,128)}, f32[24,2304]{1,0:T(8,128)}, f32[24,768]{1,0:T(8,1...) custom-call(bf16[128,768]{1,0:T(8,128)(2,1)} %get-tuple-element.27.m, ...), custom_call_target="tpu_custom_call" | custom-call | tf_op jit(solution)/shard_map/pallas_call | solution.py:956

commit v7 on v6

--- a/solution.py
+++ b/solution.py
@@ -751,9 +751,9 @@
     fq.to_pair(0, 0, 4)
     fa.ring()
     fi.ring_far()
+    fo.across()
     times(3 * o.c, 3 * o.c + 3, pair)
     dense_grad(o.c)
-    fo.across()
     fa.ring_far()
     fq.from_pair(0, 4)
     fq.ring()

time: 130 us -> 132 us (1.015)
  Pallas kernels: 128 us -> 130 us
    pallas_call x1, Pallas kernels: 125 us -> 127 us  [layer(): pl.pallas_call(layer_kernel, in_specs=[vm] * len(operands), out_specs=[vm...]
where the time goes in v7:
time: 132 us; the launch traced here: 130 us
  Pallas kernels  130 us (98%)
    pallas_call x1, Pallas kernels, layer(): pl.pallas_call(layer_kernel, in_specs=[vm] * len(operands), out_specs=[vm...  127 us

profile of v7, /device:TPU:0, one launch (start us, length us, event | category | flops | bytes accessed | tf_op | source)
XLA Modules:
  0.0 130.3 jit_solution(7528776088115021111)
XLA Ops:
  0.6 127.3 %shard_map.195 = (bf16[128,768]{1,0:T(8,128)(2,1)}, bf16[128,768]{1,0:T(8,128)(2,1)}, f32[24,2304]{1,0:T(8,128)}, f32[24,768]{1,0:T(8,128)}, f32[24,3072]{1,0:T(...) custom-call(bf16[24,2304]{1,0:T(8,128)(2,1)} %w_qkv.1, bf16[24,768]{1,0:T(8,128)(2,1)} %w_ao.1, bf16[24,3072]{1,0:T(8,128)(2,1)} %bitcast.10, ...), custom_call_target="tpu_custom_call" | custom-call | tf_op jit(solution)/shard_map/pallas_call | solution.py:896
  127.9 2.4 %shard_map.196 = (bf16[128,768]{1,0:T(8,128)(2,1)}, bf16[128,768]{1,0:T(8,128)(2,1)}, f32[1,24]{1,0:T(1,128)}, f32[24,2304]{1,0:T(8,128)}, f32[24,768]{1,0:T(8,1...) custom-call(bf16[128,768]{1,0:T(8,128)(2,1)} %get-tuple-element.27.m, ...), custom_call_target="tpu_custom_call" | custom-call | tf_op jit(solution)/shard_map/pallas_call | solution.py:956
